TPU v7x, 32 devices: a whole 2x2x4 slice. The times are simulated.
32 devices in a mesh: clip: 4 (over y, core), space: 8 (over z, x).
Axes of the slice: x: 2, y: 2, z: 4, core: 2. Of those that a mesh axis runs over, the one named last changes fastest.
Arguments:
- teacher_input: bfloat16 [4, 2, 64, 32, 512], P('clip', None, 'space'), may hold values from -6 to 6
- conv_first: bfloat16 [3, 3, 3, 512, 256], replicated, may hold values from -0.0546875 to 0.0546875
- conv_second: bfloat16 [3, 3, 3, 256, 256], replicated, may hold values from -0.078125 to 0.078125
- student_low: bfloat16 [4, 2, 64, 32, 256], P('clip', None, 'space'), may hold values from -6 to 6
- student_high: bfloat16 [4, 2, 128, 64, 128], P('clip', None, 'space'), may hold values from -6 to 6
- kernel_low: float32 [3, 3, 3, 256], replicated, may hold values from -1 to 1
- kernel_high: float32 [3, 3, 3, 128], replicated, may hold values from -1 to 1
- adapter_low: bfloat16 [256, 256], replicated, may hold values from -0.0078125 to 0.0078125
- adapter_high: bfloat16 [128, 256], replicated, may hold values from -0.009765625 to 0.009765625
Outputs:
- adapter_low_gradient: float32 [256, 256], P('clip')
- kernel_low_gradient: float32 [3, 3, 3, 256], P(None, None, None, 'clip')
- adapter_high_gradient: float32 [128, 256], P('clip')
- kernel_high_gradient: float32 [3, 3, 3, 128], P(None, None, None, 'clip')
- fine_mismatch: bfloat16 [4, 2, 128, 64, 256], P('clip', None, 'space')
All inputs are finite; a program needn't handle non-finite values.
Results may differ from a plain program's by a relative error of at most 0.0067.
Values may be sent and summed in bfloat16 or wider, within the bound.
No kernel may reach another device: no remote copies, remote signals or barrier semaphores. Data moves between devices by JAX's collectives and lax.ppermute only.
A program may use at most 192 MiB of HBM per device.

v0:
```python
import jax
import jax.numpy as jnp
from jax import lax
from jax.sharding import PartitionSpec as P


def padded_2(block, sides, width):
    for axis, dim in sides:
        count = lax.axis_size(axis)
        forward = [(i, i + 1) for i in range(count - 1)]
        backward = [(target, source) for source, target in forward]
        low = lax.ppermute(
            lax.slice_in_dim(block, block.shape[dim] - width, None, axis=dim), axis, forward
        )
        high = lax.ppermute(lax.slice_in_dim(block, 0, width, axis=dim), axis, backward)
        block = jnp.concatenate([low, block, high], axis=dim)
    return block


def pad_sides(field):
    return jnp.pad(field, ((0, 0), (1, 1), (0, 0), (1, 1), (0, 0)))


def conv_taps(padded, weight, row_count):
    frames = padded.shape[1] - 2
    col_count = padded.shape[3] - 2
    summed = jnp.zeros(
        (padded.shape[0], frames, row_count, col_count, weight.shape[-1]), jnp.float32
    )
    for tap_t in range(3):
        for tap_h in range(3):
            for tap_w in range(3):
                window_part = padded[
                    :,
                    tap_t : tap_t + frames,
                    tap_h : tap_h + row_count,
                    tap_w : tap_w + col_count,
                    :,
                ]
                summed = summed + jnp.dot(
                    window_part, weight[tap_t, tap_h, tap_w], preferred_element_type=jnp.float32
                )
    return summed


def student_level(field, extended, kernel, adapter, target, scale):
    padded = pad_sides(extended)
    frames, row_count, col_count = (field.shape[1], field.shape[2], field.shape[3])
    mixed = field.astype(jnp.float32)
    for tap_t in range(3):
        for tap_h in range(3):
            for tap_w in range(3):
                shifted = padded[
                    :,
                    tap_t : tap_t + frames,
                    tap_h : tap_h + row_count,
                    tap_w : tap_w + col_count,
                    :,
                ]
                mixed = mixed + shifted.astype(jnp.float32) * kernel[tap_t, tap_h, tap_w]
    student = mixed.astype(jnp.bfloat16)
    output = jnp.dot(student, adapter, preferred_element_type=jnp.float32)
    mismatch = output - target.astype(jnp.float32)
    resid = (mismatch * scale).astype(jnp.bfloat16)
    adapter_part = jnp.einsum("bfhwc,bfhwd->cd", student, resid, preferred_element_type=jnp.float32)
    back = jnp.einsum("bfhwd,cd->bfhwc", resid, adapter, preferred_element_type=jnp.float32)
    kernel_rows = []
    for tap_t in range(3):
        for tap_h in range(3):
            for tap_w in range(3):
                shifted = padded[
                    :,
                    tap_t : tap_t + frames,
                    tap_h : tap_h + row_count,
                    tap_w : tap_w + col_count,
                    :,
                ]
                kernel_rows.append(jnp.sum(back * shifted.astype(jnp.float32), axis=(0, 1, 2, 3)))
    kernel_part = jnp.stack(kernel_rows).reshape(kernel.shape)
    return (adapter_part, kernel_part, mismatch.astype(jnp.bfloat16))


def on_device(
    teacher_input,
    conv_first,
    conv_second,
    student_low,
    student_high,
    kernel_low,
    kernel_high,
    adapter_low,
    adapter_high,
):
    row_count = teacher_input.shape[2]
    tiles = lax.axis_size("space")
    low_count = (
        teacher_input.shape[0]
        * teacher_input.shape[1]
        * row_count
        * teacher_input.shape[3]
        * lax.axis_size("clip")
        * tiles
    )
    scale_low = 1.0 / low_count
    scale_high = 1.0 / (4 * low_count)
    input_ext = padded_2(teacher_input, (("space", 2),), 1)
    first_feature = conv_taps(pad_sides(input_ext), conv_first, row_count).astype(jnp.bfloat16)
    feature_ext = padded_2(first_feature, (("space", 2),), 1)
    gated = jax.nn.silu(feature_ext.astype(jnp.float32)).astype(jnp.bfloat16)
    upsampled = jnp.repeat(jnp.repeat(gated, 2, axis=2), 2, axis=3)[:, :, 1 : 2 * row_count + 3]
    second_feature = conv_taps(pad_sides(upsampled), conv_second, 2 * row_count).astype(
        jnp.bfloat16
    )
    low_ext = padded_2(student_low, (("space", 2),), 1)
    high_ext = padded_2(student_high, (("space", 2),), 1)
    adapter_one, kernel_one, unused_low = student_level(
        student_low, low_ext, kernel_low, adapter_low, first_feature, scale_low
    )
    adapter_two, kernel_two, mismatch_two = student_level(
        student_high, high_ext, kernel_high, adapter_high, second_feature, scale_high
    )
    summed = lax.psum((adapter_one, adapter_two, kernel_one, kernel_two), "space")
    shares = (
        lax.psum_scatter(summed[0], "clip", scatter_dimension=0, tiled=True),
        lax.psum_scatter(summed[1], "clip", scatter_dimension=0, tiled=True),
        lax.psum_scatter(summed[2], "clip", scatter_dimension=3, tiled=True),
        lax.psum_scatter(summed[3], "clip", scatter_dimension=3, tiled=True),
    )
    return (shares[0], shares[2], shares[1], shares[3], mismatch_two)


def solution(mesh):
    in_specs = (
        P("clip", None, "space", None, None),
        P(),
        P(),
        P("clip", None, "space", None, None),
        P("clip", None, "space", None, None),
        P(),
        P(),
        P(),
        P(),
    )
    out_specs = (
        P("clip", None),
        P(None, None, None, "clip"),
        P("clip", None),
        P(None, None, None, "clip"),
        P("clip", None, "space", None, None),
    )
    return jax.shard_map(
        on_device, mesh=mesh, in_specs=in_specs, out_specs=out_specs, check_vma=False
    )
```

profile of v0, /device:TPU:0, one launch (start us, length us, event | category | flops | bytes accessed | tf_op | source)
XLA Modules:
  0.0 273.2 jit_solution(1043314573551654324)
XLA Ops:
  8.2 4.8 %collective-permute-start.2 = (bf16[1,2,1,32,512]{4,3,2,1,0:T(8,128)(2,1)S(1)}, bf16[1,2,1,32,512]{4,3,2,1,0:T(8,128)(2,1)S(1)}, u32[]{:S(2)}, u32[]{:S(2)}) collective-permute-start(bf16[1,2,1,32,512]{4,3,2,1,0:T(8,128)(2,1)S(1)} %get-tuple-element.76), channel_id=1, source_target_pairs={{0,1},{1,2},{2,3},{3,4},{4,5},{5,6},{6,7},{8,9},{9,10},{10,11},{11... | collective-permute-start | bytes 196616 | tf_op jit(solution)/shard_map/ppermute | solution.py:12
  13.1 1.3 collective-permute-start.3
  15.2 4.5 %collective-permute-start.4 = (bf16[1,2,1,64,128]{4,3,2,1,0:T(8,128)(2,1)S(1)}, bf16[1,2,1,64,128]{4,3,2,1,0:T(8,128)(2,1)S(1)}, u32[]{:S(2)}, u32[]{:S(2)}) collective-permute-start(bf16[1,2,1,64,128]{4,3,2,1,0:T(8,128)(2,1)S(1)} %get-tuple-element.74), channel_id=1, source_target_pairs={{0,1},{1,2},{2,3},{3,4},{4,5},{5,6},{6,7},{8,9},{9,10},{10,11},{11... | collective-permute-start | bytes 98312 | tf_op jit(solution)/shard_map/ppermute | solution.py:12
  21.8 5.0 %collective-permute-start = (bf16[1,2,1,32,256]{4,3,2,1,0:T(8,128)(2,1)S(1)}, bf16[1,2,1,32,256]{4,3,2,1,0:T(8,128)(2,1)S(1)}, u32[]{:S(2)}, u32[]{:S(2)}) collective-permute-start(bf16[1,2,1,32,256]{4,3,2,1,0:T(8,128)(2,1)S(1)} %get-tuple-element.80), channel_id=1, source_target_pairs={{0,1},{1,2},{2,3},{3,4},{4,5},{5,6},{6,7},{8,9},{9,10},{10,11},{11... | collective-permute-start | bytes 98312 | tf_op jit(solution)/shard_map/ppermute | solution.py:12
  28.5 1.4 fusion.263
  33.3 5.0 %collective-permute-done.1 = bf16[1,2,1,32,256]{4,3,2,1,0:T(8,128)(2,1)S(1)} collective-permute-done((bf16[1,2,1,32,256]{4,3,2,1,0:T(8,128)(2,1)S(1)}, bf16[1,2,1,32,256]{4,3,2,1,0:T(8,128)(2,1)S(1)}, u32[]{:S(2)}, u32[]{:S(2)}) %collective-permute-start.1) | collective-permute-done | bytes 32800 | tf_op jit(solution)/shard_map/ppermute | solution.py:15
  38.5 4.8 %fusion.93 = bf16[1,2,16,64,128]{4,3,2,1,0:T(8,128)(2,1)} fusion(bf16[1,2,16,64,128]{4,3,2,1,0:T(8,128)(2,1)S(1)} %copy-done.6, bf16[1,2,1,64,128]{4,3,2,1,0:T(8,128)(2,1)S(1)} %collective-permute-done.5, bf16[1,2,1,64,128]{4,3,2,1,0:T(8,128)(2,1)S(1)} %collective-permute-done.4, f32[128]{0:T(128)S(1)} %get-tuple-element.134, ...), kind=kLoop, calls=%fused_computation.198 | loop fusion | flops 22020096 | bytes 13710848 | tf_op jit(solution)/shard_map/convert_element_type | solution.py:61
  43.3 2.1 fusion.228
  55.3 5.4 %collective-permute-start.6 = (bf16[1,2,1,32,256]{4,3,1,2,0:T(8,128)(2,1)}, bf16[1,2,1,32,256]{4,3,1,2,0:T(8,128)(2,1)}, u32[]{:S(2)}, u32[]{:S(2)}) collective-permute-start(bf16[1,2,1,32,256]{4,3,1,2,0:T(8,128)(2,1)} %get-tuple-element.78), channel_id=1, source_target_pairs={{0,1},{1,2},{2,3},{3,4},{4,5},{5,6},{6,7},{8,9},{9,10},{10,11},{11... | collective-permute-start | bytes 98312 | tf_op jit(solution)/shard_map/ppermute | solution.py:12
  63.5 1.7 fusion.217
  70.3 1.4 broadcast_in_dim.13
  71.7 1.5 slice.1040
  73.2 2.7 fusion.100
  75.9 1.8 fusion.103
  77.7 1.7 fusion.106
  79.5 1.7 fusion.109
  81.2 1.8 fusion.112
  83.0 1.8 fusion.115
  84.8 1.8 fusion.118
  86.5 1.8 fusion.121
  88.3 1.7 fusion.124
  90.1 1.8 fusion.127
  91.9 1.8 fusion.130
  93.7 1.8 fusion.133
  95.5 1.8 fusion.136
  97.2 1.8 fusion.139
  99.1 1.8 fusion.142
  100.8 1.8 fusion.145
  102.6 1.7 fusion.148
  104.4 1.8 fusion.151
  106.2 1.8 fusion.154
  108.0 1.8 fusion.157
  109.7 1.7 fusion.160
  111.5 1.8 fusion.163
  113.3 1.7 fusion.97
  115.0 1.7 fusion.167
  116.7 1.7 fusion.168
  118.5 1.8 fusion.169
  120.3 19.0 %add_convert_fusion = bf16[2,16,64,256]{3,2,1,0:T(8,128)(2,1)} fusion(f32[2,16,64,256]{3,2,1,0:T(8,128)} %fusion.163, f32[2,16,64,256]{3,2,1,0:T(8,128)} %fusion.160, f32[2,16,64,256]{3,2,1,0:T(8,128)} %fusion.157, f32[2,16,64,256]{3,2,1,0:T(8,128)} %fusion.154, f32[2,16,64,256]{3,2,1,0:T(8,128)} %fusion.151, f32[2,16,64,256]{3,2,1,0:T(8,128)} %fusion.148, ...), kind=kOutput, calls=%fused_computation.44 | convolution fusion | flops 282591232 | bytes 56885248 | tf_op jit(solution)/shard_map/dot_general | solution.py:40
  139.3 1.8 convert_subtract_fusion
  141.2 2.1 fusion.82
  143.3 3.3 %fusion.94 = (f32[128]{0:T(128)}, f32[128]{0:T(128)}, f32[128]{0:T(128)}, f32[128]{0:T(128)}, f32[128]{0:T(128)}, /*index=5*/f32[128]{0:T(128)}, f32[128]{0:T(12...) fusion(f32[1,2,16,64,128]{4,3,2,1,0:T(8,128)S(1)} %get-tuple-el, ...), kind=kLoop, calls=%fused_computation.199 | loop fusion | flops 14153472 | bytes 10494976 | tf_op jit(solution)/shard_map/reduce_sum | solution.py:78
  146.6 2.9 %stack.223 = f32[27,128]{1,0:T(8,128)S(1)} concatenate(f32[1,128]{1,0:T(1,128)} %bitcast.814, f32[1,128]{1,0:T(1,128)} %bitcast.815, f32[1,128]{1,0:T(1,128)} %bitcast.816, f32[1,128]{1,0:T(1,128)} %bitcast.817, f32[1,128]{1,0:T(1,128)} %bitcast.818, f32[1,128]{1,0:T(1,128)} %bitcast.819, f32[1,128]{1,0:T(1,128)} %bitcast.801, f32[1,128]{1,0:T(1,128)} %bitcast.800, ...), dimensions={0} | concatenate | bytes 27648 | tf_op jit(solution)/shard_map/stack | solution.py:79
  154.8 16.5 %reduce-scatter.15.cloned.1.call-done = f32[32,27]{1,0:T(8,128)} async-done(((f32[128,27]{1,0:T(8,128)}), f32[32,27]{1,0:T(8,128)}) %reduce-scatter.15.cloned.1.call-update) | async-done | bytes 3472
  172.3 21.1 %reduce-scatter.11.cloned.1.call-done = f32[32,256]{1,0:T(8,128)} async-done(((f32[128,256]{1,0:T(8,128)}), f32[32,256]{1,0:T(8,128)}) %reduce-scatter.11.cloned.1.call-update) | async-done | bytes 32784 | tf_op jit(solution)/shard_map/reduce_scatter | solution.py:125
  193.4 39.1 %all-reduce.4 = (f32[3,3,3,64]{3,2,1,0:T(4,128)}, f32[32,256]{1,0:T(8,128)}, f32[3,3,3,32]{3,2,1,0:T(4,128)}) all-reduce(f32[3,3,3,64]{3,2,1,0:T(4,128)S(1)} %copy.78, f32[32,256]{1,0:T(8,128)} %reduce-scatter.11.cloned.1.call-done, f32[3,3,3,32]{3,2,1,0:T(4,128)S(1)} %copy.80), channel_id=1, replica_groups=mesh['clip'=4,'space'=8] {'space'}, use_global_device_ids=true, to_apply=%region_29.30 | all-reduce | flops 10784 | bytes 86272 | tf_op jit(solution)/shard_map/psum | solution.py:122
  232.4 32.7 %all-reduce.7.cloned.1.call-done = f32[64,256]{1,0:T(8,128)} async-done(((f32[64,256]{1,0:T(8,128)}), f32[64,256]{1,0:T(8,128)}) %all-reduce.7.cloned.1.call-update) | async-done | bytes 65552 | tf_op jit(solution)/shard_map/psum | solution.py:122
  265.2 1.5 copy.84
  (113 shorter events, 32.8 us)
Async XLA Ops:
  7.2 54.8 %copy-start = (bf16[256,256]{1,0:T(8,128)(2,1)S(1)}, bf16[256,256]{1,0:T(8,128)(2,1)}, u32[]{:S(2)}) copy-start(bf16[256,256]{1,0:T(8,128)(2,1)} %param.16) | copy-start | bytes 393220
  7.2 25.7 %copy-start.6 = (bf16[1,2,16,64,128]{4,3,2,1,0:T(8,128)(2,1)S(1)}, bf16[1,2,16,64,128]{4,3,2,1,0:T(8,128)(2,1)}, u32[]{:S(2)}) copy-start(bf16[1,2,16,64,128]{4,3,2,1,0:T(8,128)(2,1)} %param.13) | copy-start | bytes 1572868
  7.2 31.1 %copy-start.8 = (bf16[1,2,8,32,256]{4,3,2,1,0:T(8,128)(2,1)S(1)}, bf16[1,2,8,32,256]{4,3,2,1,0:T(8,128)(2,1)}, u32[]{:S(2)}) copy-start(bf16[1,2,8,32,256]{4,3,2,1,0:T(8,128)(2,1)} %param.12) | copy-start | bytes 786436
  7.2 144.8 %reduce-scatter.9.cloned.1.call-start = ((), (), s32[]{:S(2)}) async-start(), calls=%async_computation.4 | async-start | bytes 327680 | tf_op jit(solution)/shard_map/reduce_scatter | solution.py:124
  8.2 37.2 %collective-permute-start.2 = (bf16[1,2,1,32,512]{4,3,2,1,0:T(8,128)(2,1)S(1)}, bf16[1,2,1,32,512]{4,3,2,1,0:T(8,128)(2,1)S(1)}, u32[]{:S(2)}, u32[]{:S(2)}) collective-permute-start(bf16[1,2,1,32,512]{4,3,2,1,0:T(8,128)(2,1)S(1)} %get-tuple-element.76), channel_id=1, source_target_pairs={{0,1},{1,2},{2,3},{3,4},{4,5},{5,6},{6,7},{8,9},{9,10},{10,11},{11... | collective-permute-start | bytes 196616 | tf_op jit(solution)/shard_map/ppermute | solution.py:12
  13.1 32.3 %collective-permute-start.3 = (bf16[1,2,1,32,512]{4,3,2,1,0:T(8,128)(2,1)S(1)}, bf16[1,2,1,32,512]{4,3,2,1,0:T(8,128)(2,1)S(1)}, u32[]{:S(2)}, u32[]{:S(2)}) collective-permute-start(bf16[1,2,1,32,512]{4,3,2,1,0:T(8,128)(2,1)S(1)} %get-tuple-element.77), channel_id=1, source_target_pairs={{1,0},{2,1},{3,2},{4,3},{5,4},{6,5},{7,6},{9,8},{10,9},{11,10},{12... | collective-permute-start | bytes 196616 | tf_op jit(solution)/shard_map/ppermute | solution.py:15
  15.2 16.4 %collective-permute-start.4 = (bf16[1,2,1,64,128]{4,3,2,1,0:T(8,128)(2,1)S(1)}, bf16[1,2,1,64,128]{4,3,2,1,0:T(8,128)(2,1)S(1)}, u32[]{:S(2)}, u32[]{:S(2)}) collective-permute-start(bf16[1,2,1,64,128]{4,3,2,1,0:T(8,128)(2,1)S(1)} %get-tuple-element.74), channel_id=1, source_target_pairs={{0,1},{1,2},{2,3},{3,4},{4,5},{5,6},{6,7},{8,9},{9,10},{10,11},{11... | collective-permute-start | bytes 98312 | tf_op jit(solution)/shard_map/ppermute | solution.py:12
  19.7 13.2 %collective-permute-start.5 = (bf16[1,2,1,64,128]{4,3,2,1,0:T(8,128)(2,1)S(1)}, bf16[1,2,1,64,128]{4,3,2,1,0:T(8,128)(2,1)S(1)}, u32[]{:S(2)}, u32[]{:S(2)}) collective-permute-start(bf16[1,2,1,64,128]{4,3,2,1,0:T(8,128)(2,1)S(1)} %get-tuple-element.75), channel_id=1, source_target_pairs={{1,0},{2,1},{3,2},{4,3},{5,4},{6,5},{7,6},{9,8},{10,9},{11,10},{12... | collective-permute-start | bytes 98312 | tf_op jit(solution)/shard_map/ppermute | solution.py:15
  21.8 11.5 %collective-permute-start = (bf16[1,2,1,32,256]{4,3,2,1,0:T(8,128)(2,1)S(1)}, bf16[1,2,1,32,256]{4,3,2,1,0:T(8,128)(2,1)S(1)}, u32[]{:S(2)}, u32[]{:S(2)}) collective-permute-start(bf16[1,2,1,32,256]{4,3,2,1,0:T(8,128)(2,1)S(1)} %get-tuple-element.80), channel_id=1, source_target_pairs={{0,1},{1,2},{2,3},{3,4},{4,5},{5,6},{6,7},{8,9},{9,10},{10,11},{11... | collective-permute-start | bytes 98312 | tf_op jit(solution)/shard_map/ppermute | solution.py:12
  31.6 11.7 %copy-start.10 = (bf16[1,2,1,64,128]{4,3,2,1,0:T(8,128)(2,1)}, bf16[1,2,1,64,128]{4,3,2,1,0:T(8,128)(2,1)S(1)}, u32[]{:S(2)}) copy-start(bf16[1,2,1,64,128]{4,3,2,1,0:T(8,128)(2,1)S(1)} %collective-permute-done.4) | copy-start | bytes 98308
  31.6 6.7 %collective-permute-start.1 = (bf16[1,2,1,32,256]{4,3,2,1,0:T(8,128)(2,1)S(1)}, bf16[1,2,1,32,256]{4,3,2,1,0:T(8,128)(2,1)S(1)}, u32[]{:S(2)}, u32[]{:S(2)}) collective-permute-start(bf16[1,2,1,32,256]{4,3,2,1,0:T(8,128)(2,1)S(1)} %get-tuple-element.81), channel_id=1, source_target_pairs={{1,0},{2,1},{3,2},{4,3},{5,4},{6,5},{7,6},{9,8},{10,9},{11,10},{12... | collective-permute-start | bytes 98312 | tf_op jit(solution)/shard_map/ppermute | solution.py:15
  32.9 10.4 %copy-start.12 = (bf16[1,2,1,64,128]{4,3,2,1,0:T(8,128)(2,1)}, bf16[1,2,1,64,128]{4,3,2,1,0:T(8,128)(2,1)S(1)}, u32[]{:S(2)}) copy-start(bf16[1,2,1,64,128]{4,3,2,1,0:T(8,128)(2,1)S(1)} %collective-permute-done.5) | copy-start | bytes 98308
  38.3 7.5 %slice-start = ((s8[7077888]{0:T(1024)(128)(4,1)}), s8[4194304]{0:T(1024)(128)(4,1)S(1)}, s32[]{:S(2)}) async-start(s8[7077888]{0:T(1024)(128)(4,1)} %bitcast.736), calls=%async_computation.9 | async-start | bytes 8388608
  38.5 7.4 %slice-start.1 = ((s8[7077888]{0:T(1024)(128)(4,1)}), s8[2883584]{0:T(1024)(128)(4,1)S(1)}, s32[]{:S(2)}) async-start(s8[7077888]{0:T(1024)(128)(4,1)} %bitcast.736), calls=%async_computation.10 | async-start | bytes 5767168
  43.3 2.1 copy-start.5
  55.3 13.0 %collective-permute-start.6 = (bf16[1,2,1,32,256]{4,3,1,2,0:T(8,128)(2,1)}, bf16[1,2,1,32,256]{4,3,1,2,0:T(8,128)(2,1)}, u32[]{:S(2)}, u32[]{:S(2)}) collective-permute-start(bf16[1,2,1,32,256]{4,3,1,2,0:T(8,128)(2,1)} %get-tuple-element.78), channel_id=1, source_target_pairs={{0,1},{1,2},{2,3},{3,4},{4,5},{5,6},{6,7},{8,9},{9,10},{10,11},{11... | collective-permute-start | bytes 98312 | tf_op jit(solution)/shard_map/ppermute | solution.py:12
  60.7 7.6 %collective-permute-start.7 = (bf16[1,2,1,32,256]{4,3,1,2,0:T(8,128)(2,1)}, bf16[1,2,1,32,256]{4,3,1,2,0:T(8,128)(2,1)}, u32[]{:S(2)}, u32[]{:S(2)}) collective-permute-start(bf16[1,2,1,32,256]{4,3,1,2,0:T(8,128)(2,1)} %get-tuple-element.79), channel_id=1, source_target_pairs={{1,0},{2,1},{3,2},{4,3},{5,4},{6,5},{7,6},{9,8},{10,9},{11,10},{12... | collective-permute-start | bytes 98312 | tf_op jit(solution)/shard_map/ppermute | solution.py:15
  62.2 1.0 copy-start.9
  63.2 90.5 %reduce-scatter.13.cloned.1.call-start = ((), (), s32[]{:S(2)}) async-start(), calls=%async_computation.7 | async-start | bytes 163840
  68.2 103.1 %reduce-scatter.15.cloned.1.call-start = ((), (), s32[]{:S(2)}) async-start(), calls=%async_computation.8 | async-start | bytes 81920
  71.7 4.2 %copy-start.4 = (bf16[3,3,3,256,256]{4,3,2,1,0:T(8,128)(2,1)S(1)}, bf16[3,3,3,256,256]{4,3,2,1,0:T(8,128)(2,1)}, u32[]{:S(2)}) copy-start(bf16[3,3,3,256,256]{4,3,2,1,0:T(8,128)(2,1)} %param.11) | copy-start | bytes 10616836
  113.3 1.7 copy-start.2
  120.3 19.0 %copy-start.14 = (bf16[128,256]{1,0:T(8,128)(2,1)S(1)}, bf16[128,256]{1,0:T(8,128)(2,1)}, u32[]{:S(2)}) copy-start(bf16[128,256]{1,0:T(8,128)(2,1)} %param.17) | copy-start | bytes 196612
  139.3 1.9 copy-start.7
  139.3 1.9 copy-start.11
  139.3 1.9 copy-start.13
  146.6 4.3 %copy-start.3 = (bf16[1,2,16,64,128]{4,3,2,1,0:T(8,128)(2,1)S(1)}, bf16[1,2,16,64,128]{4,3,2,1,0:T(8,128)(2,1)}, u32[]{:S(2)}) copy-start(bf16[1,2,16,64,128]{4,3,2,1,0:T(8,128)(2,1)} %fusion.93) | copy-start | bytes 1572868
  150.9 42.5 %reduce-scatter.11.cloned.1.call-start = ((), (), s32[]{:S(2)}) async-start(), calls=%async_computation.6 | async-start | bytes 163840 | tf_op jit(solution)/shard_map/reduce_scatter | solution.py:125
  152.0 113.2 %all-reduce.7.cloned.1.call-start = ((), (), s32[]{:S(2)}) async-start(), calls=%async_computation.5 | async-start | bytes 131072 | tf_op jit(solution)/shard_map/psum | solution.py:122
  152.6 114.1 %copy-start.1 = (bf16[256,256]{1,0:T(8,128)(2,1)S(1)}, bf16[256,256]{1,0:T(8,128)(2,1)}, u32[]{:S(2)}) copy-start(bf16[256,256]{1,0:T(8,128)(2,1)} %param.16) | copy-start | bytes 393220
Sparse Core Ops, SparseCore 0:
  63.3 20.8 reduce-scatter.8
  86.8 19.5 reduce-scatter.12
  151.0 20.2 reduce-scatter.14
  173.7 19.6 reduce-scatter.10
  196.6 68.4 all-reduce.6
where the time goes:
time: 274 us; the launch traced here: 273 us
  matrix products  83.7 us (31%)
  waiting for transfers between devices  75.9 us (28%)
  blocking collectives  39.1 us (14%)
  starting transfers between devices  25.3 us (9%)
  local copies, waits for them, and re-layouts  20.5 us (7%)
  between operations  14.4 us (5%)
  other arithmetic  14.2 us (5%)
    dot_general x54, matrix products, conv_taps(): jnp.dot(window_part, weight[tap_t, tap_h, tap_w], preferred_element_type=...  76 us
    psum x1, blocking collectives, on_device(): lax.psum((adapter_one, adapter_two, kernel_one, kernel_two), 'space')  39.1 us
    psum x1, waiting for transfers between devices, on_device(): lax.psum((adapter_one, adapter_two, kernel_one, kernel_two), 'space')  32.7 us
    reduce_scatter x1, waiting for transfers between devices, on_device(): lax.psum_scatter(summed[1], 'clip', scatter_dimension=0, tiled=True)  21.1 us
    ppermute x4, starting transfers between devices, padded_2(): lax.ppermute(lax.slice_in_dim(block, block.shape[dim] - width, None, axis...  19.8 us
    unnamed x7, waiting for transfers between devices  17.1 us
    unnamed x44, local copies, waits for them, and re-layouts  7.61 us
    convert_element_type x2, other arithmetic, student_level(): student = mixed.astype(jnp.bfloat16)  6.86 us
  transfers between devices with their start and end apart: 13, of which 4 were waited for; matrix products, arithmetic and copies ran while one was open for 39% of the time, Pallas kernels for 0%

commit v1 on v0

v1 whole, which is shorter than its diff:
```python
import functools

import jax
import jax.numpy as jnp
from jax import lax
from jax.experimental import pallas as pl
from jax.experimental.pallas import tpu as pltpu
from jax.sharding import PartitionSpec as P

F32, BF16 = jnp.float32, jnp.bfloat16
HBM = pl.BlockSpec(memory_space=pltpu.HBM)
MIB = 1 << 20


def shift_cols(value, by):
    axis = value.ndim - 2
    count = value.shape[axis]
    column = lax.broadcasted_iota(jnp.int32, value.shape, axis)
    edge = 0 if by > 0 else count - 1
    return jnp.where(column == edge, 0.0, pltpu.roll(value, by % count, axis))


def silu(value):
    return value / (1.0 + jnp.exp(-value))


def dot(a, b):
    return jnp.dot(a, b, preferred_element_type=F32)


def dot_nt(a, b):
    return lax.dot_general(a, b, (((1,), (1,)), ((), ())), preferred_element_type=F32)


def dot_tn(a, b):
    return lax.dot_general(a, b, (((0,), (0,)), ((), ())), preferred_element_type=F32)


def frame_spans(frames):
    spans = []
    for tap in (1, 0, 2):
        off = tap - 1
        count = frames - abs(off)
        if count > 0:
            spans.append((tap, max(0, -off), max(0, off), count))
    return spans


def near_frames(cell, frames):
    frame = cell % frames
    near = [cell + t for t in (-1, 0, 1) if 0 <= frame + t < frames]
    return near, near[0] - cell + 1


class Copies:
    def __init__(self, sems):
        self.sems, self.count = sems, 0

    def start(self, src, dst):
        copy = pltpu.make_async_copy(src, dst, self.sems.at[self.count])
        self.count += 1
        copy.start()
        return copy


def first_kernel(frames, x_hbm, w_hbm, low_hbm, high_hbm, inner_hbm, edge_hbm, up_hbm, down_hbm, x_ref, w_buf, acc, inner, edge, up, down, low_row, high_row, sems):
    cells, rows, cols, depth = x_ref.shape
    out = w_buf.shape[-1]
    clips = cells // frames
    spans = frame_spans(frames)
    copies = Copies(sems)
    load_x = copies.start(x_hbm, x_ref)
    loads = {}
    for tap, _, _, _ in spans:
        for tap_h in (1, 0, 2):
            loads[tap, tap_h] = copies.start(w_hbm.at[tap, tap_h], w_buf.at[tap, tap_h])
    borders = []
    for k, row, fine_row in ((0, 0, 0), (1, rows - 1, 2 * rows - 1)):
        borders.append(copies.start(low_hbm.at[:, row], low_row.at[k]))
        borders.append(copies.start(high_hbm.at[:, fine_row], high_row.at[k]))
    for tap_w in range(3):
        acc[tap_w, :, 0:1] = jnp.zeros((cells, 1, cols, out), F32)
        acc[tap_w, :, rows + 1 : rows + 2] = jnp.zeros((cells, 1, cols, out), F32)
    load_x.wait()
    for tap, to, src, count in spans:
        for tap_h in (1, 0, 2):
            loads[tap, tap_h].wait()
            at = 2 - tap_h
            for tap_w in range(3):
                weight = w_buf[tap, tap_h, tap_w]
                for clip in range(clips):
                    first = clip * frames
                    rowset = x_ref[first + src : first + src + count].reshape(-1, depth)
                    product = dot(rowset, weight).reshape(count, rows, cols, out)
                    spot = (tap_w, pl.ds(first + to, count), pl.ds(at, rows))
                    if tap == 1 and tap_h == 1:
                        acc[spot] = product
                    else:
                        acc[spot] = acc[spot] + product

    def gathered(cell, row):
        return acc[1, cell, row] + shift_cols(acc[0, cell, row], 1) + shift_cols(acc[2, cell, row], -1)

    for copy in borders:
        copy.wait()
    low_ch, high_ch = low_row.shape[-1], high_row.shape[-1]
    for k, packet in ((0, up), (1, down)):
        for cell in range(cells):
            for j in range(2):
                value = gathered(cell, k * rows + j)
                edge[k, cell, j] = value
                packet[cell, j, :, 0:out] = value.astype(BF16)
            packet[cell, 2, :, 0:low_ch] = low_row[k, cell]
            packet[cell, 3, :, 0:high_ch] = high_row[k, cell, 0:cols]
            packet[cell, 3, :, high_ch : 2 * high_ch] = high_row[k, cell, cols:]
    stores = [copies.start(up, up_hbm), copies.start(down, down_hbm), copies.start(edge, edge_hbm)]
    for cell in range(cells):

        def gather(row, _, cell=cell):
            inner[cell, row] = gathered(cell, row + 2).astype(BF16)
            return 0

        lax.fori_loop(0, rows - 2, gather, 0)
    stores.append(copies.start(inner, inner_hbm))
    for copy in stores:
        copy.wait()


def phase_weights(w_ref, wc_ref):
    depth = w_ref.shape[-2]
    chunk = 16
    for tap in range(3):

        def body(step, _, tap=tap):
            rows = pl.ds(pl.multiple_of(step * chunk, chunk), chunk)
            taps = [[w_ref[tap, h, w, rows].astype(F32) for w in range(3)] for h in range(3)]
            for p in range(2):
                if p == 0:
                    merged = (taps[0], [taps[1][w] + taps[2][w] for w in range(3)])
                else:
                    merged = ([taps[0][w] + taps[1][w] for w in range(3)], taps[2])
                for a in range(2):
                    m = merged[a]
                    wc_ref[p, 0, tap, a, 0, rows] = m[0].astype(BF16)
                    wc_ref[p, 0, tap, a, 1, rows] = (m[1] + m[2]).astype(BF16)
                    wc_ref[p, 1, tap, a, 0, rows] = (m[0] + m[1]).astype(BF16)
                    wc_ref[p, 1, tap, a, 1, rows] = m[2].astype(BF16)
            return 0

        lax.fori_loop(0, depth // chunk, body, 0)


def gate_rows(feature):
    gated = silu(feature)
    return shift_cols(gated, 1).astype(BF16), gated.astype(BF16), shift_cols(gated, -1).astype(BF16)


def second_feature(frames, gated, wc_ref, count, fine):
    _, groups, cells, _, cols, out = gated.shape
    for cell in range(cells):
        near, first_tap = near_frames(cell, frames)
        for p in range(2):
            for q in range(2):
                field = jnp.concatenate(
                    [
                        gated[q + b, :, other, p + a : p + a + count].reshape(groups * count * cols, out)
                        for other in near
                        for a in range(2)
                        for b in range(2)
                    ],
                    axis=1,
                )
                weight = wc_ref[p, q, first_tap : first_tap + len(near)].reshape(-1, out)
                product = dot(field, weight).reshape(groups, count, cols, out)
                for group in range(groups):
                    for row in range(count):
                        for block in range(out // 128):
                            fine[group, cell, row, p, block, pl.ds(q, cols, stride=2), :] = product[
                                group, row, :, 128 * block : 128 * block + 128
                            ]


def depthwise(frames, padded, kernel_ref, student):
    cells, rows, _, channels = student.shape
    for cell in range(cells):
        near, first_tap = near_frames(cell, frames)
        for lane in range(0, channels, 128):
            lanes = pl.ds(lane, 128)

            def body(row, _, cell=cell, near=near, first_tap=first_tap, lanes=lanes):
                sums = [None, None, None]
                for t, other in enumerate(near):
                    for h in range(3):
                        field = padded[other, row + h, :, lanes]
                        for w in range(3):
                            k = 9 * (t + first_tap) + 3 * h + w
                            term = field * kernel_ref[k : k + 1, lanes]
                            sums[w] = term if sums[w] is None else sums[w] + term
                student[cell, row, :, lanes] = (
                    padded[cell, row + 1, :, lanes]
                    + sums[1]
                    + shift_cols(sums[0], 1)
                    + shift_cols(sums[2], -1)
                ).astype(BF16)
                return 0

            lax.fori_loop(0, rows, body, 0)


def kernel_gradient(frames, padded, back, total, first):
    cells, rows, _, channels = back.shape
    for lane in range(0, channels, 128):
        lanes = pl.ds(lane, 128)
        sums = tuple(jnp.zeros((8, 128), F32) for _ in range(27))
        for cell in range(cells):
            near, first_tap = near_frames(cell, frames)

            def body(row, sums, cell=cell, near=near, first_tap=first_tap, lanes=lanes):
                sums = list(sums)
                center = back[cell, row, :, lanes]
                moved = (shift_cols(center, -1), center, shift_cols(center, 1))
                for t, other in enumerate(near):
                    for h in range(3):
                        field = padded[other, row + h, :, lanes]
                        for w in range(3):
                            k = 9 * (t + first_tap) + 3 * h + w
                            term = (moved[w] * field).reshape(-1, 8, 128)
                            sums[k] = sums[k] + jnp.sum(term, axis=0)
                return tuple(sums)

            sums = lax.fori_loop(0, rows, body, sums)
        for k in range(27):
            value = jnp.sum(sums[k], axis=0, keepdims=True)
            total[k : k + 1, lanes] = value if first else total[k : k + 1, lanes] + value


def level(student, target, adapter, scale, back, grad):
    mismatch = dot(student, adapter) - target
    residual = (mismatch * scale).astype(BF16)
    grad[...] += dot_tn(student, residual)
    return mismatch, dot_nt(residual, adapter)


def fine_target(fine, rows):
    blocks = fine.shape[2]
    value = jnp.concatenate([fine[rows, :, block].reshape(-1, 128) for block in range(blocks)], axis=1)
    return value.astype(BF16).astype(F32)


def second_kernel(
    frames, scale_low, scale_high,
    inner_hbm, w_hbm, low_hbm, high_hbm, klow_hbm, khigh_hbm, plow_hbm, phigh_hbm,
    wc_hbm, mismatch_hbm, glow_hbm, ghigh_hbm, gklow_hbm, gkhigh_hbm,
    feature, w_ref, low, high, klow, khigh, plow, phigh,
    wc, mismatch, glow, ghigh, gklow, gkhigh,
    gated, fine, low_pad, high_pad, low_student, high_student, low_back, high_back, sems,
):
    cells, count, cols, out = feature.shape
    rows = count + 2
    inner = rows - 4
    copies = Copies(sems)
    load_high = copies.start(high_hbm.at[:, pl.ds(3, 2 * inner + 2)], high)
    load_khigh = copies.start(khigh_hbm, khigh)
    load_w = copies.start(w_hbm, w_ref)
    load_low = copies.start(low_hbm, low)
    load_klow = copies.start(klow_hbm, klow)
    load_inner = copies.start(inner_hbm, feature)
    load_plow = copies.start(plow_hbm, plow)
    load_phigh = copies.start(phigh_hbm, phigh)

    load_high.wait()
    load_khigh.wait()
    for cell in range(cells):

        def widen_high(row, _, cell=cell):
            high_pad[cell, row] = high[cell, row].astype(F32)
            return 0

        lax.fori_loop(0, 2 * inner + 2, widen_high, 0)
    depthwise(frames, high_pad, khigh, high_student)
    load_low.wait()
    load_klow.wait()
    for cell in range(cells):

        def widen_low(row, _, cell=cell):
            low_pad[cell, row] = low[cell, row].astype(F32)
            return 0

        lax.fori_loop(0, rows, widen_low, 0)
    depthwise(frames, low_pad, klow, low_student)

    load_w.wait()
    phase_weights(w_ref, wc)
    stores = [copies.start(wc, wc_hbm)]

    load_inner.wait()
    for cell in range(cells):

        def gate(row, _, cell=cell):
            for k, value in enumerate(gate_rows(feature[cell, row].astype(F32))):
                gated[k, 0, cell, row] = value
            return 0

        lax.fori_loop(0, count, gate, 0)
    second_feature(frames, gated, wc, inner, fine)

    load_plow.wait()
    load_phigh.wait()
    glow[...] = jnp.zeros_like(glow)
    ghigh[...] = jnp.zeros_like(ghigh)
    gklow[...] = jnp.zeros_like(gklow)
    gkhigh[...] = jnp.zeros_like(gkhigh)
    for cell in range(cells):
        for row in range(0, inner, 2):
            here = slice(2 * row, 2 * row + 4)
            student = high_student[cell, here].reshape(-1, high.shape[-1])
            target = fine_target(fine.at[0, cell], slice(row, row + 2))
            value, back = level(student, target, phigh[...], scale_high, high_back, ghigh)
            mismatch[cell, here] = value.astype(BF16).reshape(4, 2 * cols, out)
            high_back[cell, here] = back.reshape(4, 2 * cols, -1)
    stores.append(copies.start(mismatch, mismatch_hbm.at[:, pl.ds(4, 2 * inner)]))
    stores.append(copies.start(ghigh, ghigh_hbm))
    for cell in range(cells):
        student = low_student[cell].reshape(-1, low.shape[-1])
        target = feature[cell].reshape(-1, out).astype(F32)
        _, back = level(student, target, plow[...], scale_low, low_back, glow)
        low_back[cell] = back.reshape(count, cols, -1)
    stores.append(copies.start(glow, glow_hbm))
    kernel_gradient(frames, low_pad, low_back, gklow, True)
    kernel_gradient(frames, high_pad, high_back, gkhigh, True)
    stores.append(copies.start(gklow, gklow_hbm))
    stores.append(copies.start(gkhigh, gkhigh_hbm))
    for copy in stores:
        copy.wait()


def third_kernel(
    frames, shards, scale_low, scale_high,
    place, above_hbm, below_hbm, edge_hbm, inner_hbm, low_hbm, high_hbm, klow_hbm, khigh_hbm, plow_hbm, phigh_hbm,
    wc_hbm, glow_hbm, ghigh_hbm, gklow_hbm, gkhigh_hbm, mismatch_in,
    mismatch_hbm, keep_hbm, send_hbm,
    packets, edge, inside, low, high, klow, khigh, plow, phigh, wc, glow, ghigh, gklow, gkhigh,
    mismatch, keep, send,
    feature, gated, fine, low_pad, high_pad, low_student, high_student, low_back, high_back, shard_sums, sems,
):
    del mismatch_in
    _, cells, _, cols, out = edge.shape
    rows = inner_hbm.shape[1] + 2
    low_ch, high_ch = low.shape[-1], high.shape[-1]
    mine = place[0]
    copies = Copies(sems)
    loads = [
        copies.start(above_hbm, packets.at[0]),
        copies.start(below_hbm, packets.at[1]),
        copies.start(high_hbm.at[:, pl.ds(0, 5)], high.at[0]),
        copies.start(high_hbm.at[:, pl.ds(2 * rows - 5, 5)], high.at[1]),
        copies.start(low_hbm.at[:, pl.ds(0, 2)], low.at[0]),
        copies.start(low_hbm.at[:, pl.ds(rows - 2, 2)], low.at[1]),
        copies.start(khigh_hbm, khigh),
        copies.start(klow_hbm, klow),
        copies.start(edge_hbm, edge),
        copies.start(inner_hbm.at[:, pl.ds(0, 2)], inside.at[0]),
        copies.start(inner_hbm.at[:, pl.ds(rows - 4, 2)], inside.at[1]),
    ]
    load_wc = copies.start(wc_hbm, wc)
    late = [
        copies.start(plow_hbm, plow),
        copies.start(phigh_hbm, phigh),
        copies.start(glow_hbm, glow),
        copies.start(ghigh_hbm, ghigh),
        copies.start(gklow_hbm, gklow),
        copies.start(gkhigh_hbm, gkhigh),
    ]
    for copy in loads:
        copy.wait()

    for side in range(2):
        for cell in range(cells):
            halo = packets.at[side, cell]
            at = 0 if side == 0 else 2
            low_pad[side, cell, at] = halo[2, :, 0:low_ch].astype(F32)
            low_pad[side, cell, pl.ds(1 - side, 2)] = low[side, cell].astype(F32)
            at = 0 if side == 0 else 5
            high_pad[side, cell, at, 0:cols] = halo[3, :, 0:high_ch].astype(F32)
            high_pad[side, cell, at, cols:] = halo[3, :, high_ch : 2 * high_ch].astype(F32)
            high_pad[side, cell, pl.ds(1 - side, 5)] = high[side, cell].astype(F32)
        depthwise(frames, high_pad.at[side], khigh, high_student.at[side])
        depthwise(frames, low_pad.at[side], klow, low_student.at[side])

    for side in range(2):
        for cell in range(cells):
            for k in range(2):
                whole = (edge[side, cell, k] + packets[side, cell, k, :, 0:out].astype(F32)).astype(BF16).astype(F32)
                if k == side:
                    whole = jnp.where(jnp.full(whole.shape, place[1 + side]) == 0, whole, 0.0)
                else:
                    feature[side, cell] = whole
                for j, value in enumerate(gate_rows(whole)):
                    gated[j, side, cell, 2 * side + k] = value
                for j, value in enumerate(gate_rows(inside[side, cell, k].astype(F32))):
                    gated[j, side, cell, 2 - 2 * side + k] = value

    for copy in late:
        copy.wait()
    student = low_student[...].reshape(-1, low_ch)
    _, back = level(student, feature[...].reshape(-1, out), plow[...], scale_low, low_back, glow)
    low_back[...] = back.reshape(low_back.shape)
    for side in range(2):
        kernel_gradient(frames, low_pad.at[side], low_back.at[side], gklow, False)

    load_wc.wait()
    second_feature(frames, gated, wc, 2, fine)
    for side in range(2):
        for cell in range(cells):
            student = high_student[side, cell].reshape(-1, high_ch)
            target = fine_target(fine.at[side, cell], slice(0, 2))
            value, back = level(student, target, phigh[...], scale_high, high_back, ghigh)
            mismatch[side, cell] = value.astype(BF16).reshape(4, 2 * cols, out)
            high_back[side, cell] = back.reshape(4, 2 * cols, high_ch)
    stores = [
        copies.start(mismatch.at[0], mismatch_hbm.at[:, pl.ds(0, 4)]),
        copies.start(mismatch.at[1], mismatch_hbm.at[:, pl.ds(2 * rows - 4, 4)]),
    ]
    for side in range(2):
        kernel_gradient(frames, high_pad.at[side], high_back.at[side], gkhigh, False)

    low_rows, high_rows = low_ch // shards, high_ch // shards
    shard_sums[...] = jnp.zeros_like(shard_sums)
    width = gklow.shape[1]
    lane = lax.broadcasted_iota(jnp.int32, gklow.shape, 1)
    wide_high = gkhigh[...]
    if high_ch < width:
        wide_high = jnp.concatenate([wide_high, jnp.zeros((wide_high.shape[0], width - high_ch), F32)], axis=1)
    for s in range(shards):
        shard_sums[s, 0:low_rows, 0:out] = glow[s * low_rows : (s + 1) * low_rows]
        shard_sums[s, low_rows : low_rows + high_rows, 0:out] = ghigh[s * high_rows : (s + 1) * high_rows]
        from_low = pltpu.roll(gklow[...], (width - s * low_rows) % width, 1)
        from_high = pltpu.roll(wide_high, (width + low_rows - s * high_rows) % width, 1)
        both = jnp.where(lane < low_rows, from_low, jnp.where(lane < low_rows + high_rows, from_high, 0.0))
        shard_sums[s, low_rows + high_rows : low_rows + high_rows + 32, 0:width] = both
    if shards == 1:
        keep[0] = shard_sums[0]
        send[0] = shard_sums[0].astype(BF16)
    else:
        bit = lax.rem(mine, 2)
        for k in range(shards // 2):
            keep[k] = shard_sums[2 * k + bit]
            send[k] = shard_sums[2 * k + 1 - bit].astype(BF16)
    stores.append(copies.start(send, send_hbm))
    stores.append(copies.start(keep, keep_hbm))
    for copy in stores:
        copy.wait()


def pairs(count, bit):
    return [(i, i ^ bit) for i in range(count)]


def sum_over_devices(keep, send, clips, tiles):
    if clips > 1:
        mine = lax.axis_index("clip")
        keep = keep + lax.ppermute(send, "clip", pairs(clips, 1)).astype(F32)
        bit = 2
        while bit < clips:
            halves = keep.reshape((keep.shape[0] // 2, 2) + keep.shape[1:])
            own = lax.rem(lax.div(mine, bit), 2)
            send = lax.dynamic_index_in_dim(halves, 1 - own, 1, False).astype(BF16)
            keep = lax.dynamic_index_in_dim(halves, own, 1, False)
            keep = keep + lax.ppermute(send, "clip", pairs(clips, bit)).astype(F32)
            bit *= 2
    total = keep[0]
    bit = 1
    while bit < tiles:
        bits = (bit, 2 * bit, 3 * bit) if 2 * bit < tiles else (bit,)
        out = total.astype(BF16)
        got = [lax.ppermute(out, "space", pairs(tiles, b)) for b in bits]
        for part in got:
            total = total + part.astype(F32)
        bit *= 2 ** (2 if len(bits) > 1 else 1)
    return total


def on_device(teacher_input, conv_first, conv_second, student_low, student_high, kernel_low, kernel_high, adapter_low, adapter_high):
    clips, tiles = lax.axis_size("clip"), lax.axis_size("space")
    held, frames, rows, cols, depth = teacher_input.shape
    cells = held * frames
    out = conv_first.shape[-1]
    low_ch, high_ch = student_low.shape[-1], student_high.shape[-1]
    low_count = held * frames * rows * cols * clips * tiles
    scales = (1.0 / low_count, 1.0 / (4 * low_count))
    inner = rows - 4
    x = teacher_input.reshape(cells, rows, cols, depth)
    low = student_low.reshape(cells, rows, cols, low_ch)
    high = student_high.reshape(cells, 2 * rows, 2 * cols, high_ch)
    klow, khigh = kernel_low.reshape(27, low_ch), kernel_high.reshape(27, high_ch)
    sems = pltpu.SemaphoreType.DMA

    def hbm(shape, dtype):
        return pltpu.HBM(shape, dtype)

    def vm(*specs):
        return [pltpu.VMEM(shape, dtype) for shape, dtype in specs]

    packet = ((cells, 4, cols, max(out, low_ch, 2 * high_ch)), BF16)
    inner_spec = ((cells, rows - 2, cols, out), BF16)
    edge_spec = ((2, cells, 2, cols, out), F32)
    inner_feature, edge, up, down = pl.pallas_call(
        functools.partial(first_kernel, frames),
        out_shape=(hbm(*inner_spec), hbm(*edge_spec), hbm(*packet), hbm(*packet)),
        in_specs=[HBM] * 4,
        out_specs=(HBM,) * 4,
        scratch_shapes=vm(
            (x.shape, BF16),
            (conv_first.shape, BF16),
            ((3, cells, rows + 2, cols, out), F32),
            inner_spec,
            edge_spec,
            packet,
            packet,
            ((2, cells, cols, low_ch), BF16),
            ((2, cells, 2 * cols, high_ch), BF16),
        )
        + [sems((18,))],
        compiler_params=pltpu.CompilerParams(vmem_limit_bytes=56 * MIB),
        cost_estimate=pl.CostEstimate(flops=3 * 10**9, bytes_accessed=9 * 10**6, transcendentals=0),
        name="teacher_first",
    )(x, conv_first, low, high)

    forward = [(i, i + 1) for i in range(tiles - 1)]
    above = lax.ppermute(down, "space", forward)
    below = lax.ppermute(up, "space", [(b, a) for a, b in forward])

    wc_spec = ((2, 2, 3, 2, 2, out, out), BF16)
    grads = (((low_ch, out), F32), ((high_ch, out), F32), ((32, low_ch), F32), ((32, high_ch), F32))
    weights = (((27, low_ch), F32), ((27, high_ch), F32), (adapter_low.shape, BF16), (adapter_high.shape, BF16))
    wc, mismatch, *sums = pl.pallas_call(
        functools.partial(second_kernel, frames, *scales),
        out_shape=(hbm(*wc_spec), hbm((cells, 2 * rows, 2 * cols, out), BF16)) + tuple(hbm(*g) for g in grads),
        in_specs=[HBM] * 8,
        out_specs=(HBM,) * 6,
        scratch_shapes=vm(
            inner_spec,
            (conv_second.shape, BF16),
            (low.shape, BF16),
            ((cells, 2 * inner + 2, 2 * cols, high_ch), BF16),
            *weights,
            wc_spec,
            ((cells, 2 * inner, 2 * cols, out), BF16),
            *grads,
            ((3, 1, cells, rows - 2, cols, out), BF16),
            ((1, cells, inner, 2, out // 128, 2 * cols, 128), F32),
            ((cells, rows, cols, low_ch), F32),
            ((cells, 2 * inner + 2, 2 * cols, high_ch), F32),
            ((cells, rows - 2, cols, low_ch), BF16),
            ((cells, 2 * inner, 2 * cols, high_ch), BF16),
            ((cells, rows - 2, cols, low_ch), F32),
            ((cells, 2 * inner, 2 * cols, high_ch), F32),
        )
        + [sems((14,))],
        compiler_params=pltpu.CompilerParams(vmem_limit_bytes=56 * MIB),
        cost_estimate=pl.CostEstimate(flops=5 * 10**9, bytes_accessed=20 * 10**6, transcendentals=0),
        name="inner_rows",
    )(inner_feature, conv_second, low, high, klow, khigh, adapter_low, adapter_high)

    clip, tile = lax.axis_index("clip"), lax.axis_index("space")
    place = jnp.stack([clip, (tile == 0).astype(jnp.int32), (tile == tiles - 1).astype(jnp.int32)])
    shard_rows = low_ch // clips + high_ch // clips + 32
    shard_rows += -shard_rows % 16
    shard = (max(clips // 2, 1), shard_rows, out)
    mismatch, keep, send = pl.pallas_call(
        functools.partial(third_kernel, frames, clips, *scales),
        out_shape=(hbm(mismatch.shape, BF16), hbm(shard, F32), hbm(shard, BF16)),
        in_specs=[pl.BlockSpec(memory_space=pltpu.SMEM)] + [HBM] * 16,
        out_specs=(HBM,) * 3,
        input_output_aliases={16: 0},
        scratch_shapes=vm(
            ((2,) + packet[0], BF16),
            edge_spec,
            ((2, cells, 2, cols, out), BF16),
            ((2, cells, 2, cols, low_ch), BF16),
            ((2, cells, 5, 2 * cols, high_ch), BF16),
            *weights,
            wc_spec,
            *grads,
            ((2, cells, 4, 2 * cols, out), BF16),
            (shard, F32),
            (shard, BF16),
            ((2, cells, cols, out), F32),
            ((3, 2, cells, 4, cols, out), BF16),
            ((2, cells, 2, 2, out // 128, 2 * cols, 128), F32),
            ((2, cells, 3, cols, low_ch), F32),
            ((2, cells, 6, 2 * cols, high_ch), F32),
            ((2, cells, 1, cols, low_ch), BF16),
            ((2, cells, 4, 2 * cols, high_ch), BF16),
            ((2, cells, 1, cols, low_ch), F32),
            ((2, cells, 4, 2 * cols, high_ch), F32),
            ((clips, shard_rows, out), F32),
        )
        + [sems((22,))],
        compiler_params=pltpu.CompilerParams(vmem_limit_bytes=56 * MIB),
        cost_estimate=pl.CostEstimate(flops=3 * 10**9, bytes_accessed=20 * 10**6, transcendentals=0),
        name="border_rows",
    )(place, above, below, edge, inner_feature, low, high, klow, khigh, adapter_low, adapter_high, wc, *sums, mismatch)

    total = sum_over_devices(keep, send, clips, tiles)
    low_rows, high_rows = low_ch // clips, high_ch // clips
    top = low_rows + high_rows
    return (
        total[:low_rows],
        total[top : top + 27, :low_rows].reshape(3, 3, 3, low_rows),
        total[low_rows:top],
        total[top : top + 27, low_rows : low_rows + high_rows].reshape(3, 3, 3, high_rows),
        mismatch.reshape(held, frames, 2 * rows, 2 * cols, out),
    )


def solution(mesh):
    tiled = P("clip", None, "space", None, None)
    return jax.shard_map(
        on_device,
        mesh=mesh,
        in_specs=(tiled, P(), P(), tiled, tiled, P(), P(), P(), P()),
        out_specs=(P("clip", None), P(None, None, None, "clip"), P("clip", None), P(None, None, None, "clip"), tiled),
        check_vma=False,
    )
```

time: 274 us -> 59.7 us (0.22)
  matrix products: 83.7 us -> 0 us
  waiting for transfers between devices: 75.9 us -> 11.5 us
  blocking collectives: 39.1 us -> 0 us
  Pallas kernels: 0 us -> 24.9 us
  local copies, waits for them, and re-layouts: 20.5 us -> 4.54 us
  between operations: 14.4 us -> 0.77 us
  other arithmetic: 14.2 us -> 1.71 us
  starting transfers between devices: 25.3 us -> 16 us
    dot_general x60 -> x0, matrix products: 83.7 us -> none  [the longest x54 76 us: conv_taps(): jnp.dot(window_part, weight[tap_t, tap_h, tap_w], preferred_element_type=...]
    psum x1 -> x0, blocking collectives: 39.1 us -> none  [on_device(): lax.psum((adapter_one, adapter_two, kernel_one, kernel_two), 'space')]
    psum x1 -> x0, waiting for transfers between devices: 32.7 us -> none  [on_device(): lax.psum((adapter_one, adapter_two, kernel_one, kernel_two), 'space')]
    pallas_call x0 -> x3, Pallas kernels: none -> 24.9 us  [the longest x1 9.22 us: on_device(): pl.pallas_call(functools.partial(second_kernel, frames, *scales), out_sha...]
    reduce_scatter x2 -> x0, waiting for transfers between devices: 21.1 us -> none  [the longest x1 21.1 us: on_device(): lax.psum_scatter(summed[1], 'clip', scatter_dimension=0, tiled=True)]
    unnamed x7 -> x0, waiting for transfers between devices: 17.1 us -> none
    ppermute x8, starting transfers between devices: 24.9 us -> 16 us  [the longest x4 8.22 us: sum_over_devices(): got = [lax.ppermute(out, 'space', pairs(tiles, b)) for b in bits]]
    convert_element_type x4 -> x2, other arithmetic: 8.96 us -> 0.06 us  [sum_over_devices(): out = total.astype(BF16)]
  transfers between devices with their start and end apart: 13 -> 8, of which waited for: 4 -> 5; matrix products, arithmetic and copies ran while one was open for 39% -> 3% of each run, Pallas kernels for 0% -> 15%
where the time goes in v1:
time: 59.7 us; the launch traced here: 59.5 us
  Pallas kernels  24.9 us (42%)
  starting transfers between devices  16 us (27%)
  waiting for transfers between devices  11.5 us (19%)
  local copies, waits for them, and re-layouts  4.54 us (8%)
  other arithmetic  1.71 us (3%)
  between operations  0.77 us (1%)
    pallas_call x1, Pallas kernels, on_device(): pl.pallas_call(functools.partial(second_kernel, frames, *scales), out_sha...  9.22 us
    pallas_call x1, Pallas kernels, on_device(): pl.pallas_call(functools.partial(third_kernel, frames, clips, *scales), o...  8.75 us
    ppermute x4, starting transfers between devices, sum_over_devices(): got = [lax.ppermute(out, 'space', pairs(tiles, b)) for b in bits]  8.22 us
    ppermute x4, waiting for transfers between devices, sum_over_devices(): got = [lax.ppermute(out, 'space', pairs(tiles, b)) for b in bits]  7.24 us
    pallas_call x1, Pallas kernels, on_device(): pl.pallas_call(functools.partial(first_kernel, frames), out_shape=(hbm(*i...  6.94 us
    ppermute x1, starting transfers between devices, on_device(): above = lax.ppermute(down, 'space', forward)  4.85 us
    ppermute x1, waiting for transfers between devices, sum_over_devices(): keep = keep + lax.ppermute(send, 'clip', pairs(clips, bit)).astype(F32)  2.75 us
    ppermute x1, starting transfers between devices, sum_over_devices(): keep = keep + lax.ppermute(send, 'clip', pairs(clips, bit)).astype(F32)  1.58 us
  transfers between devices with their start and end apart: 8, of which 5 were waited for; matrix products, arithmetic and copies ran while one was open for 3% of the time, Pallas kernels for 15%

profile of v1, /device:TPU:0, one launch (start us, length us, event | category | flops | bytes accessed | tf_op | source)
XLA Modules:
  0.0 59.5 jit_solution(16330457721971301647)
XLA Ops:
  0.6 0.0 copy-start
  0.6 0.0 copy-start.1
  0.7 6.9 %teacher_first.1 = (bf16[2,6,32,256]{3,2,1,0:T(8,128)(2,1)}, f32[2,2,2,32,256]{4,3,2,1,0:T(8,128)}, bf16[2,4,32,256]{3,2,1,0:T(8,128)(2,1)}, bf16[2,4,32,256]{3,2,1,0:T(8,128)(2,1)}) custom-call(bf16[2,8,32,512]{3,2,1,0:T(8,128)(2,1)} %bitcast.15, bf16[3,3,3,512,256]{4,3,2,1,0:T(8,128)(2,1)} %w_hbm.2, bf16[2,8,32,256]{3,2,1,0:T(8,128)(2,1)} %bitcast.19, ...), custom_call_target="tpu_custom_call" | custom-call | flops 3000000000 | bytes 9000000 | tf_op jit(solution)/shard_map/teacher_first/pallas_call | solution.py:507
  7.6 4.8 %collective-permute-start = (bf16[2,4,32,256]{3,2,1,0:T(8,128)(2,1)}, bf16[2,4,32,256]{3,2,1,0:T(8,128)(2,1)S(1)}, u32[]{:S(2)}, u32[]{:S(2)}) collective-permute-start(bf16[2,4,32,256]{3,2,1,0:T(8,128)(2,1)} %get-tuple-element.18), channel_id=1, source_target_pairs={{0,1},{1,2},{2,3},{3,4},{4,5},{5,6},{6,7},{8,9},{9,10},{10,11},{11... | collective-permute-start | bytes 393224 | tf_op jit(solution)/shard_map/ppermute | solution.py:530
  12.5 1.3 %collective-permute-start.1 = (bf16[2,4,32,256]{3,2,1,0:T(8,128)(2,1)}, bf16[2,4,32,256]{3,2,1,0:T(8,128)(2,1)S(1)}, u32[]{:S(2)}, u32[]{:S(2)}) collective-permute-start(bf16[2,4,32,256]{3,2,1,0:T(8,128)(2,1)} %get-tuple-element.19), channel_id=1, source_target_pairs={{1,0},{2,1},{3,2},{4,3},{5,4},{6,5},{7,6},{9,8},{10,9},{11,10},{12... | collective-permute-start | bytes 393224 | tf_op jit(solution)/shard_map/ppermute | solution.py:531
  13.8 0.0 copy-done
  13.8 0.6 %reshape.44.klow_hbm = f32[27,256]{1,0:T(8,128)} reshape(f32[3,3,3,256]{3,2,1,0:T(4,128)S(1)} %copy-done) | data formatting | bytes 55296 | tf_op jit(solution)/shard_map/reshape | solution.py:495
  14.4 0.0 copy-done.1
  14.4 0.6 %reshape.45.khigh_hbm = f32[27,128]{1,0:T(8,128)} reshape(f32[3,3,3,128]{3,2,1,0:T(4,128)S(1)} %copy-done.1) | data formatting | bytes 27648 | tf_op jit(solution)/shard_map/reshape | solution.py:495
  15.0 9.2 %inner_rows.1 = (bf16[2,2,3,2,2,256,256]{6,5,4,3,2,1,0:T(8,128)(2,1)}, bf16[2,16,64,256]{3,2,1,0:T(8,128)(2,1)}, f32[256,256]{1,0:T(8,128)}, f32[128,256]{1,0:T(...) custom-call(bf16[2,6,32,256]{3,2,1,0:T(8,128)(2,1)} %get-tuple-element.21.inner_hbm, bf16[3,3,3,256,256]{4,3,2,1,0:T(8,128)(2,1)} %w_hbm.3, ...), custom_call_target="tpu_custom_call" | custom-call | flops 5000000000 | bytes 20000000 | tf_op jit(solution)/shard_map/inner_rows/pallas_call | solution.py:536
  24.2 0.7 %pad_add_fusion.place = s32[3]{0:T(128)} fusion(s32[1]{0:T(128)} %bitcast.2, s32[1]{0:T(128)} %bitcast.1, s32[1]{0:T(128)} %bitcast), kind=kLoop, calls=%fused_computation.8 | loop fusion | flops 6 | bytes 24 | tf_op jit(solution)/shard_map/stack | solution.py:566
  24.9 0.0 collective-permute-done.above_hbm
  24.9 0.0 copy-start.2
  24.9 0.0 collective-permute-done.1.below_hbm
  24.9 0.0 copy-start.3
  24.9 0.6 %copy-done.2 = bf16[2,4,32,256]{3,2,1,0:T(8,128)(2,1)} copy-done((bf16[2,4,32,256]{3,2,1,0:T(8,128)(2,1)}, bf16[2,4,32,256]{3,2,1,0:T(8,128)(2,1)S(1)}, u32[]{:S(2)}) %copy-start.2) | copy-done | bytes 131096
  25.6 0.1 copy-done.3
  25.6 8.7 %border_rows.1 = (bf16[2,16,64,256]{3,2,1,0:T(8,128)(2,1)}, f32[2,128,256]{2,1,0:T(8,128)}, bf16[2,128,256]{2,1,0:T(8,128)(2,1)}) custom-call(s32[3]{0:T(128)} %pad_add_fusion.place, bf16[2,4,32,256]{3,2,1,0:T(8,128)(2,1)} %copy-done.2, bf16[2,4,32,256]{3,2,1,0:T(8,128)(2,1)} %copy-done.3, ...), custom_call_target="tpu_custom_call", output_to_operand_aliasing={{0}: (16, {})} | custom-call | flops 3000000000 | bytes 20000000 | tf_op jit(solution)/shard_map/border_rows/pallas_call | solution.py:570
  34.4 0.1 collective-permute-start.2
  34.5 1.5 %collective-permute-done.2 = bf16[2,128,256]{2,1,0:T(8,128)(2,1)S(1)} collective-permute-done((bf16[2,128,256]{2,1,0:T(8,128)(2,1)}, bf16[2,128,256]{2,1,0:T(8,128)(2,1)S(1)}, u32[]{:S(2)}, u32[]{:S(2)}) %collective-permute-start.2) | collective-permute-done | bytes 131104 | tf_op jit(solution)/shard_map/ppermute | solution.py:462
  36.0 1.0 %convert_add_fusion = f32[2,128,256]{2,1,0:T(8,128)S(1)} fusion(f32[2,128,256]{2,1,0:T(8,128)} %get-tuple-element.28, bf16[2,128,256]{2,1,0:T(8,128)(2,1)S(1)} %collective-permute-done.2), kind=kLoop, calls=%fused_computation | loop fusion | flops 131072 | bytes 655360 | tf_op jit(solution)/shard_map/add | solution.py:462
  37.0 1.6 %collective-permute-start.3 = (bf16[1,128,256]{2,1,0:T(8,128)(2,1)S(1)}, bf16[1,128,256]{2,1,0:T(8,128)(2,1)S(1)}, u32[]{:S(2)}, u32[]{:S(2)}) collective-permute-start(bf16[1,128,256]{2,1,0:T(8,128)(2,1)S(1)} %dynamic-slice_convert_fusion), channel_id=1, source_target_pairs={{0,16},{8,24},{16,0},{24,8},{1,17},{9,25},{17,1},{25,9},{2,18},{10... | collective-permute-start | bytes 196616 | tf_op jit(solution)/shard_map/ppermute | solution.py:469
  38.6 2.7 %collective-permute-done.3 = bf16[1,128,256]{2,1,0:T(8,128)(2,1)S(1)} collective-permute-done((bf16[1,128,256]{2,1,0:T(8,128)(2,1)S(1)}, bf16[1,128,256]{2,1,0:T(8,128)(2,1)S(1)}, u32[]{:S(2)}, u32[]{:S(2)}) %collective-permute-start.3) | collective-permute-done | bytes 65568 | tf_op jit(solution)/shard_map/ppermute | solution.py:469
  41.4 2.7 %collective-permute-start.4 = (bf16[128,256]{1,0:T(8,128)(2,1)S(1)}, bf16[128,256]{1,0:T(8,128)(2,1)S(1)}, u32[]{:S(2)}, u32[]{:S(2)}) collective-permute-start(bf16[128,256]{1,0:T(8,128)(2,1)S(1)} %bitcast_convert_fusion), channel_id=1, source_target_pairs={{0,1},{1,0},{2,3},{3,2},{4,5},{5,4},{6,7},{7,6},{8,9},{9,8},{10,11... | collective-permute-start | bytes 196616 | tf_op jit(solution)/shard_map/ppermute | solution.py:476
  44.1 1.6 %collective-permute-start.5 = (bf16[128,256]{1,0:T(8,128)(2,1)S(1)}, bf16[128,256]{1,0:T(8,128)(2,1)S(1)}, u32[]{:S(2)}, u32[]{:S(2)}) collective-permute-start(bf16[128,256]{1,0:T(8,128)(2,1)S(1)} %bitcast_convert_fusion), channel_id=1, source_target_pairs={{0,2},{1,3},{2,0},{3,1},{4,6},{5,7},{6,4},{7,5},{8,10},{9,11},{10,... | collective-permute-start | bytes 196616 | tf_op jit(solution)/shard_map/ppermute | solution.py:476
  45.7 0.9 %collective-permute-start.6 = (bf16[128,256]{1,0:T(8,128)(2,1)S(1)}, bf16[128,256]{1,0:T(8,128)(2,1)S(1)}, u32[]{:S(2)}, u32[]{:S(2)}) collective-permute-start(bf16[128,256]{1,0:T(8,128)(2,1)S(1)} %bitcast_convert_fusion), channel_id=1, source_target_pairs={{0,3},{1,2},{2,1},{3,0},{4,7},{5,6},{6,5},{7,4},{8,11},{9,10},{10,... | collective-permute-start | bytes 196616 | tf_op jit(solution)/shard_map/ppermute | solution.py:476
  46.5 0.0 collective-permute-done.4
  46.5 2.4 %collective-permute-done.5 = bf16[128,256]{1,0:T(8,128)(2,1)S(1)} collective-permute-done((bf16[128,256]{1,0:T(8,128)(2,1)S(1)}, bf16[128,256]{1,0:T(8,128)(2,1)S(1)}, u32[]{:S(2)}, u32[]{:S(2)}) %collective-permute-start.5) | collective-permute-done | bytes 65568 | tf_op jit(solution)/shard_map/ppermute | solution.py:476
  49.0 1.9 %collective-permute-done.6 = bf16[128,256]{1,0:T(8,128)(2,1)S(1)} collective-permute-done((bf16[128,256]{1,0:T(8,128)(2,1)S(1)}, bf16[128,256]{1,0:T(8,128)(2,1)S(1)}, u32[]{:S(2)}, u32[]{:S(2)}) %collective-permute-start.6) | collective-permute-done | bytes 65568 | tf_op jit(solution)/shard_map/ppermute | solution.py:476
  50.9 3.1 %collective-permute-start.7 = (bf16[128,256]{1,0:T(8,128)(2,1)S(1)}, bf16[128,256]{1,0:T(8,128)(2,1)S(1)}, u32[]{:S(2)}, u32[]{:S(2)}) collective-permute-start(bf16[128,256]{1,0:T(8,128)(2,1)S(1)} %get-tuple-element.31), channel_id=1, source_target_pairs={{0,4},{1,5},{2,6},{3,7},{4,0},{5,1},{6,2},{7,3},{8,12},{9,13},{10,... | collective-permute-start | bytes 196616 | tf_op jit(solution)/shard_map/ppermute | solution.py:476
  53.9 2.9 %collective-permute-done.7 = bf16[128,256]{1,0:T(8,128)(2,1)S(1)} collective-permute-done((bf16[128,256]{1,0:T(8,128)(2,1)S(1)}, bf16[128,256]{1,0:T(8,128)(2,1)S(1)}, u32[]{:S(2)}, u32[]{:S(2)}) %collective-permute-start.7) | collective-permute-done | bytes 65568 | tf_op jit(solution)/shard_map/ppermute | solution.py:476
  56.9 0.6 %slice.16 = f32[64,256]{1,0:T(8,128)} slice(f32[128,256]{1,0:T(8,128)S(1)} %convert_add_fusion.1), slice={[0:64], [0:256]} | slice | bytes 131072 | tf_op jit(solution)/shard_map/slice | solution.py:609
  57.6 0.1 slice.19
  57.6 0.6 %slice.18 = f32[32,256]{1,0:T(8,128)} slice(f32[128,256]{1,0:T(8,128)S(1)} %convert_add_fusion.1), slice={[64:96], [0:256]} | slice | bytes 65536 | tf_op jit(solution)/shard_map/slice | solution.py:611
  58.2 0.6 %reshape.46 = f32[3,3,3,64]{3,2,1,0:T(4,128)} reshape(f32[27,64]{1,0:T(8,128)S(1)} %slice.17) | data formatting | bytes 13824 | tf_op jit(solution)/shard_map/reshape | solution.py:610
  58.9 0.6 %reshape.47 = f32[3,3,3,32]{3,2,1,0:T(4,128)} reshape(f32[27,32]{1,0:T(8,128)S(1)} %slice.19) | data formatting | bytes 6912 | tf_op jit(solution)/shard_map/reshape | solution.py:612
  (5 shorter events, 0.1 us)
Async XLA Ops:
  0.6 13.1 %copy-start = (f32[3,3,3,256]{3,2,1,0:T(4,128)S(1)}, f32[3,3,3,256]{3,2,1,0:T(4,128)}, u32[]{:S(2)}) copy-start(f32[3,3,3,256]{3,2,1,0:T(4,128)} %param.14) | copy-start | bytes 82948
  0.6 13.8 %copy-start.1 = (f32[3,3,3,128]{3,2,1,0:T(4,128)S(1)}, f32[3,3,3,128]{3,2,1,0:T(4,128)}, u32[]{:S(2)}) copy-start(f32[3,3,3,128]{3,2,1,0:T(4,128)} %param.15) | copy-start | bytes 41476
  7.6 17.3 %collective-permute-start = (bf16[2,4,32,256]{3,2,1,0:T(8,128)(2,1)}, bf16[2,4,32,256]{3,2,1,0:T(8,128)(2,1)S(1)}, u32[]{:S(2)}, u32[]{:S(2)}) collective-permute-start(bf16[2,4,32,256]{3,2,1,0:T(8,128)(2,1)} %get-tuple-element.18), channel_id=1, source_target_pairs={{0,1},{1,2},{2,3},{3,4},{4,5},{5,6},{6,7},{8,9},{9,10},{10,11},{11... | collective-permute-start | bytes 393224 | tf_op jit(solution)/shard_map/ppermute | solution.py:530
  12.5 12.5 %collective-permute-start.1 = (bf16[2,4,32,256]{3,2,1,0:T(8,128)(2,1)}, bf16[2,4,32,256]{3,2,1,0:T(8,128)(2,1)S(1)}, u32[]{:S(2)}, u32[]{:S(2)}) collective-permute-start(bf16[2,4,32,256]{3,2,1,0:T(8,128)(2,1)} %get-tuple-element.19), channel_id=1, source_target_pairs={{1,0},{2,1},{3,2},{4,3},{5,4},{6,5},{7,6},{9,8},{10,9},{11,10},{12... | collective-permute-start | bytes 393224 | tf_op jit(solution)/shard_map/ppermute | solution.py:531
  24.9 0.7 %copy-start.2 = (bf16[2,4,32,256]{3,2,1,0:T(8,128)(2,1)}, bf16[2,4,32,256]{3,2,1,0:T(8,128)(2,1)S(1)}, u32[]{:S(2)}) copy-start(bf16[2,4,32,256]{3,2,1,0:T(8,128)(2,1)S(1)} %collective-permute-done.above_hbm) | copy-start | bytes 393220
  24.9 0.7 %copy-start.3 = (bf16[2,4,32,256]{3,2,1,0:T(8,128)(2,1)}, bf16[2,4,32,256]{3,2,1,0:T(8,128)(2,1)S(1)}, u32[]{:S(2)}) copy-start(bf16[2,4,32,256]{3,2,1,0:T(8,128)(2,1)S(1)} %collective-permute-done.1.below_hbm) | copy-start | bytes 393220
  34.4 1.6 %collective-permute-start.2 = (bf16[2,128,256]{2,1,0:T(8,128)(2,1)}, bf16[2,128,256]{2,1,0:T(8,128)(2,1)S(1)}, u32[]{:S(2)}, u32[]{:S(2)}) collective-permute-start(bf16[2,128,256]{2,1,0:T(8,128)(2,1)} %get-tuple-element.29), channel_id=1, source_target_pairs={{0,8},{8,0},{16,24},{24,16},{1,9},{9,1},{17,25},{25,17},{2,10},{10... | collective-permute-start | bytes 393224 | tf_op jit(solution)/shard_map/ppermute | solution.py:462
  37.0 4.3 %collective-permute-start.3 = (bf16[1,128,256]{2,1,0:T(8,128)(2,1)S(1)}, bf16[1,128,256]{2,1,0:T(8,128)(2,1)S(1)}, u32[]{:S(2)}, u32[]{:S(2)}) collective-permute-start(bf16[1,128,256]{2,1,0:T(8,128)(2,1)S(1)} %dynamic-slice_convert_fusion), channel_id=1, source_target_pairs={{0,16},{8,24},{16,0},{24,8},{1,17},{9,25},{17,1},{25,9},{2,18},{10... | collective-permute-start | bytes 196616 | tf_op jit(solution)/shard_map/ppermute | solution.py:469
  41.4 5.2 %collective-permute-start.4 = (bf16[128,256]{1,0:T(8,128)(2,1)S(1)}, bf16[128,256]{1,0:T(8,128)(2,1)S(1)}, u32[]{:S(2)}, u32[]{:S(2)}) collective-permute-start(bf16[128,256]{1,0:T(8,128)(2,1)S(1)} %bitcast_convert_fusion), channel_id=1, source_target_pairs={{0,1},{1,0},{2,3},{3,2},{4,5},{5,4},{6,7},{7,6},{8,9},{9,8},{10,11... | collective-permute-start | bytes 196616 | tf_op jit(solution)/shard_map/ppermute | solution.py:476
  44.1 4.9 %collective-permute-start.5 = (bf16[128,256]{1,0:T(8,128)(2,1)S(1)}, bf16[128,256]{1,0:T(8,128)(2,1)S(1)}, u32[]{:S(2)}, u32[]{:S(2)}) collective-permute-start(bf16[128,256]{1,0:T(8,128)(2,1)S(1)} %bitcast_convert_fusion), channel_id=1, source_target_pairs={{0,2},{1,3},{2,0},{3,1},{4,6},{5,7},{6,4},{7,5},{8,10},{9,11},{10,... | collective-permute-start | bytes 196616 | tf_op jit(solution)/shard_map/ppermute | solution.py:476
  45.7 5.2 %collective-permute-start.6 = (bf16[128,256]{1,0:T(8,128)(2,1)S(1)}, bf16[128,256]{1,0:T(8,128)(2,1)S(1)}, u32[]{:S(2)}, u32[]{:S(2)}) collective-permute-start(bf16[128,256]{1,0:T(8,128)(2,1)S(1)} %bitcast_convert_fusion), channel_id=1, source_target_pairs={{0,3},{1,2},{2,1},{3,0},{4,7},{5,6},{6,5},{7,4},{8,11},{9,10},{10,... | collective-permute-start | bytes 196616 | tf_op jit(solution)/shard_map/ppermute | solution.py:476
  50.9 6.0 %collective-permute-start.7 = (bf16[128,256]{1,0:T(8,128)(2,1)S(1)}, bf16[128,256]{1,0:T(8,128)(2,1)S(1)}, u32[]{:S(2)}, u32[]{:S(2)}) collective-permute-start(bf16[128,256]{1,0:T(8,128)(2,1)S(1)} %get-tuple-element.31), channel_id=1, source_target_pairs={{0,4},{1,5},{2,6},{3,7},{4,0},{5,1},{6,2},{7,3},{8,12},{9,13},{10,... | collective-permute-start | bytes 196616 | tf_op jit(solution)/shard_map/ppermute | solution.py:476

commit v2 on v1

--- a/solution.py
+++ b/solution.py
@@ -9,7 +9,12 @@
 
 F32, BF16 = jnp.float32, jnp.bfloat16
 HBM = pl.BlockSpec(memory_space=pltpu.HBM)
+VMEM = pl.BlockSpec(memory_space=pltpu.VMEM)
 MIB = 1 << 20
+
+
+def in_hbm(*arrays):
+    return [pltpu.with_memory_space_constraint(array, pltpu.HBM) for array in arrays]
 
 
 def shift_cols(value, by):
@@ -63,7 +68,7 @@
         return copy
 
 
-def first_kernel(frames, x_hbm, w_hbm, low_hbm, high_hbm, inner_hbm, edge_hbm, up_hbm, down_hbm, x_ref, w_buf, acc, inner, edge, up, down, low_row, high_row, sems):
+def first_kernel(frames, x_hbm, w_hbm, low_hbm, high_hbm, inner, edge, first, second, x_ref, w_buf, acc, low_row, high_row, sems):
     cells, rows, cols, depth = x_ref.shape
     out = w_buf.shape[-1]
     clips = cells // frames
@@ -89,10 +94,10 @@
             for tap_w in range(3):
                 weight = w_buf[tap, tap_h, tap_w]
                 for clip in range(clips):
-                    first = clip * frames
-                    rowset = x_ref[first + src : first + src + count].reshape(-1, depth)
+                    base = clip * frames
+                    rowset = x_ref[base + src : base + src + count].reshape(-1, depth)
                     product = dot(rowset, weight).reshape(count, rows, cols, out)
-                    spot = (tap_w, pl.ds(first + to, count), pl.ds(at, rows))
+                    spot = (tap_w, pl.ds(base + to, count), pl.ds(at, rows))
                     if tap == 1 and tap_h == 1:
                         acc[spot] = product
                     else:
@@ -104,16 +109,21 @@
     for copy in borders:
         copy.wait()
     low_ch, high_ch = low_row.shape[-1], high_row.shape[-1]
-    for k, packet in ((0, up), (1, down)):
-        for cell in range(cells):
-            for j in range(2):
-                value = gathered(cell, k * rows + j)
-                edge[k, cell, j] = value
-                packet[cell, j, :, 0:out] = value.astype(BF16)
-            packet[cell, 2, :, 0:low_ch] = low_row[k, cell]
-            packet[cell, 3, :, 0:high_ch] = high_row[k, cell, 0:cols]
-            packet[cell, 3, :, high_ch : 2 * high_ch] = high_row[k, cell, cols:]
-    stores = [copies.start(up, up_hbm), copies.start(down, down_hbm), copies.start(edge, edge_hbm)]
+    even = lax.rem(lax.axis_index("space"), 2) == 0
+    for cell in range(cells):
+        for j in range(2):
+            up, down = gathered(cell, j), gathered(cell, rows + j)
+            edge[0, cell, j], edge[1, cell, j] = up, down
+            first[cell, j, :, 0:out] = jnp.where(even, down, up).astype(BF16)
+            second[cell, j, :, 0:out] = jnp.where(even, up, down).astype(BF16)
+        up, down = low_row[0, cell].astype(F32), low_row[1, cell].astype(F32)
+        first[cell, 2, :, 0:low_ch] = jnp.where(even, down, up).astype(BF16)
+        second[cell, 2, :, 0:low_ch] = jnp.where(even, up, down).astype(BF16)
+        for half in range(2):
+            here, lanes = slice(half * cols, (half + 1) * cols), slice(half * high_ch, (half + 1) * high_ch)
+            up, down = high_row[0, cell, here].astype(F32), high_row[1, cell, here].astype(F32)
+            first[cell, 3, :, lanes] = jnp.where(even, down, up).astype(BF16)
+            second[cell, 3, :, lanes] = jnp.where(even, up, down).astype(BF16)
     for cell in range(cells):
 
         def gather(row, _, cell=cell):
@@ -121,9 +131,6 @@
             return 0
 
         lax.fori_loop(0, rows - 2, gather, 0)
-    stores.append(copies.start(inner, inner_hbm))
-    for copy in stores:
-        copy.wait()
 
 
 def phase_weights(w_ref, wc_ref):
@@ -193,8 +200,7 @@
                     for h in range(3):
                         field = padded[other, row + h, :, lanes]
                         for w in range(3):
-                            k = 9 * (t + first_tap) + 3 * h + w
-                            term = field * kernel_ref[k : k + 1, lanes]
+                            term = field * kernel_ref[t + first_tap, h, w : w + 1, lanes]
                             sums[w] = term if sums[w] is None else sums[w] + term
                 student[cell, row, :, lanes] = (
                     padded[cell, row + 1, :, lanes]
@@ -249,10 +255,9 @@
 
 def second_kernel(
     frames, scale_low, scale_high,
-    inner_hbm, w_hbm, low_hbm, high_hbm, klow_hbm, khigh_hbm, plow_hbm, phigh_hbm,
-    wc_hbm, mismatch_hbm, glow_hbm, ghigh_hbm, gklow_hbm, gkhigh_hbm,
-    feature, w_ref, low, high, klow, khigh, plow, phigh,
-    wc, mismatch, glow, ghigh, gklow, gkhigh,
+    feature, w_hbm, low_hbm, high_hbm, klow_hbm, khigh_hbm, plow_hbm, phigh_hbm,
+    wc, mismatch_hbm, glow, ghigh, gklow, gkhigh,
+    w_ref, low, high, klow, khigh, plow, phigh, mismatch,
     gated, fine, low_pad, high_pad, low_student, high_student, low_back, high_back, sems,
 ):
     cells, count, cols, out = feature.shape
@@ -261,12 +266,20 @@
     copies = Copies(sems)
     load_high = copies.start(high_hbm.at[:, pl.ds(3, 2 * inner + 2)], high)
     load_khigh = copies.start(khigh_hbm, khigh)
-    load_w = copies.start(w_hbm, w_ref)
     load_low = copies.start(low_hbm, low)
     load_klow = copies.start(klow_hbm, klow)
-    load_inner = copies.start(inner_hbm, feature)
+    load_w = copies.start(w_hbm, w_ref)
     load_plow = copies.start(plow_hbm, plow)
     load_phigh = copies.start(phigh_hbm, phigh)
+
+    for cell in range(cells):
+
+        def gate(row, _, cell=cell):
+            for k, value in enumerate(gate_rows(feature[cell, row].astype(F32))):
+                gated[k, 0, cell, row] = value
+            return 0
+
+        lax.fori_loop(0, count, gate, 0)
 
     load_high.wait()
     load_khigh.wait()
@@ -291,17 +304,6 @@
 
     load_w.wait()
     phase_weights(w_ref, wc)
-    stores = [copies.start(wc, wc_hbm)]
-
-    load_inner.wait()
-    for cell in range(cells):
-
-        def gate(row, _, cell=cell):
-            for k, value in enumerate(gate_rows(feature[cell, row].astype(F32))):
-                gated[k, 0, cell, row] = value
-            return 0
-
-        lax.fori_loop(0, count, gate, 0)
     second_feature(frames, gated, wc, inner, fine)
 
     load_plow.wait()
@@ -318,98 +320,86 @@
             value, back = level(student, target, phigh[...], scale_high, high_back, ghigh)
             mismatch[cell, here] = value.astype(BF16).reshape(4, 2 * cols, out)
             high_back[cell, here] = back.reshape(4, 2 * cols, -1)
-    stores.append(copies.start(mismatch, mismatch_hbm.at[:, pl.ds(4, 2 * inner)]))
-    stores.append(copies.start(ghigh, ghigh_hbm))
+    store = copies.start(mismatch, mismatch_hbm.at[:, pl.ds(4, 2 * inner)])
     for cell in range(cells):
         student = low_student[cell].reshape(-1, low.shape[-1])
         target = feature[cell].reshape(-1, out).astype(F32)
         _, back = level(student, target, plow[...], scale_low, low_back, glow)
         low_back[cell] = back.reshape(count, cols, -1)
-    stores.append(copies.start(glow, glow_hbm))
     kernel_gradient(frames, low_pad, low_back, gklow, True)
     kernel_gradient(frames, high_pad, high_back, gkhigh, True)
-    stores.append(copies.start(gklow, gklow_hbm))
-    stores.append(copies.start(gkhigh, gkhigh_hbm))
-    for copy in stores:
-        copy.wait()
+    store.wait()
 
 
 def third_kernel(
-    frames, shards, scale_low, scale_high,
-    place, above_hbm, below_hbm, edge_hbm, inner_hbm, low_hbm, high_hbm, klow_hbm, khigh_hbm, plow_hbm, phigh_hbm,
-    wc_hbm, glow_hbm, ghigh_hbm, gklow_hbm, gkhigh_hbm, mismatch_in,
-    mismatch_hbm, keep_hbm, send_hbm,
-    packets, edge, inside, low, high, klow, khigh, plow, phigh, wc, glow, ghigh, gklow, gkhigh,
-    mismatch, keep, send,
+    frames, shards, tiles, scale_low, scale_high,
+    first, second, edge, inner, wc, glow_in, ghigh_in, gklow_in, gkhigh_in,
+    low_hbm, high_hbm, klow_hbm, khigh_hbm, plow_hbm, phigh_hbm, mismatch_in,
+    mismatch_hbm, keep, send,
+    low, high, klow, khigh, plow, phigh, glow, ghigh, gklow, gkhigh, mismatch,
     feature, gated, fine, low_pad, high_pad, low_student, high_student, low_back, high_back, shard_sums, sems,
 ):
     del mismatch_in
     _, cells, _, cols, out = edge.shape
-    rows = inner_hbm.shape[1] + 2
+    rows = inner.shape[1] + 2
     low_ch, high_ch = low.shape[-1], high.shape[-1]
-    mine = place[0]
+    mine, tile = lax.axis_index("clip"), lax.axis_index("space")
+    even = lax.rem(tile, 2) == 0
+    outside = (tile == 0, tile == tiles - 1)
     copies = Copies(sems)
     loads = [
-        copies.start(above_hbm, packets.at[0]),
-        copies.start(below_hbm, packets.at[1]),
         copies.start(high_hbm.at[:, pl.ds(0, 5)], high.at[0]),
         copies.start(high_hbm.at[:, pl.ds(2 * rows - 5, 5)], high.at[1]),
+        copies.start(khigh_hbm, khigh),
         copies.start(low_hbm.at[:, pl.ds(0, 2)], low.at[0]),
         copies.start(low_hbm.at[:, pl.ds(rows - 2, 2)], low.at[1]),
-        copies.start(khigh_hbm, khigh),
         copies.start(klow_hbm, klow),
-        copies.start(edge_hbm, edge),
-        copies.start(inner_hbm.at[:, pl.ds(0, 2)], inside.at[0]),
-        copies.start(inner_hbm.at[:, pl.ds(rows - 4, 2)], inside.at[1]),
-    ]
-    load_wc = copies.start(wc_hbm, wc)
-    late = [
         copies.start(plow_hbm, plow),
         copies.start(phigh_hbm, phigh),
-        copies.start(glow_hbm, glow),
-        copies.start(ghigh_hbm, ghigh),
-        copies.start(gklow_hbm, gklow),
-        copies.start(gkhigh_hbm, gkhigh),
     ]
-    for copy in loads:
-        copy.wait()
-
-    for side in range(2):
-        for cell in range(cells):
-            halo = packets.at[side, cell]
-            at = 0 if side == 0 else 2
-            low_pad[side, cell, at] = halo[2, :, 0:low_ch].astype(F32)
-            low_pad[side, cell, pl.ds(1 - side, 2)] = low[side, cell].astype(F32)
-            at = 0 if side == 0 else 5
-            high_pad[side, cell, at, 0:cols] = halo[3, :, 0:high_ch].astype(F32)
-            high_pad[side, cell, at, cols:] = halo[3, :, high_ch : 2 * high_ch].astype(F32)
-            high_pad[side, cell, pl.ds(1 - side, 5)] = high[side, cell].astype(F32)
-        depthwise(frames, high_pad.at[side], khigh, high_student.at[side])
-        depthwise(frames, low_pad.at[side], klow, low_student.at[side])
+    for total, part in ((glow, glow_in), (ghigh, ghigh_in), (gklow, gklow_in), (gkhigh, gkhigh_in)):
+        total[...] = part[...]
+
+    def halo(side, cell, row):
+        ours, other = first[cell, row].astype(F32), second[cell, row].astype(F32)
+        return jnp.where(even, other, ours) if side == 0 else jnp.where(even, ours, other)
 
     for side in range(2):
         for cell in range(cells):
             for k in range(2):
-                whole = (edge[side, cell, k] + packets[side, cell, k, :, 0:out].astype(F32)).astype(BF16).astype(F32)
+                whole = (edge[side, cell, k] + halo(side, cell, k)[:, 0:out]).astype(BF16).astype(F32)
                 if k == side:
-                    whole = jnp.where(jnp.full(whole.shape, place[1 + side]) == 0, whole, 0.0)
+                    whole = jnp.where(outside[side], 0.0, whole)
                 else:
                     feature[side, cell] = whole
                 for j, value in enumerate(gate_rows(whole)):
                     gated[j, side, cell, 2 * side + k] = value
-                for j, value in enumerate(gate_rows(inside[side, cell, k].astype(F32))):
+                for j, value in enumerate(gate_rows(inner[cell, side * (rows - 4) + k].astype(F32))):
                     gated[j, side, cell, 2 - 2 * side + k] = value
 
-    for copy in late:
+    second_feature(frames, gated, wc, 2, fine)
+    for copy in loads:
         copy.wait()
+
+    for side in range(2):
+        for cell in range(cells):
+            low_halo, high_halo = halo(side, cell, 2), halo(side, cell, 3)
+            at = 0 if side == 0 else 2
+            low_pad[side, cell, at] = low_halo[:, 0:low_ch]
+            low_pad[side, cell, pl.ds(1 - side, 2)] = low[side, cell].astype(F32)
+            at = 0 if side == 0 else 5
+            high_pad[side, cell, at, 0:cols] = high_halo[:, 0:high_ch]
+            high_pad[side, cell, at, cols:] = high_halo[:, high_ch : 2 * high_ch]
+            high_pad[side, cell, pl.ds(1 - side, 5)] = high[side, cell].astype(F32)
+        depthwise(frames, high_pad.at[side], khigh, high_student.at[side])
+        depthwise(frames, low_pad.at[side], klow, low_student.at[side])
+
     student = low_student[...].reshape(-1, low_ch)
     _, back = level(student, feature[...].reshape(-1, out), plow[...], scale_low, low_back, glow)
     low_back[...] = back.reshape(low_back.shape)
     for side in range(2):
         kernel_gradient(frames, low_pad.at[side], low_back.at[side], gklow, False)
 
-    load_wc.wait()
-    second_feature(frames, gated, wc, 2, fine)
     for side in range(2):
         for cell in range(cells):
             student = high_student[side, cell].reshape(-1, high_ch)
@@ -446,10 +436,13 @@
         for k in range(shards // 2):
             keep[k] = shard_sums[2 * k + bit]
             send[k] = shard_sums[2 * k + 1 - bit].astype(BF16)
-    stores.append(copies.start(send, send_hbm))
-    stores.append(copies.start(keep, keep_hbm))
     for copy in stores:
         copy.wait()
+
+
+def swaps(start, count):
+    lower = range(start, count - 1, 2)
+    return [(i, i + 1) for i in lower] + [(i + 1, i) for i in lower]
 
 
 def pairs(count, bit):
@@ -474,10 +467,29 @@
         bits = (bit, 2 * bit, 3 * bit) if 2 * bit < tiles else (bit,)
         out = total.astype(BF16)
         got = [lax.ppermute(out, "space", pairs(tiles, b)) for b in bits]
+        bit *= 2 ** (2 if len(bits) > 1 else 1)
+        if bit >= tiles:
+            return total, got
         for part in got:
             total = total + part.astype(F32)
-        bit *= 2 ** (2 if len(bits) > 1 else 1)
-    return total
+    return total, []
+
+
+def unpack_kernel(total_ref, *refs):
+    got, (glow, gklow, ghigh, gkhigh), sums = refs[:-5], refs[-5:-1], refs[-1]
+    value = total_ref[...]
+    for part in got:
+        value = value + part[...].astype(F32)
+    sums[...] = value
+    low_rows, high_rows, out = glow.shape[0], ghigh.shape[0], glow.shape[1]
+    top = low_rows + high_rows
+    glow[...] = sums[0:low_rows, 0:out]
+    ghigh[...] = sums[low_rows:top, 0:out]
+    for t in range(3):
+        for h in range(3):
+            at = top + 9 * t + 3 * h
+            gklow[t, h] = sums[at : at + 3, 0:low_rows]
+            gkhigh[t, h] = sums[at : at + 3, low_rows:top]
 
 
 def on_device(teacher_input, conv_first, conv_second, student_low, student_high, kernel_low, kernel_high, adapter_low, adapter_high):
@@ -492,11 +504,7 @@
     x = teacher_input.reshape(cells, rows, cols, depth)
     low = student_low.reshape(cells, rows, cols, low_ch)
     high = student_high.reshape(cells, 2 * rows, 2 * cols, high_ch)
-    klow, khigh = kernel_low.reshape(27, low_ch), kernel_high.reshape(27, high_ch)
     sems = pltpu.SemaphoreType.DMA
-
-    def hbm(shape, dtype):
-        return pltpu.HBM(shape, dtype)
 
     def vm(*specs):
         return [pltpu.VMEM(shape, dtype) for shape, dtype in specs]
@@ -504,49 +512,41 @@
     packet = ((cells, 4, cols, max(out, low_ch, 2 * high_ch)), BF16)
     inner_spec = ((cells, rows - 2, cols, out), BF16)
     edge_spec = ((2, cells, 2, cols, out), F32)
-    inner_feature, edge, up, down = pl.pallas_call(
+    inner_feature, edge, first, second = pl.pallas_call(
         functools.partial(first_kernel, frames),
-        out_shape=(hbm(*inner_spec), hbm(*edge_spec), hbm(*packet), hbm(*packet)),
+        out_shape=tuple(vm(inner_spec, edge_spec, packet, packet)),
         in_specs=[HBM] * 4,
-        out_specs=(HBM,) * 4,
+        out_specs=(VMEM,) * 4,
         scratch_shapes=vm(
             (x.shape, BF16),
             (conv_first.shape, BF16),
             ((3, cells, rows + 2, cols, out), F32),
-            inner_spec,
-            edge_spec,
-            packet,
-            packet,
             ((2, cells, cols, low_ch), BF16),
             ((2, cells, 2 * cols, high_ch), BF16),
         )
         + [sems((18,))],
-        compiler_params=pltpu.CompilerParams(vmem_limit_bytes=56 * MIB),
+        compiler_params=pltpu.CompilerParams(vmem_limit_bytes=20 * MIB),
         cost_estimate=pl.CostEstimate(flops=3 * 10**9, bytes_accessed=9 * 10**6, transcendentals=0),
         name="teacher_first",
-    )(x, conv_first, low, high)
-
-    forward = [(i, i + 1) for i in range(tiles - 1)]
-    above = lax.ppermute(down, "space", forward)
-    below = lax.ppermute(up, "space", [(b, a) for a, b in forward])
+    )(*in_hbm(x, conv_first, low, high))
+
+    first_got = lax.ppermute(first, "space", swaps(0, tiles))
+    second_got = lax.ppermute(second, "space", swaps(1, tiles))
 
     wc_spec = ((2, 2, 3, 2, 2, out, out), BF16)
     grads = (((low_ch, out), F32), ((high_ch, out), F32), ((32, low_ch), F32), ((32, high_ch), F32))
-    weights = (((27, low_ch), F32), ((27, high_ch), F32), (adapter_low.shape, BF16), (adapter_high.shape, BF16))
+    weights = ((kernel_low.shape, F32), (kernel_high.shape, F32), (adapter_low.shape, BF16), (adapter_high.shape, BF16))
     wc, mismatch, *sums = pl.pallas_call(
         functools.partial(second_kernel, frames, *scales),
-        out_shape=(hbm(*wc_spec), hbm((cells, 2 * rows, 2 * cols, out), BF16)) + tuple(hbm(*g) for g in grads),
-        in_specs=[HBM] * 8,
-        out_specs=(HBM,) * 6,
+        out_shape=(*vm(wc_spec), pltpu.HBM((cells, 2 * rows, 2 * cols, out), BF16), *vm(*grads)),
+        in_specs=[VMEM] + [HBM] * 7,
+        out_specs=(VMEM, HBM) + (VMEM,) * 4,
         scratch_shapes=vm(
-            inner_spec,
             (conv_second.shape, BF16),
             (low.shape, BF16),
             ((cells, 2 * inner + 2, 2 * cols, high_ch), BF16),
             *weights,
-            wc_spec,
             ((cells, 2 * inner, 2 * cols, out), BF16),
-            *grads,
             ((3, 1, cells, rows - 2, cols, out), BF16),
             ((1, cells, inner, 2, out // 128, 2 * cols, 128), F32),
             ((cells, rows, cols, low_ch), F32),
@@ -557,34 +557,26 @@
             ((cells, 2 * inner, 2 * cols, high_ch), F32),
         )
         + [sems((14,))],
-        compiler_params=pltpu.CompilerParams(vmem_limit_bytes=56 * MIB),
+        compiler_params=pltpu.CompilerParams(vmem_limit_bytes=20 * MIB),
         cost_estimate=pl.CostEstimate(flops=5 * 10**9, bytes_accessed=20 * 10**6, transcendentals=0),
         name="inner_rows",
-    )(inner_feature, conv_second, low, high, klow, khigh, adapter_low, adapter_high)
-
-    clip, tile = lax.axis_index("clip"), lax.axis_index("space")
-    place = jnp.stack([clip, (tile == 0).astype(jnp.int32), (tile == tiles - 1).astype(jnp.int32)])
+    )(inner_feature, *in_hbm(conv_second, low, high, kernel_low, kernel_high, adapter_low, adapter_high))
+
     shard_rows = low_ch // clips + high_ch // clips + 32
     shard_rows += -shard_rows % 16
     shard = (max(clips // 2, 1), shard_rows, out)
     mismatch, keep, send = pl.pallas_call(
-        functools.partial(third_kernel, frames, clips, *scales),
-        out_shape=(hbm(mismatch.shape, BF16), hbm(shard, F32), hbm(shard, BF16)),
-        in_specs=[pl.BlockSpec(memory_space=pltpu.SMEM)] + [HBM] * 16,
-        out_specs=(HBM,) * 3,
-        input_output_aliases={16: 0},
+        functools.partial(third_kernel, frames, clips, tiles, *scales),
+        out_shape=(pltpu.HBM(mismatch.shape, BF16), *vm((shard, F32), (shard, BF16))),
+        in_specs=[VMEM] * 9 + [HBM] * 7,
+        out_specs=(HBM, VMEM, VMEM),
+        input_output_aliases={15: 0},
         scratch_shapes=vm(
-            ((2,) + packet[0], BF16),
-            edge_spec,
-            ((2, cells, 2, cols, out), BF16),
             ((2, cells, 2, cols, low_ch), BF16),
             ((2, cells, 5, 2 * cols, high_ch), BF16),
             *weights,
-            wc_spec,
             *grads,
             ((2, cells, 4, 2 * cols, out), BF16),
-            (shard, F32),
-            (shard, BF16),
             ((2, cells, cols, out), F32),
             ((3, 2, cells, 4, cols, out), BF16),
             ((2, cells, 2, 2, out // 128, 2 * cols, 128), F32),
@@ -597,21 +589,28 @@
             ((clips, shard_rows, out), F32),
         )
         + [sems((22,))],
-        compiler_params=pltpu.CompilerParams(vmem_limit_bytes=56 * MIB),
+        compiler_params=pltpu.CompilerParams(vmem_limit_bytes=20 * MIB),
         cost_estimate=pl.CostEstimate(flops=3 * 10**9, bytes_accessed=20 * 10**6, transcendentals=0),
         name="border_rows",
-    )(place, above, below, edge, inner_feature, low, high, klow, khigh, adapter_low, adapter_high, wc, *sums, mismatch)
-
-    total = sum_over_devices(keep, send, clips, tiles)
+    )(first_got, second_got, edge, inner_feature, wc, *sums, *in_hbm(low, high, kernel_low, kernel_high, adapter_low, adapter_high, mismatch))
+
+    total, got = sum_over_devices(keep, send, clips, tiles)
     low_rows, high_rows = low_ch // clips, high_ch // clips
-    top = low_rows + high_rows
-    return (
-        total[:low_rows],
-        total[top : top + 27, :low_rows].reshape(3, 3, 3, low_rows),
-        total[low_rows:top],
-        total[top : top + 27, low_rows : low_rows + high_rows].reshape(3, 3, 3, high_rows),
-        mismatch.reshape(held, frames, 2 * rows, 2 * cols, out),
-    )
+    glow, gklow, ghigh, gkhigh = pl.pallas_call(
+        unpack_kernel,
+        out_shape=(
+            jax.ShapeDtypeStruct((low_rows, out), F32),
+            jax.ShapeDtypeStruct((3, 3, 3, low_rows), F32),
+            jax.ShapeDtypeStruct((high_rows, out), F32),
+            jax.ShapeDtypeStruct((3, 3, 3, high_rows), F32),
+        ),
+        in_specs=[VMEM] * (1 + len(got)),
+        out_specs=(VMEM,) * 4,
+        scratch_shapes=[pltpu.VMEM(shard[1:], F32)],
+        compiler_params=pltpu.CompilerParams(vmem_limit_bytes=4 * MIB),
+        name="unpack",
+    )(total, *got)
+    return glow, gklow, ghigh, gkhigh, mismatch.reshape(held, frames, 2 * rows, 2 * cols, out)
 
 
 def solution(mesh):

time: 59.7 us -> 48.3 us (0.81)
  local copies, waits for them, and re-layouts: 4.54 us -> 0.02 us
  Pallas kernels: 24.9 us -> 21 us
  starting transfers between devices: 16 us -> 12.3 us
  waiting for transfers between devices: 11.5 us -> 14 us
  other arithmetic: 1.71 us -> 0.08 us
    pallas_call x2 -> x3, Pallas kernels: 15.7 us -> 12.9 us  [the longest x1 6.26 us: on_device(): pl.pallas_call(functools.partial(first_kernel, frames), out_shape=tuple(v...]
    ppermute x4, waiting for transfers between devices: 7.24 us -> 9.9 us  [sum_over_devices(): got = [lax.ppermute(out, 'space', pairs(tiles, b)) for b in bits]]
    ppermute x2, starting transfers between devices: 6.14 us -> 3.66 us  [the longest x1 3 us: on_device(): first_got = lax.ppermute(first, 'space', swaps(0, tiles))]
    reshape x4 -> x0, local copies, waits for them, and re-layouts: 2.48 us -> none  [the longest x1 0.63 us: on_device(): kernel_low.reshape(27, low_ch)]
    slice x4 -> x0, local copies, waits for them, and re-layouts: 1.33 us -> none  [the longest x1 0.63 us: on_device(): total[:low_rows]]
    ppermute x4, starting transfers between devices: 8.22 us -> 7 us  [sum_over_devices(): got = [lax.ppermute(out, 'space', pairs(tiles, b)) for b in bits]]
    pallas_call x1, Pallas kernels: 9.22 us -> 8.13 us  [on_device(): pl.pallas_call(functools.partial(second_kernel, frames, *scales), out_sha...]
    add x1, other arithmetic: 0.97 us -> 0.02 us  [sum_over_devices(): keep = keep + lax.ppermute(send, 'clip', pairs(clips, 1)).astype(F32)]
  transfers between devices with their start and end apart: 8 -> 8, of which waited for: 5 -> 6; matrix products, arithmetic and copies ran while one was open for 3% -> 0% of each run, Pallas kernels for 15% -> 17%
where the time goes in v2:
time: 48.3 us; the launch traced here: 48.1 us
  Pallas kernels  21 us (43%)
  waiting for transfers between devices  14 us (29%)
  starting transfers between devices  12.3 us (25%)
  between operations  0.72 us (1%)
    ppermute x4, waiting for transfers between devices, sum_over_devices(): got = [lax.ppermute(out, 'space', pairs(tiles, b)) for b in bits]  9.9 us
    pallas_call x1, Pallas kernels, on_device(): pl.pallas_call(functools.partial(second_kernel, frames, *scales), out_sha...  8.13 us
    ppermute x4, starting transfers between devices, sum_over_devices(): got = [lax.ppermute(out, 'space', pairs(tiles, b)) for b in bits]  7 us
    pallas_call x1, Pallas kernels, on_device(): pl.pallas_call(functools.partial(first_kernel, frames), out_shape=tuple(v...  6.26 us
    pallas_call x1, Pallas kernels, on_device(): pl.pallas_call(functools.partial(third_kernel, frames, clips, tiles, *sca...  5.91 us
    ppermute x1, starting transfers between devices, on_device(): first_got = lax.ppermute(first, 'space', swaps(0, tiles))  3 us
    ppermute x1, waiting for transfers between devices, sum_over_devices(): keep = keep + lax.ppermute(send, 'clip', pairs(clips, bit)).astype(F32)  2.75 us
    ppermute x1, starting transfers between devices, sum_over_devices(): keep = keep + lax.ppermute(send, 'clip', pairs(clips, bit)).astype(F32)  1.58 us
  transfers between devices with their start and end apart: 8, of which 6 were waited for; matrix products, arithmetic and copies ran while one was open for 0% of the time, Pallas kernels for 17%

profile of v2, /device:TPU:0, one launch (start us, length us, event | category | flops | bytes accessed | tf_op | source)
XLA Modules:
  0.0 48.1 jit_solution(12294857940514275785)
XLA Ops:
  0.6 6.3 %teacher_first.1 = (bf16[2,6,32,256]{3,2,1,0:T(8,128)(2,1)S(1)}, f32[2,2,2,32,256]{4,3,2,1,0:T(8,128)S(1)}, bf16[2,4,32,256]{3,2,1,0:T(8,128)(2,1)S(1)}, bf16[2,4,32,256]{3,2,1,0:T(8,128)(2,1)S(1)}) custom-call(bf16[2,8,32,512]{3,2,1,0:T(8,128)(2,1)} %bitcast.12, bf16[3,3,3,512,256]{4,3,2,1,0:T(8,128)(2,1)} %w_hbm.2, bf16[2,8,32,256]{3,2,1,0:T(8,128)(2,1)} %bitcast.16, ...), custom_call_target="tpu_custom_call" | custom-call | flops 3000000000 | bytes 9000000 | tf_op jit(solution)/shard_map/teacher_first/pallas_call | solution.py:515
  6.9 3.0 %collective-permute-start = (bf16[2,4,32,256]{3,2,1,0:T(8,128)(2,1)S(1)}, bf16[2,4,32,256]{3,2,1,0:T(8,128)(2,1)S(1)}, u32[]{:S(2)}, u32[]{:S(2)}) collective-permute-start(bf16[2,4,32,256]{3,2,1,0:T(8,128)(2,1)S(1)} %get-tuple-element.22), channel_id=1, source_target_pairs={{0,1},{2,3},{4,5},{6,7},{1,0},{3,2},{5,4},{7,6},{8,9},{10,11},{12,... | collective-permute-start | bytes 393224 | tf_op jit(solution)/shard_map/ppermute | solution.py:533
  9.9 0.7 %collective-permute-start.1 = (bf16[2,4,32,256]{3,2,1,0:T(8,128)(2,1)S(1)}, bf16[2,4,32,256]{3,2,1,0:T(8,128)(2,1)S(1)}, u32[]{:S(2)}, u32[]{:S(2)}) collective-permute-start(bf16[2,4,32,256]{3,2,1,0:T(8,128)(2,1)S(1)} %get-tuple-element.23), channel_id=1, source_target_pairs={{1,2},{3,4},{5,6},{2,1},{4,3},{6,5},{9,10},{11,12},{13,14},{10,9},... | collective-permute-start | bytes 393224 | tf_op jit(solution)/shard_map/ppermute | solution.py:534
  10.6 8.1 %inner_rows.1 = (bf16[2,2,3,2,2,256,256]{6,5,4,3,2,1,0:T(8,128)(2,1)S(1)}, bf16[2,16,64,256]{3,2,1,0:T(8,128)(2,1)}, f32[256,256]{1,0:T(8,128)S(1)}, f32[128,256...) custom-call(bf16[2,6,32,256]{3,2,1,0:T(8,128)(2,1)S(1)} %get-tuple-element.25.feature.inner, ...), custom_call_target="tpu_custom_call" | custom-call | flops 5000000000 | bytes 20000000 | tf_op jit(solution)/shard_map/inner_rows/pallas_call | solution.py:539
  18.7 0.0 collective-permute-done.first
  18.7 0.0 collective-permute-done.1.second
  18.7 5.9 %border_rows.1 = (bf16[2,16,64,256]{3,2,1,0:T(8,128)(2,1)}, f32[2,128,256]{2,1,0:T(8,128)S(1)}, bf16[2,128,256]{2,1,0:T(8,128)(2,1)S(1)}) custom-call(bf16[2,4,32,256]{3,2,1,0:T(8,128)(2,1)S(1)} %collective-permute-done.first, bf16[2,4,32,256]{3,2,1,0:T(8,128)(2,1)S(1)} %collective-permute-done.1.second, ...), custom_call_target="tpu_custom_call", output_to_operand_aliasing={{0}: (15, {})} | custom-call | flops 3000000000 | bytes 20000000 | tf_op jit(solution)/shard_map/border_rows/pallas_call | solution.py:568
  24.6 0.1 collective-permute-start.2
  24.7 1.3 %collective-permute-done.2 = bf16[2,128,256]{2,1,0:T(8,128)(2,1)S(1)} collective-permute-done((bf16[2,128,256]{2,1,0:T(8,128)(2,1)S(1)}, bf16[2,128,256]{2,1,0:T(8,128)(2,1)S(1)}, u32[]{:S(2)}, u32[]{:S(2)}) %collective-permute-start.2) | collective-permute-done | bytes 131104 | tf_op jit(solution)/shard_map/ppermute | solution.py:455
  26.1 1.6 %collective-permute-start.3 = (bf16[1,128,256]{2,1,0:T(8,128)(2,1)S(1)}, bf16[1,128,256]{2,1,0:T(8,128)(2,1)S(1)}, u32[]{:S(2)}, u32[]{:S(2)}) collective-permute-start(bf16[1,128,256]{2,1,0:T(8,128)(2,1)S(1)} %dynamic-slice_convert_fusion), channel_id=1, source_target_pairs={{0,16},{8,24},{16,0},{24,8},{1,17},{9,25},{17,1},{25,9},{2,18},{10... | collective-permute-start | bytes 196616 | tf_op jit(solution)/shard_map/ppermute | solution.py:462
  27.7 2.7 %collective-permute-done.3 = bf16[1,128,256]{2,1,0:T(8,128)(2,1)S(1)} collective-permute-done((bf16[1,128,256]{2,1,0:T(8,128)(2,1)S(1)}, bf16[1,128,256]{2,1,0:T(8,128)(2,1)S(1)}, u32[]{:S(2)}, u32[]{:S(2)}) %collective-permute-start.3) | collective-permute-done | bytes 65568 | tf_op jit(solution)/shard_map/ppermute | solution.py:462
  30.5 4.3 %collective-permute-start.4 = (bf16[128,256]{1,0:T(8,128)(2,1)S(1)}, bf16[128,256]{1,0:T(8,128)(2,1)S(1)}, u32[]{:S(2)}, u32[]{:S(2)}) collective-permute-start(bf16[128,256]{1,0:T(8,128)(2,1)S(1)} %bitcast_convert_fusion), channel_id=1, source_target_pairs={{0,1},{1,0},{2,3},{3,2},{4,5},{5,4},{6,7},{7,6},{8,9},{9,8},{10,11... | collective-permute-start | bytes 196616 | tf_op jit(solution)/shard_map/ppermute | solution.py:469
  34.8 1.6 %collective-permute-start.5 = (bf16[128,256]{1,0:T(8,128)(2,1)S(1)}, bf16[128,256]{1,0:T(8,128)(2,1)S(1)}, u32[]{:S(2)}, u32[]{:S(2)}) collective-permute-start(bf16[128,256]{1,0:T(8,128)(2,1)S(1)} %bitcast_convert_fusion), channel_id=1, source_target_pairs={{0,2},{1,3},{2,0},{3,1},{4,6},{5,7},{6,4},{7,5},{8,10},{9,11},{10,... | collective-permute-start | bytes 196616 | tf_op jit(solution)/shard_map/ppermute | solution.py:469
  36.4 0.0 collective-permute-start.6
  36.4 0.9 %collective-permute-done.4 = bf16[128,256]{1,0:T(8,128)(2,1)S(1)} collective-permute-done((bf16[128,256]{1,0:T(8,128)(2,1)S(1)}, bf16[128,256]{1,0:T(8,128)(2,1)S(1)}, u32[]{:S(2)}, u32[]{:S(2)}) %collective-permute-start.4) | collective-permute-done | bytes 65568 | tf_op jit(solution)/shard_map/ppermute | solution.py:469
  37.3 1.7 %collective-permute-done.5 = bf16[128,256]{1,0:T(8,128)(2,1)S(1)} collective-permute-done((bf16[128,256]{1,0:T(8,128)(2,1)S(1)}, bf16[128,256]{1,0:T(8,128)(2,1)S(1)}, u32[]{:S(2)}, u32[]{:S(2)}) %collective-permute-start.5) | collective-permute-done | bytes 65568 | tf_op jit(solution)/shard_map/ppermute | solution.py:469
  39.1 2.5 %collective-permute-done.6 = bf16[128,256]{1,0:T(8,128)(2,1)S(1)} collective-permute-done((bf16[128,256]{1,0:T(8,128)(2,1)S(1)}, bf16[128,256]{1,0:T(8,128)(2,1)S(1)}, u32[]{:S(2)}, u32[]{:S(2)}) %collective-permute-start.6) | collective-permute-done | bytes 65568 | tf_op jit(solution)/shard_map/ppermute | solution.py:469
  41.6 1.1 %collective-permute-start.7 = (bf16[128,256]{1,0:T(8,128)(2,1)S(1)}, bf16[128,256]{1,0:T(8,128)(2,1)S(1)}, u32[]{:S(2)}, u32[]{:S(2)}) collective-permute-start(bf16[128,256]{1,0:T(8,128)(2,1)S(1)} %get-tuple-element.39), channel_id=1, source_target_pairs={{0,4},{1,5},{2,6},{3,7},{4,0},{5,1},{6,2},{7,3},{8,12},{9,13},{10,... | collective-permute-start | bytes 196616 | tf_op jit(solution)/shard_map/ppermute | solution.py:469
  42.7 4.7 %collective-permute-done.7.refs_0_ = bf16[128,256]{1,0:T(8,128)(2,1)S(1)} collective-permute-done((bf16[128,256]{1,0:T(8,128)(2,1)S(1)}, bf16[128,256]{1,0:T(8,128)(2,1)S(1)}, u32[]{:S(2)}, u32[]{:S(2)}) %collective-permute-start.7) | collective-permute-done | bytes 65568 | tf_op jit(solution)/shard_map/ppermute | solution.py:469
  47.4 0.7 %unpack.1 = (f32[64,256]{1,0:T(8,128)}, f32[3,3,3,64]{3,2,1,0:T(4,128)}, f32[32,256]{1,0:T(8,128)}, f32[3,3,3,32]{3,2,1,0:T(4,128)}) custom-call(f32[128,256]{1,0:T(8,128)S(1)} %get-tuple-element.40.total_ref, bf16[128,256]{1,0:T(8,128)(2,1)S(1)} %collective-permute-done.7.refs_0_), custom_call_target="tpu_custom_call" | custom-call | tf_op jit(solution)/shard_map/unpack/pallas_call | solution.py:599
  (4 shorter events, 0.1 us)
Async XLA Ops:
  6.9 11.8 %collective-permute-start = (bf16[2,4,32,256]{3,2,1,0:T(8,128)(2,1)S(1)}, bf16[2,4,32,256]{3,2,1,0:T(8,128)(2,1)S(1)}, u32[]{:S(2)}, u32[]{:S(2)}) collective-permute-start(bf16[2,4,32,256]{3,2,1,0:T(8,128)(2,1)S(1)} %get-tuple-element.22), channel_id=1, source_target_pairs={{0,1},{2,3},{4,5},{6,7},{1,0},{3,2},{5,4},{7,6},{8,9},{10,11},{12,... | collective-permute-start | bytes 393224 | tf_op jit(solution)/shard_map/ppermute | solution.py:533
  9.9 8.8 %collective-permute-start.1 = (bf16[2,4,32,256]{3,2,1,0:T(8,128)(2,1)S(1)}, bf16[2,4,32,256]{3,2,1,0:T(8,128)(2,1)S(1)}, u32[]{:S(2)}, u32[]{:S(2)}) collective-permute-start(bf16[2,4,32,256]{3,2,1,0:T(8,128)(2,1)S(1)} %get-tuple-element.23), channel_id=1, source_target_pairs={{1,2},{3,4},{5,6},{2,1},{4,3},{6,5},{9,10},{11,12},{13,14},{10,9},... | collective-permute-start | bytes 393224 | tf_op jit(solution)/shard_map/ppermute | solution.py:534
  24.6 1.4 %collective-permute-start.2 = (bf16[2,128,256]{2,1,0:T(8,128)(2,1)S(1)}, bf16[2,128,256]{2,1,0:T(8,128)(2,1)S(1)}, u32[]{:S(2)}, u32[]{:S(2)}) collective-permute-start(bf16[2,128,256]{2,1,0:T(8,128)(2,1)S(1)} %get-tuple-element.33), channel_id=1, source_target_pairs={{0,8},{8,0},{16,24},{24,16},{1,9},{9,1},{17,25},{25,17},{2,10},{10... | collective-permute-start | bytes 393224 | tf_op jit(solution)/shard_map/ppermute | solution.py:455
  26.1 4.3 %collective-permute-start.3 = (bf16[1,128,256]{2,1,0:T(8,128)(2,1)S(1)}, bf16[1,128,256]{2,1,0:T(8,128)(2,1)S(1)}, u32[]{:S(2)}, u32[]{:S(2)}) collective-permute-start(bf16[1,128,256]{2,1,0:T(8,128)(2,1)S(1)} %dynamic-slice_convert_fusion), channel_id=1, source_target_pairs={{0,16},{8,24},{16,0},{24,8},{1,17},{9,25},{17,1},{25,9},{2,18},{10... | collective-permute-start | bytes 196616 | tf_op jit(solution)/shard_map/ppermute | solution.py:462
  30.5 6.9 %collective-permute-start.4 = (bf16[128,256]{1,0:T(8,128)(2,1)S(1)}, bf16[128,256]{1,0:T(8,128)(2,1)S(1)}, u32[]{:S(2)}, u32[]{:S(2)}) collective-permute-start(bf16[128,256]{1,0:T(8,128)(2,1)S(1)} %bitcast_convert_fusion), channel_id=1, source_target_pairs={{0,1},{1,0},{2,3},{3,2},{4,5},{5,4},{6,7},{7,6},{8,9},{9,8},{10,11... | collective-permute-start | bytes 196616 | tf_op jit(solution)/shard_map/ppermute | solution.py:469
  34.8 4.3 %collective-permute-start.5 = (bf16[128,256]{1,0:T(8,128)(2,1)S(1)}, bf16[128,256]{1,0:T(8,128)(2,1)S(1)}, u32[]{:S(2)}, u32[]{:S(2)}) collective-permute-start(bf16[128,256]{1,0:T(8,128)(2,1)S(1)} %bitcast_convert_fusion), channel_id=1, source_target_pairs={{0,2},{1,3},{2,0},{3,1},{4,6},{5,7},{6,4},{7,5},{8,10},{9,11},{10,... | collective-permute-start | bytes 196616 | tf_op jit(solution)/shard_map/ppermute | solution.py:469
  36.4 5.2 %collective-permute-start.6 = (bf16[128,256]{1,0:T(8,128)(2,1)S(1)}, bf16[128,256]{1,0:T(8,128)(2,1)S(1)}, u32[]{:S(2)}, u32[]{:S(2)}) collective-permute-start(bf16[128,256]{1,0:T(8,128)(2,1)S(1)} %bitcast_convert_fusion), channel_id=1, source_target_pairs={{0,3},{1,2},{2,1},{3,0},{4,7},{5,6},{6,5},{7,4},{8,11},{9,10},{10,... | collective-permute-start | bytes 196616 | tf_op jit(solution)/shard_map/ppermute | solution.py:469
  41.6 5.8 %collective-permute-start.7 = (bf16[128,256]{1,0:T(8,128)(2,1)S(1)}, bf16[128,256]{1,0:T(8,128)(2,1)S(1)}, u32[]{:S(2)}, u32[]{:S(2)}) collective-permute-start(bf16[128,256]{1,0:T(8,128)(2,1)S(1)} %get-tuple-element.39), channel_id=1, source_target_pairs={{0,4},{1,5},{2,6},{3,7},{4,0},{5,1},{6,2},{7,3},{8,12},{9,13},{10,... | collective-permute-start | bytes 196616 | tf_op jit(solution)/shard_map/ppermute | solution.py:469

commit v3 on v2

v3 whole, which is shorter than its diff:
```python
import functools

import jax
import jax.numpy as jnp
from jax import lax
from jax.experimental import pallas as pl
from jax.experimental.pallas import tpu as pltpu
from jax.sharding import PartitionSpec as P

F32, BF16 = jnp.float32, jnp.bfloat16
HBM = pl.BlockSpec(memory_space=pltpu.HBM)
VMEM = pl.BlockSpec(memory_space=pltpu.VMEM)
MIB = 1 << 20


def in_hbm(*arrays):
    return [pltpu.with_memory_space_constraint(array, pltpu.HBM) for array in arrays]


def shift_cols(value, by):
    axis = value.ndim - 2
    count = value.shape[axis]
    column = lax.broadcasted_iota(jnp.int32, value.shape, axis)
    edge = 0 if by > 0 else count - 1
    return jnp.where(column == edge, 0.0, pltpu.roll(value, by % count, axis))


def silu(value):
    return value / (1.0 + jnp.exp(-value))


def dot(a, b):
    return jnp.dot(a, b, preferred_element_type=F32)


def dot_nt(a, b):
    return lax.dot_general(a, b, (((1,), (1,)), ((), ())), preferred_element_type=F32)


def dot_tn(a, b):
    return lax.dot_general(a, b, (((0,), (0,)), ((), ())), preferred_element_type=F32)


def frame_spans(frames):
    spans = []
    for tap in (1, 0, 2):
        off = tap - 1
        count = frames - abs(off)
        if count > 0:
            spans.append((tap, max(0, -off), max(0, off), count))
    return spans


def near_frames(cell, frames):
    frame = cell % frames
    near = [cell + t for t in (-1, 0, 1) if 0 <= frame + t < frames]
    return near, near[0] - cell + 1


class Copies:
    def __init__(self, sems):
        self.sems, self.count = sems, 0

    def start(self, src, dst):
        copy = pltpu.make_async_copy(src, dst, self.sems.at[self.count])
        self.count += 1
        copy.start()
        return copy


def phase_weights(w_ref, wc_ref):
    depth = w_ref.shape[-2]
    chunk = 16

    def step(tap, at):
        rows = slice(at, at + chunk)
        taps = [[w_ref[tap, h, w, rows].astype(F32) for w in range(3)] for h in range(3)]
        for p in range(2):
            if p == 0:
                merged = (taps[0], [taps[1][w] + taps[2][w] for w in range(3)])
            else:
                merged = ([taps[0][w] + taps[1][w] for w in range(3)], taps[2])
            for a in range(2):
                m = merged[a]
                wc_ref[p, 0, tap, a, 0, rows] = m[0].astype(BF16)
                wc_ref[p, 0, tap, a, 1, rows] = (m[1] + m[2]).astype(BF16)
                wc_ref[p, 1, tap, a, 0, rows] = (m[0] + m[1]).astype(BF16)
                wc_ref[p, 1, tap, a, 1, rows] = m[2].astype(BF16)

    return [functools.partial(step, tap, at) for tap in range(3) for at in range(0, depth, chunk)]


def widen(field, wide):
    def step(cell, row):
        wide[cell, row] = field[cell, row].astype(F32)

    return [functools.partial(step, cell, row) for cell in range(field.shape[0]) for row in range(field.shape[1])]


def gate_rows(feature):
    gated = silu(feature)
    return shift_cols(gated, 1).astype(BF16), gated.astype(BF16), shift_cols(gated, -1).astype(BF16)


def second_feature(frames, gated, wc_ref, count, fine):
    _, groups, cells, _, cols, out = gated.shape
    for cell in range(cells):
        near, first_tap = near_frames(cell, frames)
        for p in range(2):
            for q in range(2):
                field = jnp.concatenate(
                    [
                        gated[q + b, :, other, p + a : p + a + count].reshape(groups * count * cols, out)
                        for other in near
                        for a in range(2)
                        for b in range(2)
                    ],
                    axis=1,
                )
                weight = wc_ref[p, q, first_tap : first_tap + len(near)].reshape(-1, out)
                product = dot(field, weight).reshape(groups, count, cols, out)
                for group in range(groups):
                    for row in range(count):
                        for block in range(out // 128):
                            fine[group, cell, row, p, block, pl.ds(q, cols, stride=2), :] = product[
                                group, row, :, 128 * block : 128 * block + 128
                            ]


def depthwise(frames, padded, kernel_ref, student):
    cells, rows, _, channels = student.shape

    def step(cell, row, lane):
        near, first_tap = near_frames(cell, frames)
        lanes = pl.ds(lane, 128)
        sums = [None, None, None]
        for t, other in enumerate(near):
            for h in range(3):
                field = padded[other, row + h, :, lanes]
                for w in range(3):
                    term = field * kernel_ref[t + first_tap, h, w : w + 1, lanes]
                    sums[w] = term if sums[w] is None else sums[w] + term
        total = padded[cell, row + 1, :, lanes] + sums[1] + shift_cols(sums[0], 1) + shift_cols(sums[2], -1)
        student[cell, row, :, lanes] = total.astype(BF16)

    return [
        functools.partial(step, cell, row, lane)
        for cell in range(cells)
        for lane in range(0, channels, 128)
        for row in range(rows)
    ]


def kernel_gradient(frames, padded, back, total, first):
    cells, rows, _, channels = back.shape
    for lane in range(0, channels, 128):
        lanes = pl.ds(lane, 128)
        sums = tuple(jnp.zeros((8, 128), F32) for _ in range(27))
        for cell in range(cells):
            near, first_tap = near_frames(cell, frames)

            def body(row, sums, cell=cell, near=near, first_tap=first_tap, lanes=lanes):
                sums = list(sums)
                center = back[cell, row, :, lanes]
                moved = (shift_cols(center, -1), center, shift_cols(center, 1))
                for t, other in enumerate(near):
                    for h in range(3):
                        field = padded[other, row + h, :, lanes]
                        for w in range(3):
                            k = 9 * (t + first_tap) + 3 * h + w
                            term = (moved[w] * field).reshape(-1, 8, 128)
                            sums[k] = sums[k] + jnp.sum(term, axis=0)
                return tuple(sums)

            sums = lax.fori_loop(0, rows, body, sums)
        for k in range(27):
            value = jnp.sum(sums[k], axis=0, keepdims=True)
            total[k : k + 1, lanes] = value if first else total[k : k + 1, lanes] + value


def level(student, target, adapter, scale, grad):
    mismatch = dot(student, adapter) - target
    residual = (mismatch * scale).astype(BF16)
    grad[...] += dot_tn(student, residual)
    return mismatch, dot_nt(residual, adapter)


def fine_target(fine, rows):
    blocks = fine.shape[2]
    value = jnp.concatenate([fine[rows, :, block].reshape(-1, 128) for block in range(blocks)], axis=1)
    return value.astype(BF16).astype(F32)


def first_kernel(
    frames, x_hbm, w_hbm, w2_hbm, low_hbm, high_hbm, klow_hbm, khigh_hbm, plow_hbm, phigh_hbm,
    inner, edge, first, second, wc, low_wide, high_wide, low_student, high_student, klow, khigh, plow, phigh,
    x_ref, w_buf, w2, acc, low, high, sems,
):
    cells, rows, cols, depth = x_ref.shape
    out = w_buf.shape[-1]
    clips = cells // frames
    spans = frame_spans(frames)
    copies = Copies(sems)
    load_x = copies.start(x_hbm, x_ref)
    loads = {}
    for tap_h in (1, 0, 2):
        loads[1, tap_h] = copies.start(w_hbm.at[1, tap_h], w_buf.at[1, tap_h])
    fields = [
        copies.start(high_hbm, high),
        copies.start(khigh_hbm, khigh),
        copies.start(low_hbm, low),
        copies.start(klow_hbm, klow),
    ]
    load_w2 = copies.start(w2_hbm, w2)
    for tap, _, _, _ in spans[1:]:
        for tap_h in (1, 0, 2):
            loads[tap, tap_h] = copies.start(w_hbm.at[tap, tap_h], w_buf.at[tap, tap_h])
    late = [copies.start(plow_hbm, plow), copies.start(phigh_hbm, phigh)]
    for tap_w in range(3):
        acc[tap_w, :, 0:1] = jnp.zeros((cells, 1, cols, out), F32)
        acc[tap_w, :, rows + 1 : rows + 2] = jnp.zeros((cells, 1, cols, out), F32)

    students = (
        widen(high, high_wide)
        + widen(low, low_wide)
        + depthwise(frames, high_wide.at[:, 3 : 2 * rows - 3], khigh, high_student)
        + depthwise(frames, low_wide, klow, low_student)
    )
    load_x.wait()
    pending, share = [], 0
    for number, (tap, to, src, count) in enumerate(spans):
        for tap_h in (1, 0, 2):
            loads[tap, tap_h].wait()
            if number == 0 and tap_h == 0:
                for copy in fields:
                    copy.wait()
                pending = list(students)
                share = -(-len(pending) // 6)
            if number == min(1, len(spans) - 1) and tap_h == (1 if number else 2):
                for step in pending:
                    step()
                load_w2.wait()
                pending = phase_weights(w2, wc)
                share = -(-len(pending) // (9 * max(1, len(spans) - 1)))
            at = 2 - tap_h
            for tap_w in range(3):
                weight = w_buf[tap, tap_h, tap_w]
                for clip in range(clips):
                    base = clip * frames
                    rowset = x_ref[base + src : base + src + count].reshape(-1, depth)
                    product = dot(rowset, weight).reshape(count, rows, cols, out)
                    spot = (tap_w, pl.ds(base + to, count), pl.ds(at, rows))
                    if tap == 1 and tap_h == 1:
                        acc[spot] = product
                    else:
                        acc[spot] = acc[spot] + product
                for step in pending[:share]:
                    step()
                pending = pending[share:]
    for step in pending:
        step()

    def gathered(cell, row):
        return acc[1, cell, row] + shift_cols(acc[0, cell, row], 1) + shift_cols(acc[2, cell, row], -1)

    for copy in late:
        copy.wait()
    low_ch, high_ch = low.shape[-1], high.shape[-1]
    even = lax.rem(lax.axis_index("space"), 2) == 0
    for cell in range(cells):
        for j in range(2):
            up, down = gathered(cell, j), gathered(cell, rows + j)
            edge[0, cell, j], edge[1, cell, j] = up, down
            first[cell, j, :, 0:out] = jnp.where(even, down, up).astype(BF16)
            second[cell, j, :, 0:out] = jnp.where(even, up, down).astype(BF16)
        up, down = low_wide[cell, 0], low_wide[cell, rows - 1]
        first[cell, 2, :, 0:low_ch] = jnp.where(even, down, up).astype(BF16)
        second[cell, 2, :, 0:low_ch] = jnp.where(even, up, down).astype(BF16)
        for half in range(2):
            here, lanes = slice(half * cols, (half + 1) * cols), slice(half * high_ch, (half + 1) * high_ch)
            up, down = high_wide[cell, 0, here], high_wide[cell, 2 * rows - 1, here]
            first[cell, 3, :, lanes] = jnp.where(even, down, up).astype(BF16)
            second[cell, 3, :, lanes] = jnp.where(even, up, down).astype(BF16)
    for cell in range(cells):

        def gather(row, _, cell=cell):
            inner[cell, row] = gathered(cell, row + 2).astype(BF16)
            return 0

        lax.fori_loop(0, rows - 2, gather, 0)


def second_kernel(
    frames, scale_low, scale_high,
    feature, wc, low_wide, high_wide, low_student, high_student, plow, phigh,
    mismatch_hbm, glow, ghigh, gklow, gkhigh,
    mismatch, gated, fine, low_back, high_back, sems,
):
    cells, count, cols, out = feature.shape
    rows = count + 2
    inner = rows - 4
    copies = Copies(sems)
    for cell in range(cells):

        def gate(row, _, cell=cell):
            for k, value in enumerate(gate_rows(feature[cell, row].astype(F32))):
                gated[k, 0, cell, row] = value
            return 0

        lax.fori_loop(0, count, gate, 0)
    second_feature(frames, gated, wc, inner, fine)

    glow[...] = jnp.zeros_like(glow)
    ghigh[...] = jnp.zeros_like(ghigh)
    gklow[...] = jnp.zeros_like(gklow)
    gkhigh[...] = jnp.zeros_like(gkhigh)
    for cell in range(cells):
        student = high_student[cell].reshape(-1, high_student.shape[-1])
        target = fine_target(fine.at[0, cell], slice(0, inner))
        value, back = level(student, target, phigh[...], scale_high, ghigh)
        mismatch[cell] = value.astype(BF16).reshape(2 * inner, 2 * cols, out)
        high_back[cell] = back.reshape(2 * inner, 2 * cols, -1)
    store = copies.start(mismatch, mismatch_hbm.at[:, pl.ds(4, 2 * inner)])
    student = low_student[...].reshape(-1, low_student.shape[-1])
    target = feature[...].reshape(-1, out).astype(F32)
    _, back = level(student, target, plow[...], scale_low, glow)
    low_back[...] = back.reshape(low_back.shape)
    kernel_gradient(frames, low_wide, low_back, gklow, True)
    kernel_gradient(frames, high_wide.at[:, 3 : 2 * rows - 3], high_back, gkhigh, True)
    store.wait()


def third_kernel(
    frames, shards, tiles, scale_low, scale_high,
    first, second, edge, inner, wc, glow_in, ghigh_in, gklow_in, gkhigh_in, low_wide, high_wide, klow, khigh, plow, phigh, mismatch_in,
    mismatch_hbm, keep, send,
    glow, ghigh, gklow, gkhigh, mismatch,
    feature, gated, fine, low_pad, high_pad, low_student, high_student, low_back, high_back, shard_sums, sems,
):
    del mismatch_in
    _, cells, _, cols, out = edge.shape
    rows = inner.shape[1] + 2
    low_ch, high_ch = low_wide.shape[-1], high_wide.shape[-1]
    mine, tile = lax.axis_index("clip"), lax.axis_index("space")
    even = lax.rem(tile, 2) == 0
    outside = (tile == 0, tile == tiles - 1)
    copies = Copies(sems)
    for total, part in ((glow, glow_in), (ghigh, ghigh_in), (gklow, gklow_in), (gkhigh, gkhigh_in)):
        total[...] = part[...]

    def halo(side, cell, row):
        ours, other = first[cell, row].astype(F32), second[cell, row].astype(F32)
        return jnp.where(even, other, ours) if side == 0 else jnp.where(even, ours, other)

    for side in range(2):
        for cell in range(cells):
            for k in range(2):
                whole = (edge[side, cell, k] + halo(side, cell, k)[:, 0:out]).astype(BF16).astype(F32)
                if k == side:
                    whole = jnp.where(outside[side], 0.0, whole)
                else:
                    feature[side, cell] = whole
                for j, value in enumerate(gate_rows(whole)):
                    gated[j, side, cell, 2 * side + k] = value
                for j, value in enumerate(gate_rows(inner[cell, side * (rows - 4) + k].astype(F32))):
                    gated[j, side, cell, 2 - 2 * side + k] = value

    second_feature(frames, gated, wc, 2, fine)

    for side in range(2):
        for cell in range(cells):
            low_halo, high_halo = halo(side, cell, 2), halo(side, cell, 3)
            at = 0 if side == 0 else 2
            low_pad[side, cell, at] = low_halo[:, 0:low_ch]
            low_pad[side, cell, pl.ds(1 - side, 2)] = low_wide[cell, pl.ds(side * (rows - 2), 2)]
            at = 0 if side == 0 else 5
            high_pad[side, cell, at, 0:cols] = high_halo[:, 0:high_ch]
            high_pad[side, cell, at, cols:] = high_halo[:, high_ch : 2 * high_ch]
            high_pad[side, cell, pl.ds(1 - side, 5)] = high_wide[cell, pl.ds(side * (2 * rows - 5), 5)]
        for step in depthwise(frames, high_pad.at[side], khigh, high_student.at[side]):
            step()
        for step in depthwise(frames, low_pad.at[side], klow, low_student.at[side]):
            step()

    student = low_student[...].reshape(-1, low_ch)
    _, back = level(student, feature[...].reshape(-1, out), plow[...], scale_low, glow)
    low_back[...] = back.reshape(low_back.shape)
    for side in range(2):
        kernel_gradient(frames, low_pad.at[side], low_back.at[side], gklow, False)

    student = high_student[...].reshape(-1, high_ch)
    target = jnp.concatenate(
        [fine_target(fine.at[side, cell], slice(0, 2)) for side in range(2) for cell in range(cells)], axis=0
    )
    value, back = level(student, target, phigh[...], scale_high, ghigh)
    mismatch[...] = value.astype(BF16).reshape(mismatch.shape)
    high_back[...] = back.reshape(high_back.shape)
    stores = [
        copies.start(mismatch.at[0], mismatch_hbm.at[:, pl.ds(0, 4)]),
        copies.start(mismatch.at[1], mismatch_hbm.at[:, pl.ds(2 * rows - 4, 4)]),
    ]
    for side in range(2):
        kernel_gradient(frames, high_pad.at[side], high_back.at[side], gkhigh, False)

    low_rows, high_rows = low_ch // shards, high_ch // shards
    shard_sums[...] = jnp.zeros_like(shard_sums)
    width = gklow.shape[1]
    lane = lax.broadcasted_iota(jnp.int32, gklow.shape, 1)
    wide_high = gkhigh[...]
    if high_ch < width:
        wide_high = jnp.concatenate([wide_high, jnp.zeros((wide_high.shape[0], width - high_ch), F32)], axis=1)
    for s in range(shards):
        shard_sums[s, 0:low_rows, 0:out] = glow[s * low_rows : (s + 1) * low_rows]
        shard_sums[s, low_rows : low_rows + high_rows, 0:out] = ghigh[s * high_rows : (s + 1) * high_rows]
        from_low = pltpu.roll(gklow[...], (width - s * low_rows) % width, 1)
        from_high = pltpu.roll(wide_high, (width + low_rows - s * high_rows) % width, 1)
        both = jnp.where(lane < low_rows, from_low, jnp.where(lane < low_rows + high_rows, from_high, 0.0))
        shard_sums[s, low_rows + high_rows : low_rows + high_rows + 32, 0:width] = both
    if shards == 1:
        keep[0] = shard_sums[0]
        send[0] = shard_sums[0].astype(BF16)
    else:
        bit = lax.rem(mine, 2)
        for k in range(shards // 2):
            keep[k] = shard_sums[2 * k + bit]
            send[k] = shard_sums[2 * k + 1 - bit].astype(BF16)
    for copy in stores:
        copy.wait()


def swaps(start, count):
    lower = range(start, count - 1, 2)
    return [(i, i + 1) for i in lower] + [(i + 1, i) for i in lower]


def pairs(count, bit):
    return [(i, i ^ bit) for i in range(count)]


def sum_over_devices(keep, send, clips, tiles):
    if clips > 1:
        mine = lax.axis_index("clip")
        keep = keep + lax.ppermute(send, "clip", pairs(clips, 1)).astype(F32)
        bit = 2
        while bit < clips:
            halves = keep.reshape((keep.shape[0] // 2, 2) + keep.shape[1:])
            own = lax.rem(lax.div(mine, bit), 2)
            send = lax.dynamic_index_in_dim(halves, 1 - own, 1, False).astype(BF16)
            keep = lax.dynamic_index_in_dim(halves, own, 1, False)
            keep = keep + lax.ppermute(send, "clip", pairs(clips, bit)).astype(F32)
            bit *= 2
    total = keep[0]
    bit = 1
    while bit < tiles:
        bits = (bit, 2 * bit, 3 * bit) if 2 * bit < tiles else (bit,)
        out = total.astype(BF16)
        got = [lax.ppermute(out, "space", pairs(tiles, b)) for b in bits]
        bit *= 2 ** (2 if len(bits) > 1 else 1)
        if bit >= tiles:
            return total, got
        for part in got:
            total = total + part.astype(F32)
    return total, []


def unpack_kernel(total_ref, *refs):
    got, (glow, gklow, ghigh, gkhigh), sums = refs[:-5], refs[-5:-1], refs[-1]
    value = total_ref[...]
    for part in got:
        value = value + part[...].astype(F32)
    sums[...] = value
    low_rows, high_rows, out = glow.shape[0], ghigh.shape[0], glow.shape[1]
    top = low_rows + high_rows
    glow[...] = sums[0:low_rows, 0:out]
    ghigh[...] = sums[low_rows:top, 0:out]
    for t in range(3):
        for h in range(3):
            at = top + 9 * t + 3 * h
            gklow[t, h] = sums[at : at + 3, 0:low_rows]
            gkhigh[t, h] = sums[at : at + 3, low_rows:top]


def on_device(teacher_input, conv_first, conv_second, student_low, student_high, kernel_low, kernel_high, adapter_low, adapter_high):
    clips, tiles = lax.axis_size("clip"), lax.axis_size("space")
    held, frames, rows, cols, depth = teacher_input.shape
    cells = held * frames
    out = conv_first.shape[-1]
    low_ch, high_ch = student_low.shape[-1], student_high.shape[-1]
    low_count = held * frames * rows * cols * clips * tiles
    scales = (1.0 / low_count, 1.0 / (4 * low_count))
    inner = rows - 4
    x = teacher_input.reshape(cells, rows, cols, depth)
    low = student_low.reshape(cells, rows, cols, low_ch)
    high = student_high.reshape(cells, 2 * rows, 2 * cols, high_ch)
    sems = pltpu.SemaphoreType.DMA

    def vm(*specs):
        return [pltpu.VMEM(shape, dtype) for shape, dtype in specs]

    packet = ((cells, 4, cols, max(out, low_ch, 2 * high_ch)), BF16)
    inner_spec = ((cells, rows - 2, cols, out), BF16)
    edge_spec = ((2, cells, 2, cols, out), F32)
    wc_spec = ((2, 2, 3, 2, 2, out, out), BF16)
    weights = ((kernel_low.shape, F32), (kernel_high.shape, F32), (adapter_low.shape, BF16), (adapter_high.shape, BF16))
    inner_feature, edge, first, second, wc, low_wide, high_wide, low_student, high_student, klow, khigh, plow, phigh = pl.pallas_call(
        functools.partial(first_kernel, frames),
        out_shape=tuple(
            vm(
                inner_spec,
                edge_spec,
                packet,
                packet,
                wc_spec,
                (low.shape, F32),
                (high.shape, F32),
                ((cells, rows - 2, cols, low_ch), BF16),
                ((cells, 2 * inner, 2 * cols, high_ch), BF16),
                *weights,
            )
        ),
        in_specs=[HBM] * 9,
        out_specs=(VMEM,) * 13,
        scratch_shapes=vm(
            (x.shape, BF16),
            (conv_first.shape, BF16),
            (conv_second.shape, BF16),
            ((3, cells, rows + 2, cols, out), F32),
            (low.shape, BF16),
            (high.shape, BF16),
        )
        + [sems((18,))],
        compiler_params=pltpu.CompilerParams(vmem_limit_bytes=20 * MIB),
        cost_estimate=pl.CostEstimate(flops=3 * 10**9, bytes_accessed=9 * 10**6, transcendentals=0),
        name="teacher_first",
    )(*in_hbm(x, conv_first, conv_second, low, high, kernel_low, kernel_high, adapter_low, adapter_high))

    first_got = lax.ppermute(first, "space", swaps(0, tiles))
    second_got = lax.ppermute(second, "space", swaps(1, tiles))

    grads = (((low_ch, out), F32), ((high_ch, out), F32), ((32, low_ch), F32), ((32, high_ch), F32))
    mismatch, *sums = pl.pallas_call(
        functools.partial(second_kernel, frames, *scales),
        out_shape=(pltpu.HBM((cells, 2 * rows, 2 * cols, out), BF16), *vm(*grads)),
        in_specs=[VMEM] * 8,
        out_specs=(HBM,) + (VMEM,) * 4,
        scratch_shapes=vm(
            ((cells, 2 * inner, 2 * cols, out), BF16),
            ((3, 1, cells, rows - 2, cols, out), BF16),
            ((1, cells, inner, 2, out // 128, 2 * cols, 128), F32),
            ((cells, rows - 2, cols, low_ch), F32),
            ((cells, 2 * inner, 2 * cols, high_ch), F32),
        )
        + [sems((1,))],
        compiler_params=pltpu.CompilerParams(vmem_limit_bytes=20 * MIB),
        cost_estimate=pl.CostEstimate(flops=5 * 10**9, bytes_accessed=20 * 10**6, transcendentals=0),
        name="inner_rows",
    )(inner_feature, wc, low_wide, high_wide, low_student, high_student, plow, phigh)

    shard_rows = low_ch // clips + high_ch // clips + 32
    shard_rows += -shard_rows % 16
    shard = (max(clips // 2, 1), shard_rows, out)
    mismatch, keep, send = pl.pallas_call(
        functools.partial(third_kernel, frames, clips, tiles, *scales),
        out_shape=(pltpu.HBM(mismatch.shape, BF16), *vm((shard, F32), (shard, BF16))),
        in_specs=[VMEM] * 15 + [HBM],
        out_specs=(HBM, VMEM, VMEM),
        input_output_aliases={15: 0},
        scratch_shapes=vm(
            *grads,
            ((2, cells, 4, 2 * cols, out), BF16),
            ((2, cells, cols, out), F32),
            ((3, 2, cells, 4, cols, out), BF16),
            ((2, cells, 2, 2, out // 128, 2 * cols, 128), F32),
            ((2, cells, 3, cols, low_ch), F32),
            ((2, cells, 6, 2 * cols, high_ch), F32),
            ((2, cells, 1, cols, low_ch), BF16),
            ((2, cells, 4, 2 * cols, high_ch), BF16),
            ((2, cells, 1, cols, low_ch), F32),
            ((2, cells, 4, 2 * cols, high_ch), F32),
            ((clips, shard_rows, out), F32),
        )
        + [sems((2,))],
        compiler_params=pltpu.CompilerParams(vmem_limit_bytes=20 * MIB),
        cost_estimate=pl.CostEstimate(flops=3 * 10**9, bytes_accessed=20 * 10**6, transcendentals=0),
        name="border_rows",
    )(first_got, second_got, edge, inner_feature, wc, *sums, low_wide, high_wide, klow, khigh, plow, phigh, *in_hbm(mismatch))

    total, got = sum_over_devices(keep, send, clips, tiles)
    low_rows, high_rows = low_ch // clips, high_ch // clips
    glow, gklow, ghigh, gkhigh = pl.pallas_call(
        unpack_kernel,
        out_shape=(
            jax.ShapeDtypeStruct((low_rows, out), F32),
            jax.ShapeDtypeStruct((3, 3, 3, low_rows), F32),
            jax.ShapeDtypeStruct((high_rows, out), F32),
            jax.ShapeDtypeStruct((3, 3, 3, high_rows), F32),
        ),
        in_specs=[VMEM] * (1 + len(got)),
        out_specs=(VMEM,) * 4,
        scratch_shapes=[pltpu.VMEM(shard[1:], F32)],
        compiler_params=pltpu.CompilerParams(vmem_limit_bytes=4 * MIB),
        name="unpack",
    )(total, *got)
    return glow, gklow, ghigh, gkhigh, mismatch.reshape(held, frames, 2 * rows, 2 * cols, out)


def solution(mesh):
    tiled = P("clip", None, "space", None, None)
    return jax.shard_map(
        on_device,
        mesh=mesh,
        in_specs=(tiled, P(), P(), tiled, tiled, P(), P(), P(), P()),
        out_specs=(P("clip", None), P(None, None, None, "clip"), P("clip", None), P(None, None, None, "clip"), tiled),
        check_vma=False,
    )
```

time: 48.3 us -> 43.9 us (0.909)
  Pallas kernels: 21 us -> 16.6 us
  starting transfers between devices: 12.3 us -> 12.8 us
  waiting for transfers between devices: 14 us -> 13.5 us
    pallas_call x1, Pallas kernels: 8.13 us -> 4.08 us  [on_device(): pl.pallas_call(functools.partial(second_kernel, frames, *scales), out_sha...]
    pallas_call x1, Pallas kernels: 5.91 us -> 4.29 us  [on_device(): pl.pallas_call(functools.partial(third_kernel, frames, clips, tiles, *sca...]
    pallas_call x1, Pallas kernels: 6.26 us -> 7.55 us  [on_device(): pl.pallas_call(functools.partial(first_kernel, frames), out_shape=tuple(v...]
    ppermute x4, starting transfers between devices: 7 us -> 7.49 us  [sum_over_devices(): got = [lax.ppermute(out, 'space', pairs(tiles, b)) for b in bits]]
    ppermute x4, waiting for transfers between devices: 9.9 us -> 9.42 us  [sum_over_devices(): got = [lax.ppermute(out, 'space', pairs(tiles, b)) for b in bits]]
  transfers between devices with their start and end apart: 8 -> 8, of which waited for: 6 -> 6; matrix products, arithmetic and copies ran while one was open for 0% -> 0% of each run, Pallas kernels for 17% -> 9%
where the time goes in v3:
time: 43.9 us; the launch traced here: 43.7 us
  Pallas kernels  16.6 us (38%)
  waiting for transfers between devices  13.5 us (31%)
  starting transfers between devices  12.8 us (29%)
  between operations  0.73 us (2%)
    ppermute x4, waiting for transfers between devices, sum_over_devices(): got = [lax.ppermute(out, 'space', pairs(tiles, b)) for b in bits]  9.42 us
    pallas_call x1, Pallas kernels, on_device(): pl.pallas_call(functools.partial(first_kernel, frames), out_shape=tuple(v...  7.55 us
    ppermute x4, starting transfers between devices, sum_over_devices(): got = [lax.ppermute(out, 'space', pairs(tiles, b)) for b in bits]  7.49 us
    pallas_call x1, Pallas kernels, on_device(): pl.pallas_call(functools.partial(third_kernel, frames, clips, tiles, *sca...  4.29 us
    pallas_call x1, Pallas kernels, on_device(): pl.pallas_call(functools.partial(second_kernel, frames, *scales), out_sha...  4.08 us
    ppermute x1, starting transfers between devices, on_device(): first_got = lax.ppermute(first, 'space', swaps(0, tiles))  3 us
    ppermute x1, waiting for transfers between devices, sum_over_devices(): keep = keep + lax.ppermute(send, 'clip', pairs(clips, bit)).astype(F32)  2.74 us
    ppermute x1, starting transfers between devices, sum_over_devices(): keep = keep + lax.ppermute(send, 'clip', pairs(clips, bit)).astype(F32)  1.59 us
  transfers between devices with their start and end apart: 8, of which 6 were waited for; matrix products, arithmetic and copies ran while one was open for 0% of the time, Pallas kernels for 9%

profile of v3, /device:TPU:0, one launch (start us, length us, event | category | flops | bytes accessed | tf_op | source)
XLA Modules:
  0.0 43.7 jit_solution(8874957601081418406)
XLA Ops:
  0.6 7.6 %teacher_first.1 = (bf16[2,6,32,256]{3,2,1,0:T(8,128)(2,1)S(1)}, f32[2,2,2,32,256]{4,3,2,1,0:T(8,128)S(1)}, bf16[2,4,32,256]{3,2,1,0:T(8,128)(2,1)S(1)}, bf16[2,...) custom-call(bf16[2,8,32,512]{3,2,1,0:T(8,128)(2,1)} %bitcast.12, ...), custom_call_target="tpu_custom_call" | custom-call | flops 3000000000 | bytes 9000000 | tf_op jit(solution)/shard_map/teacher_first/pallas_call | solution.py:505
  8.2 3.0 %collective-permute-start = (bf16[2,4,32,256]{3,2,1,0:T(8,128)(2,1)S(1)}, bf16[2,4,32,256]{3,2,1,0:T(8,128)(2,1)S(1)}, u32[]{:S(2)}, u32[]{:S(2)}) collective-permute-start(bf16[2,4,32,256]{3,2,1,0:T(8,128)(2,1)S(1)} %get-tuple-element.30), channel_id=1, source_target_pairs={{0,1},{2,3},{4,5},{6,7},{1,0},{3,2},{5,4},{7,6},{8,9},{10,11},{12,... | collective-permute-start | bytes 393224 | tf_op jit(solution)/shard_map/ppermute | solution.py:537
  11.2 0.7 %collective-permute-start.1 = (bf16[2,4,32,256]{3,2,1,0:T(8,128)(2,1)S(1)}, bf16[2,4,32,256]{3,2,1,0:T(8,128)(2,1)S(1)}, u32[]{:S(2)}, u32[]{:S(2)}) collective-permute-start(bf16[2,4,32,256]{3,2,1,0:T(8,128)(2,1)S(1)} %get-tuple-element.31), channel_id=1, source_target_pairs={{1,2},{3,4},{5,6},{2,1},{4,3},{6,5},{9,10},{11,12},{13,14},{10,9},... | collective-permute-start | bytes 393224 | tf_op jit(solution)/shard_map/ppermute | solution.py:538
  11.9 4.1 %inner_rows.1 = (bf16[2,16,64,256]{3,2,1,0:T(8,128)(2,1)}, f32[256,256]{1,0:T(8,128)S(1)}, f32[128,256]{1,0:T(8,128)S(1)}, f32[32,256]{1,0:T(8,128)S(1)}, f32[32,128]{1,0:T(8,128)S(1)}) custom-call(bf16[2,6,32,256]{3,2,1,0:T(8,128)(2,1)S(1)} %get-tuple-element.33.feature.inner, bf16[2,2,3,2,2,256,256]{6,5,4,3,2,1,0:T(8,128)(2,1)S(1)} %get-tuple-element.34.wc, ...), custom_call_target="tpu_custom_call" | custom-call | flops 5000000000 | bytes 20000000 | tf_op jit(solution)/shard_map/inner_rows/pallas_call | solution.py:541
  16.0 0.0 collective-permute-done.first
  16.0 0.0 collective-permute-done.1.second
  16.0 4.3 %border_rows.1 = (bf16[2,16,64,256]{3,2,1,0:T(8,128)(2,1)}, f32[2,128,256]{2,1,0:T(8,128)S(1)}, bf16[2,128,256]{2,1,0:T(8,128)(2,1)S(1)}) custom-call(bf16[2,4,32,256]{3,2,1,0:T(8,128)(2,1)S(1)} %collective-permute-done.first, bf16[2,4,32,256]{3,2,1,0:T(8,128)(2,1)S(1)} %collective-permute-done.1.second, ...), custom_call_target="tpu_custom_call", output_to_operand_aliasing={{0}: (15, {})} | custom-call | flops 3000000000 | bytes 20000000 | tf_op jit(solution)/shard_map/border_rows/pallas_call | solution.py:562
  20.3 0.1 collective-permute-start.2
  20.4 1.3 %collective-permute-done.2 = bf16[2,128,256]{2,1,0:T(8,128)(2,1)S(1)} collective-permute-done((bf16[2,128,256]{2,1,0:T(8,128)(2,1)S(1)}, bf16[2,128,256]{2,1,0:T(8,128)(2,1)S(1)}, u32[]{:S(2)}, u32[]{:S(2)}) %collective-permute-start.2) | collective-permute-done | bytes 131104 | tf_op jit(solution)/shard_map/ppermute | solution.py:443
  21.7 1.6 %collective-permute-start.3 = (bf16[1,128,256]{2,1,0:T(8,128)(2,1)S(1)}, bf16[1,128,256]{2,1,0:T(8,128)(2,1)S(1)}, u32[]{:S(2)}, u32[]{:S(2)}) collective-permute-start(bf16[1,128,256]{2,1,0:T(8,128)(2,1)S(1)} %dynamic-slice_convert_fusion), channel_id=1, source_target_pairs={{0,16},{8,24},{16,0},{24,8},{1,17},{9,25},{17,1},{25,9},{2,18},{10... | collective-permute-start | bytes 196616 | tf_op jit(solution)/shard_map/ppermute | solution.py:450
  23.3 2.7 %collective-permute-done.3 = bf16[1,128,256]{2,1,0:T(8,128)(2,1)S(1)} collective-permute-done((bf16[1,128,256]{2,1,0:T(8,128)(2,1)S(1)}, bf16[1,128,256]{2,1,0:T(8,128)(2,1)S(1)}, u32[]{:S(2)}, u32[]{:S(2)}) %collective-permute-start.3) | collective-permute-done | bytes 65568 | tf_op jit(solution)/shard_map/ppermute | solution.py:450
  26.1 4.3 %collective-permute-start.4 = (bf16[128,256]{1,0:T(8,128)(2,1)S(1)}, bf16[128,256]{1,0:T(8,128)(2,1)S(1)}, u32[]{:S(2)}, u32[]{:S(2)}) collective-permute-start(bf16[128,256]{1,0:T(8,128)(2,1)S(1)} %bitcast_convert_fusion), channel_id=1, source_target_pairs={{0,1},{1,0},{2,3},{3,2},{4,5},{5,4},{6,7},{7,6},{8,9},{9,8},{10,11... | collective-permute-start | bytes 196616 | tf_op jit(solution)/shard_map/ppermute | solution.py:457
  30.4 1.6 %collective-permute-start.5 = (bf16[128,256]{1,0:T(8,128)(2,1)S(1)}, bf16[128,256]{1,0:T(8,128)(2,1)S(1)}, u32[]{:S(2)}, u32[]{:S(2)}) collective-permute-start(bf16[128,256]{1,0:T(8,128)(2,1)S(1)} %bitcast_convert_fusion), channel_id=1, source_target_pairs={{0,2},{1,3},{2,0},{3,1},{4,6},{5,7},{6,4},{7,5},{8,10},{9,11},{10,... | collective-permute-start | bytes 196616 | tf_op jit(solution)/shard_map/ppermute | solution.py:457
  32.0 0.1 collective-permute-start.6
  32.2 0.5 %collective-permute-done.4 = bf16[128,256]{1,0:T(8,128)(2,1)S(1)} collective-permute-done((bf16[128,256]{1,0:T(8,128)(2,1)S(1)}, bf16[128,256]{1,0:T(8,128)(2,1)S(1)}, u32[]{:S(2)}, u32[]{:S(2)}) %collective-permute-start.4) | collective-permute-done | bytes 65568 | tf_op jit(solution)/shard_map/ppermute | solution.py:457
  32.7 2.0 %collective-permute-done.5 = bf16[128,256]{1,0:T(8,128)(2,1)S(1)} collective-permute-done((bf16[128,256]{1,0:T(8,128)(2,1)S(1)}, bf16[128,256]{1,0:T(8,128)(2,1)S(1)}, u32[]{:S(2)}, u32[]{:S(2)}) %collective-permute-start.5) | collective-permute-done | bytes 65568 | tf_op jit(solution)/shard_map/ppermute | solution.py:457
  34.7 2.5 %collective-permute-done.6 = bf16[128,256]{1,0:T(8,128)(2,1)S(1)} collective-permute-done((bf16[128,256]{1,0:T(8,128)(2,1)S(1)}, bf16[128,256]{1,0:T(8,128)(2,1)S(1)}, u32[]{:S(2)}, u32[]{:S(2)}) %collective-permute-start.6) | collective-permute-done | bytes 65568 | tf_op jit(solution)/shard_map/ppermute | solution.py:457
  37.2 1.4 %collective-permute-start.7 = (bf16[128,256]{1,0:T(8,128)(2,1)S(1)}, bf16[128,256]{1,0:T(8,128)(2,1)S(1)}, u32[]{:S(2)}, u32[]{:S(2)}) collective-permute-start(bf16[128,256]{1,0:T(8,128)(2,1)S(1)} %get-tuple-element.55), channel_id=1, source_target_pairs={{0,4},{1,5},{2,6},{3,7},{4,0},{5,1},{6,2},{7,3},{8,12},{9,13},{10,... | collective-permute-start | bytes 196616 | tf_op jit(solution)/shard_map/ppermute | solution.py:457
  38.6 4.4 %collective-permute-done.7.refs_0_ = bf16[128,256]{1,0:T(8,128)(2,1)S(1)} collective-permute-done((bf16[128,256]{1,0:T(8,128)(2,1)S(1)}, bf16[128,256]{1,0:T(8,128)(2,1)S(1)}, u32[]{:S(2)}, u32[]{:S(2)}) %collective-permute-start.7) | collective-permute-done | bytes 65568 | tf_op jit(solution)/shard_map/ppermute | solution.py:457
  43.0 0.7 %unpack.1 = (f32[64,256]{1,0:T(8,128)}, f32[3,3,3,64]{3,2,1,0:T(4,128)}, f32[32,256]{1,0:T(8,128)}, f32[3,3,3,32]{3,2,1,0:T(4,128)}) custom-call(f32[128,256]{1,0:T(8,128)S(1)} %get-tuple-element.56.total_ref, bf16[128,256]{1,0:T(8,128)(2,1)S(1)} %collective-permute-done.7.refs_0_), custom_call_target="tpu_custom_call" | custom-call | tf_op jit(solution)/shard_map/unpack/pallas_call | solution.py:590
  (4 shorter events, 0.1 us)
Async XLA Ops:
  8.2 7.8 %collective-permute-start = (bf16[2,4,32,256]{3,2,1,0:T(8,128)(2,1)S(1)}, bf16[2,4,32,256]{3,2,1,0:T(8,128)(2,1)S(1)}, u32[]{:S(2)}, u32[]{:S(2)}) collective-permute-start(bf16[2,4,32,256]{3,2,1,0:T(8,128)(2,1)S(1)} %get-tuple-element.30), channel_id=1, source_target_pairs={{0,1},{2,3},{4,5},{6,7},{1,0},{3,2},{5,4},{7,6},{8,9},{10,11},{12,... | collective-permute-start | bytes 393224 | tf_op jit(solution)/shard_map/ppermute | solution.py:537
  11.2 4.8 %collective-permute-start.1 = (bf16[2,4,32,256]{3,2,1,0:T(8,128)(2,1)S(1)}, bf16[2,4,32,256]{3,2,1,0:T(8,128)(2,1)S(1)}, u32[]{:S(2)}, u32[]{:S(2)}) collective-permute-start(bf16[2,4,32,256]{3,2,1,0:T(8,128)(2,1)S(1)} %get-tuple-element.31), channel_id=1, source_target_pairs={{1,2},{3,4},{5,6},{2,1},{4,3},{6,5},{9,10},{11,12},{13,14},{10,9},... | collective-permute-start | bytes 393224 | tf_op jit(solution)/shard_map/ppermute | solution.py:538
  20.3 1.4 %collective-permute-start.2 = (bf16[2,128,256]{2,1,0:T(8,128)(2,1)S(1)}, bf16[2,128,256]{2,1,0:T(8,128)(2,1)S(1)}, u32[]{:S(2)}, u32[]{:S(2)}) collective-permute-start(bf16[2,128,256]{2,1,0:T(8,128)(2,1)S(1)} %get-tuple-element.49), channel_id=1, source_target_pairs={{0,8},{8,0},{16,24},{24,16},{1,9},{9,1},{17,25},{25,17},{2,10},{10... | collective-permute-start | bytes 393224 | tf_op jit(solution)/shard_map/ppermute | solution.py:443
  21.7 4.3 %collective-permute-start.3 = (bf16[1,128,256]{2,1,0:T(8,128)(2,1)S(1)}, bf16[1,128,256]{2,1,0:T(8,128)(2,1)S(1)}, u32[]{:S(2)}, u32[]{:S(2)}) collective-permute-start(bf16[1,128,256]{2,1,0:T(8,128)(2,1)S(1)} %dynamic-slice_convert_fusion), channel_id=1, source_target_pairs={{0,16},{8,24},{16,0},{24,8},{1,17},{9,25},{17,1},{25,9},{2,18},{10... | collective-permute-start | bytes 196616 | tf_op jit(solution)/shard_map/ppermute | solution.py:450
  26.1 6.6 %collective-permute-start.4 = (bf16[128,256]{1,0:T(8,128)(2,1)S(1)}, bf16[128,256]{1,0:T(8,128)(2,1)S(1)}, u32[]{:S(2)}, u32[]{:S(2)}) collective-permute-start(bf16[128,256]{1,0:T(8,128)(2,1)S(1)} %bitcast_convert_fusion), channel_id=1, source_target_pairs={{0,1},{1,0},{2,3},{3,2},{4,5},{5,4},{6,7},{7,6},{8,9},{9,8},{10,11... | collective-permute-start | bytes 196616 | tf_op jit(solution)/shard_map/ppermute | solution.py:457
  30.4 4.3 %collective-permute-start.5 = (bf16[128,256]{1,0:T(8,128)(2,1)S(1)}, bf16[128,256]{1,0:T(8,128)(2,1)S(1)}, u32[]{:S(2)}, u32[]{:S(2)}) collective-permute-start(bf16[128,256]{1,0:T(8,128)(2,1)S(1)} %bitcast_convert_fusion), channel_id=1, source_target_pairs={{0,2},{1,3},{2,0},{3,1},{4,6},{5,7},{6,4},{7,5},{8,10},{9,11},{10,... | collective-permute-start | bytes 196616 | tf_op jit(solution)/shard_map/ppermute | solution.py:457
  32.0 5.2 %collective-permute-start.6 = (bf16[128,256]{1,0:T(8,128)(2,1)S(1)}, bf16[128,256]{1,0:T(8,128)(2,1)S(1)}, u32[]{:S(2)}, u32[]{:S(2)}) collective-permute-start(bf16[128,256]{1,0:T(8,128)(2,1)S(1)} %bitcast_convert_fusion), channel_id=1, source_target_pairs={{0,3},{1,2},{2,1},{3,0},{4,7},{5,6},{6,5},{7,4},{8,11},{9,10},{10,... | collective-permute-start | bytes 196616 | tf_op jit(solution)/shard_map/ppermute | solution.py:457
  37.2 5.8 %collective-permute-start.7 = (bf16[128,256]{1,0:T(8,128)(2,1)S(1)}, bf16[128,256]{1,0:T(8,128)(2,1)S(1)}, u32[]{:S(2)}, u32[]{:S(2)}) collective-permute-start(bf16[128,256]{1,0:T(8,128)(2,1)S(1)} %get-tuple-element.55), channel_id=1, source_target_pairs={{0,4},{1,5},{2,6},{3,7},{4,0},{5,1},{6,2},{7,3},{8,12},{9,13},{10,... | collective-permute-start | bytes 196616 | tf_op jit(solution)/shard_map/ppermute | solution.py:457

commit v4 on v3

--- a/solution.py
+++ b/solution.py
@@ -350,7 +350,8 @@
 
     def halo(side, cell, row):
         ours, other = first[cell, row].astype(F32), second[cell, row].astype(F32)
-        return jnp.where(even, other, ours) if side == 0 else jnp.where(even, ours, other)
+        found = jnp.where(even, other, ours) if side == 0 else jnp.where(even, ours, other)
+        return jnp.where(outside[side], 0.0, found)
 
     for side in range(2):
         for cell in range(cells):
@@ -405,6 +406,7 @@
     low_rows, high_rows = low_ch // shards, high_ch // shards
     shard_sums[...] = jnp.zeros_like(shard_sums)
     width = gklow.shape[1]
+    half = out // 2
     lane = lax.broadcasted_iota(jnp.int32, gklow.shape, 1)
     wide_high = gkhigh[...]
     if high_ch < width:
@@ -415,7 +417,9 @@
         from_low = pltpu.roll(gklow[...], (width - s * low_rows) % width, 1)
         from_high = pltpu.roll(wide_high, (width + low_rows - s * high_rows) % width, 1)
         both = jnp.where(lane < low_rows, from_low, jnp.where(lane < low_rows + high_rows, from_high, 0.0))
-        shard_sums[s, low_rows + high_rows : low_rows + high_rows + 32, 0:width] = both
+        top = low_rows + high_rows
+        shard_sums[s, top : top + 16, 0:half] = both[0:16, 0:half]
+        shard_sums[s, top : top + 16, half : 2 * half] = both[16:32, 0:half]
     if shards == 1:
         keep[0] = shard_sums[0]
         send[0] = shard_sums[0].astype(BF16)
@@ -428,39 +432,57 @@
         copy.wait()
 
 
-def swaps(start, count):
-    lower = range(start, count - 1, 2)
-    return [(i, i + 1) for i in lower] + [(i + 1, i) for i in lower]
+def swaps(clips, tiles, start):
+    found = []
+    for clip in range(clips):
+        for tile in range(tiles):
+            other = tile + 1 if (tile - start) % 2 == 0 else tile - 1
+            if 0 <= other < tiles:
+                found.append((clip * tiles + tile, clip * tiles + other))
+            elif clips % 2 == 0:
+                found.append((clip * tiles + tile, (clip ^ 1) * tiles + tile))
+    return found
 
 
 def pairs(count, bit):
     return [(i, i ^ bit) for i in range(count)]
 
 
+def split_shards(keep, bit):
+    halves = keep.reshape((keep.shape[0] // 2, 2) + keep.shape[1:])
+    own = lax.rem(lax.div(lax.axis_index("clip"), bit), 2)
+    send = lax.dynamic_index_in_dim(halves, 1 - own, 1, False).astype(BF16)
+    return lax.dynamic_index_in_dim(halves, own, 1, False), send
+
+
 def sum_over_devices(keep, send, clips, tiles):
+    clip_bit, tile_bit = 2, 1
     if clips > 1:
-        mine = lax.axis_index("clip")
         keep = keep + lax.ppermute(send, "clip", pairs(clips, 1)).astype(F32)
-        bit = 2
-        while bit < clips:
-            halves = keep.reshape((keep.shape[0] // 2, 2) + keep.shape[1:])
-            own = lax.rem(lax.div(mine, bit), 2)
-            send = lax.dynamic_index_in_dim(halves, 1 - own, 1, False).astype(BF16)
-            keep = lax.dynamic_index_in_dim(halves, own, 1, False)
-            keep = keep + lax.ppermute(send, "clip", pairs(clips, bit)).astype(F32)
-            bit *= 2
-    total = keep[0]
-    bit = 1
-    while bit < tiles:
-        bits = (bit, 2 * bit, 3 * bit) if 2 * bit < tiles else (bit,)
+    if clips > 2 and tiles > 1:
+        keep, send = split_shards(keep, 2)
+        across = [(c * tiles + t, (c ^ 2) * tiles + (t ^ 1)) for c in range(clips) for t in range(tiles)]
+        got = (
+            lax.ppermute(send, "clip", pairs(clips, 2)),
+            lax.ppermute(send, ("clip", "space"), across),
+            lax.ppermute(keep.astype(BF16), "space", pairs(tiles, 1)),
+        )
+        for part in got:
+            keep = keep + part.astype(F32)
+        clip_bit, tile_bit = 4, 2
+    while clip_bit < clips:
+        keep, send = split_shards(keep, clip_bit)
+        keep = keep + lax.ppermute(send, "clip", pairs(clips, clip_bit)).astype(F32)
+        clip_bit *= 2
+    total, got = keep[0], []
+    while tile_bit < tiles:
+        for part in got:
+            total = total + part.astype(F32)
+        bits = (tile_bit, 2 * tile_bit, 3 * tile_bit) if 2 * tile_bit < tiles else (tile_bit,)
         out = total.astype(BF16)
         got = [lax.ppermute(out, "space", pairs(tiles, b)) for b in bits]
-        bit *= 2 ** (2 if len(bits) > 1 else 1)
-        if bit >= tiles:
-            return total, got
-        for part in got:
-            total = total + part.astype(F32)
-    return total, []
+        tile_bit *= 2 ** (2 if len(bits) > 1 else 1)
+    return total, got
 
 
 def unpack_kernel(total_ref, *refs):
@@ -473,11 +495,11 @@
     top = low_rows + high_rows
     glow[...] = sums[0:low_rows, 0:out]
     ghigh[...] = sums[low_rows:top, 0:out]
-    for t in range(3):
-        for h in range(3):
-            at = top + 9 * t + 3 * h
-            gklow[t, h] = sums[at : at + 3, 0:low_rows]
-            gkhigh[t, h] = sums[at : at + 3, low_rows:top]
+    for k in range(27):
+        at, lane = top + k % 16, k // 16 * (out // 2)
+        tap, row, col = k // 9, k // 3 % 3, k % 3
+        gklow[tap, row, col : col + 1] = sums[at : at + 1, lane : lane + low_rows]
+        gkhigh[tap, row, col : col + 1] = sums[at : at + 1, lane + low_rows : lane + top]
 
 
 def on_device(teacher_input, conv_first, conv_second, student_low, student_high, kernel_low, kernel_high, adapter_low, adapter_high):
@@ -534,8 +556,8 @@
         name="teacher_first",
     )(*in_hbm(x, conv_first, conv_second, low, high, kernel_low, kernel_high, adapter_low, adapter_high))
 
-    first_got = lax.ppermute(first, "space", swaps(0, tiles))
-    second_got = lax.ppermute(second, "space", swaps(1, tiles))
+    first_got = lax.ppermute(first, ("clip", "space"), swaps(clips, tiles, 0))
+    second_got = lax.ppermute(second, ("clip", "space"), swaps(clips, tiles, 1))
 
     grads = (((low_ch, out), F32), ((high_ch, out), F32), ((32, low_ch), F32), ((32, high_ch), F32))
     mismatch, *sums = pl.pallas_call(
@@ -556,7 +578,7 @@
         name="inner_rows",
     )(inner_feature, wc, low_wide, high_wide, low_student, high_student, plow, phigh)
 
-    shard_rows = low_ch // clips + high_ch // clips + 32
+    shard_rows = low_ch // clips + high_ch // clips + 16
     shard_rows += -shard_rows % 16
     shard = (max(clips // 2, 1), shard_rows, out)
     mismatch, keep, send = pl.pallas_call(

time: 43.9 us -> 41.4 us (0.943)
  waiting for transfers between devices: 13.5 us -> 12.2 us
  starting transfers between devices: 12.8 us -> 11.6 us
    ppermute x4 -> x3, waiting for transfers between devices: 9.42 us -> 5.35 us  [sum_over_devices(): got = [lax.ppermute(out, 'space', pairs(tiles, b)) for b in bits]]
    ppermute x4 -> x3, starting transfers between devices: 7.49 us -> 4.45 us  [sum_over_devices(): got = [lax.ppermute(out, 'space', pairs(tiles, b)) for b in bits]]
    ppermute x3 -> x5, waiting for transfers between devices: 2.74 us -> 5.59 us  [the longest x1 2.42 us: sum_over_devices(): lax.ppermute(send, ('clip', 'space'), across)]
    ppermute x3 -> x5, starting transfers between devices: 5.25 us -> 7.07 us  [the longest x1 3 us: on_device(): first_got = lax.ppermute(first, ('clip', 'space'), swaps(clips, tiles, 0))]
  transfers between devices with their start and end apart: 8 -> 9, of which waited for: 6 -> 8; matrix products, arithmetic and copies ran while one was open for 0% -> 0% of each run, Pallas kernels for 9% -> 10%
where the time goes in v4:
time: 41.4 us; the launch traced here: 41.3 us
  Pallas kernels  16.7 us (40%)
  waiting for transfers between devices  12.2 us (29%)
  starting transfers between devices  11.6 us (28%)
  between operations  0.71 us (2%)
    pallas_call x1, Pallas kernels, on_device(): pl.pallas_call(functools.partial(first_kernel, frames), out_shape=tuple(v...  7.56 us
    ppermute x3, waiting for transfers between devices, sum_over_devices(): got = [lax.ppermute(out, 'space', pairs(tiles, b)) for b in bits]  5.35 us
    ppermute x3, starting transfers between devices, sum_over_devices(): got = [lax.ppermute(out, 'space', pairs(tiles, b)) for b in bits]  4.45 us
    pallas_call x1, Pallas kernels, on_device(): pl.pallas_call(functools.partial(third_kernel, frames, clips, tiles, *sca...  4.3 us
    pallas_call x1, Pallas kernels, on_device(): pl.pallas_call(functools.partial(second_kernel, frames, *scales), out_sha...  4.09 us
    ppermute x1, starting transfers between devices, on_device(): first_got = lax.ppermute(first, ('clip', 'space'), swaps(clips, tiles, 0))  3 us
    ppermute x1, starting transfers between devices, sum_over_devices(): lax.ppermute(send, ('clip', 'space'), across)  2.42 us
    ppermute x1, waiting for transfers between devices, sum_over_devices(): lax.ppermute(send, ('clip', 'space'), across)  2.42 us
  transfers between devices with their start and end apart: 9, of which 8 were waited for; matrix products, arithmetic and copies ran while one was open for 0% of the time, Pallas kernels for 10%

profile of v4, /device:TPU:0, one launch (start us, length us, event | category | flops | bytes accessed | tf_op | source)
XLA Modules:
  0.0 41.3 jit_solution(3877319704355948246)
XLA Ops:
  0.6 7.6 %teacher_first.1 = (bf16[2,6,32,256]{3,2,1,0:T(8,128)(2,1)S(1)}, f32[2,2,2,32,256]{4,3,2,1,0:T(8,128)S(1)}, bf16[2,4,32,256]{3,2,1,0:T(8,128)(2,1)S(1)}, bf16[2,...) custom-call(bf16[2,8,32,512]{3,2,1,0:T(8,128)(2,1)} %bitcast.7, ...), custom_call_target="tpu_custom_call" | custom-call | flops 3000000000 | bytes 9000000 | tf_op jit(solution)/shard_map/teacher_first/pallas_call | solution.py:527
  8.2 3.0 %collective-permute-start = (bf16[2,4,32,256]{3,2,1,0:T(8,128)(2,1)S(1)}, bf16[2,4,32,256]{3,2,1,0:T(8,128)(2,1)S(1)}, u32[]{:S(2)}, u32[]{:S(2)}) collective-permute-start(bf16[2,4,32,256]{3,2,1,0:T(8,128)(2,1)S(1)} %get-tuple-element.30), channel_id=1, source_target_pairs={{0,1},{1,0},{2,3},{3,2},{4,5},{5,4},{6,7},{7,6},{8,9},{9,8},{10,11... | collective-permute-start | bytes 393224 | tf_op jit(solution)/shard_map/ppermute | solution.py:559
  11.2 0.0 collective-permute-start.1
  11.2 4.1 %inner_rows.1 = (bf16[2,16,64,256]{3,2,1,0:T(8,128)(2,1)}, f32[256,256]{1,0:T(8,128)S(1)}, f32[128,256]{1,0:T(8,128)S(1)}, f32[32,256]{1,0:T(8,128)S(1)}, f32[32,128]{1,0:T(8,128)S(1)}) custom-call(bf16[2,6,32,256]{3,2,1,0:T(8,128)(2,1)S(1)} %get-tuple-element.33.feature.inner, bf16[2,2,3,2,2,256,256]{6,5,4,3,2,1,0:T(8,128)(2,1)S(1)} %get-tuple-element.34.wc, ...), custom_call_target="tpu_custom_call" | custom-call | flops 5000000000 | bytes 20000000 | tf_op jit(solution)/shard_map/inner_rows/pallas_call | solution.py:563
  15.3 1.5 %collective-permute-done.first = bf16[2,4,32,256]{3,2,1,0:T(8,128)(2,1)S(1)} collective-permute-done((bf16[2,4,32,256]{3,2,1,0:T(8,128)(2,1)S(1)}, bf16[2,4,32,256]{3,2,1,0:T(8,128)(2,1)S(1)}, u32[]{:S(2)}, u32[]{:S(2)}) %collective-permute-start) | collective-permute-done | bytes 131104 | tf_op jit(solution)/shard_map/ppermute | solution.py:559
  16.8 0.0 collective-permute-done.1.second
  16.8 4.3 %border_rows.1 = (bf16[2,16,64,256]{3,2,1,0:T(8,128)(2,1)}, f32[2,112,256]{2,1,0:T(8,128)S(1)}, bf16[2,112,256]{2,1,0:T(8,128)(2,1)S(1)}) custom-call(bf16[2,4,32,256]{3,2,1,0:T(8,128)(2,1)S(1)} %collective-permute-done.first, bf16[2,4,32,256]{3,2,1,0:T(8,128)(2,1)S(1)} %collective-permute-done.1.second, ...), custom_call_target="tpu_custom_call", output_to_operand_aliasing={{0}: (15, {})} | custom-call | flops 3000000000 | bytes 20000000 | tf_op jit(solution)/shard_map/border_rows/pallas_call | solution.py:584
  21.1 0.1 collective-permute-start.2
  21.2 1.3 %collective-permute-done.2 = bf16[2,112,256]{2,1,0:T(8,128)(2,1)S(1)} collective-permute-done((bf16[2,112,256]{2,1,0:T(8,128)(2,1)S(1)}, bf16[2,112,256]{2,1,0:T(8,128)(2,1)S(1)}, u32[]{:S(2)}, u32[]{:S(2)}) %collective-permute-start.2) | collective-permute-done | bytes 114720 | tf_op jit(solution)/shard_map/ppermute | solution.py:461
  22.5 1.6 %collective-permute-start.3 = (bf16[1,112,256]{2,1,0:T(8,128)(2,1)S(1)}, bf16[1,112,256]{2,1,0:T(8,128)(2,1)S(1)}, u32[]{:S(2)}, u32[]{:S(2)}) collective-permute-start(bf16[1,112,256]{2,1,0:T(8,128)(2,1)S(1)} %get-tuple-element.57), channel_id=1, source_target_pairs={{0,16},{8,24},{16,0},{24,8},{1,17},{9,25},{17,1},{25,9},{2,18},{10... | collective-permute-start | bytes 172040 | tf_op jit(solution)/shard_map/ppermute | solution.py:466
  24.1 2.4 %collective-permute-start.4 = (bf16[1,112,256]{2,1,0:T(8,128)(2,1)S(1)}, bf16[1,112,256]{2,1,0:T(8,128)(2,1)S(1)}, u32[]{:S(2)}, u32[]{:S(2)}) collective-permute-start(bf16[1,112,256]{2,1,0:T(8,128)(2,1)S(1)} %get-tuple-element.57), channel_id=1, source_target_pairs={{0,17},{1,16},{2,19},{3,18},{4,21},{5,20},{6,23},{7,22},{8,25},{9,... | collective-permute-start | bytes 172040 | tf_op jit(solution)/shard_map/ppermute | solution.py:467
  26.5 0.1 collective-permute-start.5
  26.6 0.2 collective-permute-done.3
  26.8 2.4 %collective-permute-done.4 = bf16[1,112,256]{2,1,0:T(8,128)(2,1)S(1)} collective-permute-done((bf16[1,112,256]{2,1,0:T(8,128)(2,1)S(1)}, bf16[1,112,256]{2,1,0:T(8,128)(2,1)S(1)}, u32[]{:S(2)}, u32[]{:S(2)}) %collective-permute-start.4) | collective-permute-done | bytes 57376 | tf_op jit(solution)/shard_map/ppermute | solution.py:467
  29.2 1.5 %collective-permute-done.5 = bf16[1,112,256]{2,1,0:T(8,128)(2,1)S(1)} collective-permute-done((bf16[1,112,256]{2,1,0:T(8,128)(2,1)S(1)}, bf16[1,112,256]{2,1,0:T(8,128)(2,1)S(1)}, u32[]{:S(2)}, u32[]{:S(2)}) %collective-permute-start.5) | collective-permute-done | bytes 57376 | tf_op jit(solution)/shard_map/ppermute | solution.py:468
  30.7 1.6 %collective-permute-start.6 = (bf16[112,256]{1,0:T(8,128)(2,1)S(1)}, bf16[112,256]{1,0:T(8,128)(2,1)S(1)}, u32[]{:S(2)}, u32[]{:S(2)}) collective-permute-start(bf16[112,256]{1,0:T(8,128)(2,1)S(1)} %get-tuple-element.55), channel_id=1, source_target_pairs={{0,2},{1,3},{2,0},{3,1},{4,6},{5,7},{6,4},{7,5},{8,10},{9,11},{10,... | collective-permute-start | bytes 172040 | tf_op jit(solution)/shard_map/ppermute | solution.py:483
  32.4 2.2 %collective-permute-start.7 = (bf16[112,256]{1,0:T(8,128)(2,1)S(1)}, bf16[112,256]{1,0:T(8,128)(2,1)S(1)}, u32[]{:S(2)}, u32[]{:S(2)}) collective-permute-start(bf16[112,256]{1,0:T(8,128)(2,1)S(1)} %get-tuple-element.55), channel_id=1, source_target_pairs={{0,4},{1,5},{2,6},{3,7},{4,0},{5,1},{6,2},{7,3},{8,12},{9,13},{10,... | collective-permute-start | bytes 172040 | tf_op jit(solution)/shard_map/ppermute | solution.py:483
  34.6 0.6 %collective-permute-start.8 = (bf16[112,256]{1,0:T(8,128)(2,1)S(1)}, bf16[112,256]{1,0:T(8,128)(2,1)S(1)}, u32[]{:S(2)}, u32[]{:S(2)}) collective-permute-start(bf16[112,256]{1,0:T(8,128)(2,1)S(1)} %get-tuple-element.55), channel_id=1, source_target_pairs={{0,6},{1,7},{2,4},{3,5},{4,2},{5,3},{6,0},{7,1},{8,14},{9,15},{10,... | collective-permute-start | bytes 172040 | tf_op jit(solution)/shard_map/ppermute | solution.py:483
  35.2 0.3 collective-permute-done.6.refs_0_
  35.5 3.2 %collective-permute-done.7.refs_1_ = bf16[112,256]{1,0:T(8,128)(2,1)S(1)} collective-permute-done((bf16[112,256]{1,0:T(8,128)(2,1)S(1)}, bf16[112,256]{1,0:T(8,128)(2,1)S(1)}, u32[]{:S(2)}, u32[]{:S(2)}) %collective-permute-start.7) | collective-permute-done | bytes 57376 | tf_op jit(solution)/shard_map/ppermute | solution.py:483
  38.7 1.9 %collective-permute-done.8.refs_2_ = bf16[112,256]{1,0:T(8,128)(2,1)S(1)} collective-permute-done((bf16[112,256]{1,0:T(8,128)(2,1)S(1)}, bf16[112,256]{1,0:T(8,128)(2,1)S(1)}, u32[]{:S(2)}, u32[]{:S(2)}) %collective-permute-start.8) | collective-permute-done | bytes 57376 | tf_op jit(solution)/shard_map/ppermute | solution.py:483
  40.6 0.7 %unpack.1 = (f32[64,256]{1,0:T(8,128)}, f32[3,3,3,64]{3,2,1,0:T(4,128)}, f32[32,256]{1,0:T(8,128)}, f32[3,3,3,32]{3,2,1,0:T(4,128)}) custom-call(f32[112,256]{1,0:T(8,128)S(1)} %get-tuple-element.56.total_ref, bf16[112,256]{1,0:T(8,128)(2,1)S(1)} %collective-permute-done.6.refs_0_, bf16[112,256]{1,0:T(8,128)(2,1)S(1)} %collective-permute-done.7.refs_1_, ...), custom_call_target="tpu_custom_call" | custom-call | tf_op jit(solution)/shard_map/unpack/pallas_call | solution.py:612
  (3 shorter events, 0.1 us)
Async XLA Ops:
  8.2 8.6 %collective-permute-start = (bf16[2,4,32,256]{3,2,1,0:T(8,128)(2,1)S(1)}, bf16[2,4,32,256]{3,2,1,0:T(8,128)(2,1)S(1)}, u32[]{:S(2)}, u32[]{:S(2)}) collective-permute-start(bf16[2,4,32,256]{3,2,1,0:T(8,128)(2,1)S(1)} %get-tuple-element.30), channel_id=1, source_target_pairs={{0,1},{1,0},{2,3},{3,2},{4,5},{5,4},{6,7},{7,6},{8,9},{9,8},{10,11... | collective-permute-start | bytes 393224 | tf_op jit(solution)/shard_map/ppermute | solution.py:559
  11.2 5.6 %collective-permute-start.1 = (bf16[2,4,32,256]{3,2,1,0:T(8,128)(2,1)S(1)}, bf16[2,4,32,256]{3,2,1,0:T(8,128)(2,1)S(1)}, u32[]{:S(2)}, u32[]{:S(2)}) collective-permute-start(bf16[2,4,32,256]{3,2,1,0:T(8,128)(2,1)S(1)} %get-tuple-element.31), channel_id=1, source_target_pairs={{0,8},{1,2},{2,1},{3,4},{4,3},{5,6},{6,5},{7,15},{8,0},{9,10},{10,... | collective-permute-start | bytes 393224 | tf_op jit(solution)/shard_map/ppermute | solution.py:560
  21.1 1.4 %collective-permute-start.2 = (bf16[2,112,256]{2,1,0:T(8,128)(2,1)S(1)}, bf16[2,112,256]{2,1,0:T(8,128)(2,1)S(1)}, u32[]{:S(2)}, u32[]{:S(2)}) collective-permute-start(bf16[2,112,256]{2,1,0:T(8,128)(2,1)S(1)} %get-tuple-element.49), channel_id=1, source_target_pairs={{0,8},{8,0},{16,24},{24,16},{1,9},{9,1},{17,25},{25,17},{2,10},{10... | collective-permute-start | bytes 344072 | tf_op jit(solution)/shard_map/ppermute | solution.py:461
  22.5 4.2 %collective-permute-start.3 = (bf16[1,112,256]{2,1,0:T(8,128)(2,1)S(1)}, bf16[1,112,256]{2,1,0:T(8,128)(2,1)S(1)}, u32[]{:S(2)}, u32[]{:S(2)}) collective-permute-start(bf16[1,112,256]{2,1,0:T(8,128)(2,1)S(1)} %get-tuple-element.57), channel_id=1, source_target_pairs={{0,16},{8,24},{16,0},{24,8},{1,17},{9,25},{17,1},{25,9},{2,18},{10... | collective-permute-start | bytes 172040 | tf_op jit(solution)/shard_map/ppermute | solution.py:466
  24.1 5.1 %collective-permute-start.4 = (bf16[1,112,256]{2,1,0:T(8,128)(2,1)S(1)}, bf16[1,112,256]{2,1,0:T(8,128)(2,1)S(1)}, u32[]{:S(2)}, u32[]{:S(2)}) collective-permute-start(bf16[1,112,256]{2,1,0:T(8,128)(2,1)S(1)} %get-tuple-element.57), channel_id=1, source_target_pairs={{0,17},{1,16},{2,19},{3,18},{4,21},{5,20},{6,23},{7,22},{8,25},{9,... | collective-permute-start | bytes 172040 | tf_op jit(solution)/shard_map/ppermute | solution.py:467
  26.5 4.2 %collective-permute-start.5 = (bf16[1,112,256]{2,1,0:T(8,128)(2,1)S(1)}, bf16[1,112,256]{2,1,0:T(8,128)(2,1)S(1)}, u32[]{:S(2)}, u32[]{:S(2)}) collective-permute-start(bf16[1,112,256]{2,1,0:T(8,128)(2,1)S(1)} %get-tuple-element.58), channel_id=1, source_target_pairs={{0,1},{1,0},{2,3},{3,2},{4,5},{5,4},{6,7},{7,6},{8,9},{9,8},{10,11... | collective-permute-start | bytes 172040 | tf_op jit(solution)/shard_map/ppermute | solution.py:468
  30.7 4.8 %collective-permute-start.6 = (bf16[112,256]{1,0:T(8,128)(2,1)S(1)}, bf16[112,256]{1,0:T(8,128)(2,1)S(1)}, u32[]{:S(2)}, u32[]{:S(2)}) collective-permute-start(bf16[112,256]{1,0:T(8,128)(2,1)S(1)} %get-tuple-element.55), channel_id=1, source_target_pairs={{0,2},{1,3},{2,0},{3,1},{4,6},{5,7},{6,4},{7,5},{8,10},{9,11},{10,... | collective-permute-start | bytes 172040 | tf_op jit(solution)/shard_map/ppermute | solution.py:483
  32.4 6.3 %collective-permute-start.7 = (bf16[112,256]{1,0:T(8,128)(2,1)S(1)}, bf16[112,256]{1,0:T(8,128)(2,1)S(1)}, u32[]{:S(2)}, u32[]{:S(2)}) collective-permute-start(bf16[112,256]{1,0:T(8,128)(2,1)S(1)} %get-tuple-element.55), channel_id=1, source_target_pairs={{0,4},{1,5},{2,6},{3,7},{4,0},{5,1},{6,2},{7,3},{8,12},{9,13},{10,... | collective-permute-start | bytes 172040 | tf_op jit(solution)/shard_map/ppermute | solution.py:483
  34.6 6.0 %collective-permute-start.8 = (bf16[112,256]{1,0:T(8,128)(2,1)S(1)}, bf16[112,256]{1,0:T(8,128)(2,1)S(1)}, u32[]{:S(2)}, u32[]{:S(2)}) collective-permute-start(bf16[112,256]{1,0:T(8,128)(2,1)S(1)} %get-tuple-element.55), channel_id=1, source_target_pairs={{0,6},{1,7},{2,4},{3,5},{4,2},{5,3},{6,0},{7,1},{8,14},{9,15},{10,... | collective-permute-start | bytes 172040 | tf_op jit(solution)/shard_map/ppermute | solution.py:483

commit v5 on v4

--- a/solution.py
+++ b/solution.py
@@ -104,21 +104,29 @@
 
 def second_feature(frames, gated, wc_ref, count, fine):
     _, groups, cells, _, cols, out = gated.shape
-    for cell in range(cells):
-        near, first_tap = near_frames(cell, frames)
-        for p in range(2):
-            for q in range(2):
-                field = jnp.concatenate(
+    size = groups * count * cols
+    for p in range(2):
+        for q in range(2):
+            fields = [
+                jnp.concatenate(
                     [
-                        gated[q + b, :, other, p + a : p + a + count].reshape(groups * count * cols, out)
-                        for other in near
+                        gated[q + b, :, cell, p + a : p + a + count].reshape(size, out)
                         for a in range(2)
                         for b in range(2)
                     ],
                     axis=1,
                 )
-                weight = wc_ref[p, q, first_tap : first_tap + len(near)].reshape(-1, out)
-                product = dot(field, weight).reshape(groups, count, cols, out)
+                for cell in range(cells)
+            ]
+            weights = [wc_ref[p, q, tap].reshape(4 * out, out) for tap in range(3)]
+            center = dot(jnp.concatenate(fields, axis=0), weights[1])
+            for cell in range(cells):
+                near, first_tap = near_frames(cell, frames)
+                product = center[cell * size : (cell + 1) * size]
+                for t, other in enumerate(near):
+                    if other != cell:
+                        product = product + dot(fields[other], weights[t + first_tap])
+                product = product.reshape(groups, count, cols, out)
                 for group in range(groups):
                     for row in range(count):
                         for block in range(out // 128):
@@ -151,31 +159,32 @@
     ]
 
 
-def kernel_gradient(frames, padded, back, total, first):
-    cells, rows, _, channels = back.shape
+def kernel_gradient(frames, blocks, start, finish):
+    channels = blocks[0][1].shape[-1]
     for lane in range(0, channels, 128):
         lanes = pl.ds(lane, 128)
-        sums = tuple(jnp.zeros((8, 128), F32) for _ in range(27))
-        for cell in range(cells):
-            near, first_tap = near_frames(cell, frames)
-
-            def body(row, sums, cell=cell, near=near, first_tap=first_tap, lanes=lanes):
-                sums = list(sums)
-                center = back[cell, row, :, lanes]
-                moved = (shift_cols(center, -1), center, shift_cols(center, 1))
-                for t, other in enumerate(near):
-                    for h in range(3):
-                        field = padded[other, row + h, :, lanes]
-                        for w in range(3):
-                            k = 9 * (t + first_tap) + 3 * h + w
-                            term = (moved[w] * field).reshape(-1, 8, 128)
-                            sums[k] = sums[k] + jnp.sum(term, axis=0)
-                return tuple(sums)
-
-            sums = lax.fori_loop(0, rows, body, sums)
+        sums = tuple(start(k, lanes) for k in range(27))
+        for padded, back in blocks:
+            cells, rows = back.shape[:2]
+            for cell in range(cells):
+                near, first_tap = near_frames(cell, frames)
+
+                def body(row, sums, padded=padded, back=back, cell=cell, near=near, first_tap=first_tap, lanes=lanes):
+                    sums = list(sums)
+                    center = back[cell, row, :, lanes]
+                    moved = (shift_cols(center, -1), center, shift_cols(center, 1))
+                    for t, other in enumerate(near):
+                        for h in range(3):
+                            field = padded[other, row + h, :, lanes]
+                            for w in range(3):
+                                k = 9 * (t + first_tap) + 3 * h + w
+                                term = (moved[w] * field).reshape(-1, 8, 128)
+                                sums[k] = sums[k] + jnp.sum(term, axis=0)
+                    return tuple(sums)
+
+                sums = lax.fori_loop(0, rows, body, sums) if rows > 1 else body(0, sums)
         for k in range(27):
-            value = jnp.sum(sums[k], axis=0, keepdims=True)
-            total[k : k + 1, lanes] = value if first else total[k : k + 1, lanes] + value
+            finish(k, lanes, sums[k])
 
 
 def level(student, target, adapter, scale, grad):
@@ -193,8 +202,8 @@
 
 def first_kernel(
     frames, x_hbm, w_hbm, w2_hbm, low_hbm, high_hbm, klow_hbm, khigh_hbm, plow_hbm, phigh_hbm,
-    inner, edge, first, second, wc, low_wide, high_wide, low_student, high_student, klow, khigh, plow, phigh,
-    x_ref, w_buf, w2, acc, low, high, sems,
+    inner, edge, first, second, w2, low_wide, high_wide, high_student, klow, khigh, plow, phigh,
+    x_ref, w_buf, acc, low, high, sems,
 ):
     cells, rows, cols, depth = x_ref.shape
     out = w_buf.shape[-1]
@@ -211,11 +220,10 @@
         copies.start(low_hbm, low),
         copies.start(klow_hbm, klow),
     ]
-    load_w2 = copies.start(w2_hbm, w2)
     for tap, _, _, _ in spans[1:]:
         for tap_h in (1, 0, 2):
             loads[tap, tap_h] = copies.start(w_hbm.at[tap, tap_h], w_buf.at[tap, tap_h])
-    late = [copies.start(plow_hbm, plow), copies.start(phigh_hbm, phigh)]
+    late = [copies.start(plow_hbm, plow), copies.start(phigh_hbm, phigh), copies.start(w2_hbm, w2)]
     for tap_w in range(3):
         acc[tap_w, :, 0:1] = jnp.zeros((cells, 1, cols, out), F32)
         acc[tap_w, :, rows + 1 : rows + 2] = jnp.zeros((cells, 1, cols, out), F32)
@@ -224,7 +232,6 @@
         widen(high, high_wide)
         + widen(low, low_wide)
         + depthwise(frames, high_wide.at[:, 3 : 2 * rows - 3], khigh, high_student)
-        + depthwise(frames, low_wide, klow, low_student)
     )
     load_x.wait()
     pending, share = [], 0
@@ -235,13 +242,7 @@
                 for copy in fields:
                     copy.wait()
                 pending = list(students)
-                share = -(-len(pending) // 6)
-            if number == min(1, len(spans) - 1) and tap_h == (1 if number else 2):
-                for step in pending:
-                    step()
-                load_w2.wait()
-                pending = phase_weights(w2, wc)
-                share = -(-len(pending) // (9 * max(1, len(spans) - 1)))
+                share = -(-len(pending) // (9 * len(spans) - 3))
             at = 2 - tap_h
             for tap_w in range(3):
                 weight = w_buf[tap, tap_h, tap_w]
@@ -292,9 +293,9 @@
 
 def second_kernel(
     frames, scale_low, scale_high,
-    feature, wc, low_wide, high_wide, low_student, high_student, plow, phigh,
-    mismatch_hbm, glow, ghigh, gklow, gkhigh,
-    mismatch, gated, fine, low_back, high_back, sems,
+    feature, w2, low_wide, high_wide, high_student, klow, khigh, plow, phigh,
+    mismatch_hbm, wc, border_student, glow, ghigh, gklow, gkhigh,
+    mismatch, gated, fine, low_student, low_back, high_back, sems,
 ):
     cells, count, cols, out = feature.shape
     rows = count + 2
@@ -308,12 +309,15 @@
             return 0
 
         lax.fori_loop(0, count, gate, 0)
+    for step in depthwise(frames, low_wide, klow, low_student) + phase_weights(w2, wc):
+        step()
     second_feature(frames, gated, wc, inner, fine)
+    for side, top in ((0, 0), (1, 2 * rows - 5)):
+        for step in depthwise(frames, high_wide.at[:, top : top + 5], khigh, border_student.at[side]):
+            step()
 
     glow[...] = jnp.zeros_like(glow)
     ghigh[...] = jnp.zeros_like(ghigh)
-    gklow[...] = jnp.zeros_like(gklow)
-    gkhigh[...] = jnp.zeros_like(gkhigh)
     for cell in range(cells):
         student = high_student[cell].reshape(-1, high_student.shape[-1])
         target = fine_target(fine.at[0, cell], slice(0, inner))
@@ -325,14 +329,18 @@
     target = feature[...].reshape(-1, out).astype(F32)
     _, back = level(student, target, plow[...], scale_low, glow)
     low_back[...] = back.reshape(low_back.shape)
-    kernel_gradient(frames, low_wide, low_back, gklow, True)
-    kernel_gradient(frames, high_wide.at[:, 3 : 2 * rows - 3], high_back, gkhigh, True)
+    for blocks, total in (([(low_wide, low_back)], gklow), ([(high_wide.at[:, 3 : 2 * rows - 3], high_back)], gkhigh)):
+
+        def keep(k, lanes, sums, total=total):
+            total[k, :, lanes] = sums
+
+        kernel_gradient(frames, blocks, lambda k, lanes: jnp.zeros((8, 128), F32), keep)
     store.wait()
 
 
 def third_kernel(
     frames, shards, tiles, scale_low, scale_high,
-    first, second, edge, inner, wc, glow_in, ghigh_in, gklow_in, gkhigh_in, low_wide, high_wide, klow, khigh, plow, phigh, mismatch_in,
+    first, second, edge, inner, wc, border_student, glow_in, ghigh_in, gklow_in, gkhigh_in, low_wide, high_wide, klow, khigh, plow, phigh, mismatch_in,
     mismatch_hbm, keep, send,
     glow, ghigh, gklow, gkhigh, mismatch,
     feature, gated, fine, low_pad, high_pad, low_student, high_student, low_back, high_back, shard_sums, sems,
@@ -345,8 +353,18 @@
     even = lax.rem(tile, 2) == 0
     outside = (tile == 0, tile == tiles - 1)
     copies = Copies(sems)
-    for total, part in ((glow, glow_in), (ghigh, ghigh_in), (gklow, gklow_in), (gkhigh, gkhigh_in)):
-        total[...] = part[...]
+    glow[...] = glow_in[...]
+    ghigh[...] = ghigh_in[...]
+    gklow[27:] = jnp.zeros_like(gklow[27:])
+    gkhigh[27:] = jnp.zeros_like(gkhigh[27:])
+
+    def border_gradient(padded, back, part, total):
+        def finish(k, lanes, sums):
+            total[k : k + 1, lanes] = jnp.sum(sums, axis=0, keepdims=True)
+
+        kernel_gradient(
+            frames, [(padded.at[side], back.at[side]) for side in range(2)], lambda k, lanes: part[k, :, lanes], finish
+        )
 
     def halo(side, cell, row):
         ours, other = first[cell, row].astype(F32), second[cell, row].astype(F32)
@@ -378,16 +396,18 @@
             high_pad[side, cell, at, 0:cols] = high_halo[:, 0:high_ch]
             high_pad[side, cell, at, cols:] = high_halo[:, high_ch : 2 * high_ch]
             high_pad[side, cell, pl.ds(1 - side, 5)] = high_wide[cell, pl.ds(side * (2 * rows - 5), 5)]
-        for step in depthwise(frames, high_pad.at[side], khigh, high_student.at[side]):
+        at = 3 * side
+        for step in depthwise(frames, high_pad.at[side, :, at : at + 3], khigh, high_student.at[side, :, at : at + 1]):
             step()
+        for cell in range(cells):
+            high_student[side, cell, 1 - side : 4 - side] = border_student[side, cell]
         for step in depthwise(frames, low_pad.at[side], klow, low_student.at[side]):
             step()
 
     student = low_student[...].reshape(-1, low_ch)
     _, back = level(student, feature[...].reshape(-1, out), plow[...], scale_low, glow)
     low_back[...] = back.reshape(low_back.shape)
-    for side in range(2):
-        kernel_gradient(frames, low_pad.at[side], low_back.at[side], gklow, False)
+    border_gradient(low_pad, low_back, gklow_in, gklow)
 
     student = high_student[...].reshape(-1, high_ch)
     target = jnp.concatenate(
@@ -400,8 +420,7 @@
         copies.start(mismatch.at[0], mismatch_hbm.at[:, pl.ds(0, 4)]),
         copies.start(mismatch.at[1], mismatch_hbm.at[:, pl.ds(2 * rows - 4, 4)]),
     ]
-    for side in range(2):
-        kernel_gradient(frames, high_pad.at[side], high_back.at[side], gkhigh, False)
+    border_gradient(high_pad, high_back, gkhigh_in, gkhigh)
 
     low_rows, high_rows = low_ch // shards, high_ch // shards
     shard_sums[...] = jnp.zeros_like(shard_sums)
@@ -463,9 +482,9 @@
         keep, send = split_shards(keep, 2)
         across = [(c * tiles + t, (c ^ 2) * tiles + (t ^ 1)) for c in range(clips) for t in range(tiles)]
         got = (
+            lax.ppermute(keep.astype(BF16), "space", pairs(tiles, 1)),
             lax.ppermute(send, "clip", pairs(clips, 2)),
             lax.ppermute(send, ("clip", "space"), across),
-            lax.ppermute(keep.astype(BF16), "space", pairs(tiles, 1)),
         )
         for part in got:
             keep = keep + part.astype(F32)
@@ -480,7 +499,7 @@
             total = total + part.astype(F32)
         bits = (tile_bit, 2 * tile_bit, 3 * tile_bit) if 2 * tile_bit < tiles else (tile_bit,)
         out = total.astype(BF16)
-        got = [lax.ppermute(out, "space", pairs(tiles, b)) for b in bits]
+        got = [lax.ppermute(out, "space", pairs(tiles, b)) for b in bits[::-1]]
         tile_bit *= 2 ** (2 if len(bits) > 1 else 1)
     return total, got
 
@@ -524,7 +543,7 @@
     edge_spec = ((2, cells, 2, cols, out), F32)
     wc_spec = ((2, 2, 3, 2, 2, out, out), BF16)
     weights = ((kernel_low.shape, F32), (kernel_high.shape, F32), (adapter_low.shape, BF16), (adapter_high.shape, BF16))
-    inner_feature, edge, first, second, wc, low_wide, high_wide, low_student, high_student, klow, khigh, plow, phigh = pl.pallas_call(
+    inner_feature, edge, first, second, w2, low_wide, high_wide, high_student, klow, khigh, plow, phigh = pl.pallas_call(
         functools.partial(first_kernel, frames),
         out_shape=tuple(
             vm(
@@ -532,20 +551,18 @@
                 edge_spec,
                 packet,
                 packet,
-                wc_spec,
+                (conv_second.shape, BF16),
                 (low.shape, F32),
                 (high.shape, F32),
-                ((cells, rows - 2, cols, low_ch), BF16),
                 ((cells, 2 * inner, 2 * cols, high_ch), BF16),
                 *weights,
             )
         ),
         in_specs=[HBM] * 9,
-        out_specs=(VMEM,) * 13,
+        out_specs=(VMEM,) * 12,
         scratch_shapes=vm(
             (x.shape, BF16),
             (conv_first.shape, BF16),
-            (conv_second.shape, BF16),
             ((3, cells, rows + 2, cols, out), F32),
             (low.shape, BF16),
             (high.shape, BF16),
@@ -559,16 +576,22 @@
     first_got = lax.ppermute(first, ("clip", "space"), swaps(clips, tiles, 0))
     second_got = lax.ppermute(second, ("clip", "space"), swaps(clips, tiles, 1))
 
-    grads = (((low_ch, out), F32), ((high_ch, out), F32), ((32, low_ch), F32), ((32, high_ch), F32))
-    mismatch, *sums = pl.pallas_call(
+    adapters = (((low_ch, out), F32), ((high_ch, out), F32))
+    partial_sums = (((27, 8, low_ch), F32), ((27, 8, high_ch), F32))
+    kernels = (((32, low_ch), F32), ((32, high_ch), F32))
+    mismatch, wc, border_student, *sums = pl.pallas_call(
         functools.partial(second_kernel, frames, *scales),
-        out_shape=(pltpu.HBM((cells, 2 * rows, 2 * cols, out), BF16), *vm(*grads)),
-        in_specs=[VMEM] * 8,
-        out_specs=(HBM,) + (VMEM,) * 4,
+        out_shape=(
+            pltpu.HBM((cells, 2 * rows, 2 * cols, out), BF16),
+            *vm(wc_spec, ((2, cells, 3, 2 * cols, high_ch), BF16), *adapters, *partial_sums),
+        ),
+        in_specs=[VMEM] * 9,
+        out_specs=(HBM,) + (VMEM,) * 6,
         scratch_shapes=vm(
             ((cells, 2 * inner, 2 * cols, out), BF16),
             ((3, 1, cells, rows - 2, cols, out), BF16),
             ((1, cells, inner, 2, out // 128, 2 * cols, 128), F32),
+            ((cells, rows - 2, cols, low_ch), BF16),
             ((cells, rows - 2, cols, low_ch), F32),
             ((cells, 2 * inner, 2 * cols, high_ch), F32),
         )
@@ -576,7 +599,7 @@
         compiler_params=pltpu.CompilerParams(vmem_limit_bytes=20 * MIB),
         cost_estimate=pl.CostEstimate(flops=5 * 10**9, bytes_accessed=20 * 10**6, transcendentals=0),
         name="inner_rows",
-    )(inner_feature, wc, low_wide, high_wide, low_student, high_student, plow, phigh)
+    )(inner_feature, w2, low_wide, high_wide, high_student, klow, khigh, plow, phigh)
 
     shard_rows = low_ch // clips + high_ch // clips + 16
     shard_rows += -shard_rows % 16
@@ -584,11 +607,12 @@
     mismatch, keep, send = pl.pallas_call(
         functools.partial(third_kernel, frames, clips, tiles, *scales),
         out_shape=(pltpu.HBM(mismatch.shape, BF16), *vm((shard, F32), (shard, BF16))),
-        in_specs=[VMEM] * 15 + [HBM],
+        in_specs=[VMEM] * 16 + [HBM],
         out_specs=(HBM, VMEM, VMEM),
-        input_output_aliases={15: 0},
+        input_output_aliases={16: 0},
         scratch_shapes=vm(
-            *grads,
+            *adapters,
+            *kernels,
             ((2, cells, 4, 2 * cols, out), BF16),
             ((2, cells, cols, out), F32),
             ((3, 2, cells, 4, cols, out), BF16),
@@ -605,7 +629,7 @@
         compiler_params=pltpu.CompilerParams(vmem_limit_bytes=20 * MIB),
         cost_estimate=pl.CostEstimate(flops=3 * 10**9, bytes_accessed=20 * 10**6, transcendentals=0),
         name="border_rows",
-    )(first_got, second_got, edge, inner_feature, wc, *sums, low_wide, high_wide, klow, khigh, plow, phigh, *in_hbm(mismatch))
+    )(first_got, second_got, edge, inner_feature, wc, border_student, *sums, low_wide, high_wide, klow, khigh, plow, phigh, *in_hbm(mismatch))
 
     total, got = sum_over_devices(keep, send, clips, tiles)
     low_rows, high_rows = low_ch // clips, high_ch // clips

time: 41.4 us -> 38.4 us (0.928)
  waiting for transfers between devices: 12.2 us -> 9.02 us
  starting transfers between devices: 11.6 us -> 12.2 us
    ppermute x1, waiting for transfers between devices: 0.17 us -> 1.95 us  [sum_over_devices(): lax.ppermute(send, 'clip', pairs(clips, 2))]
    ppermute x3, waiting for transfers between devices: 5.35 us -> 3.63 us  [sum_over_devices(): got = [lax.ppermute(out, 'space', pairs(tiles, b)) for b in bits[::-1]]]
    ppermute x1, starting transfers between devices: 2.42 us -> 3.81 us  [sum_over_devices(): lax.ppermute(send, ('clip', 'space'), across)]
    pallas_call x1, Pallas kernels: 4.09 us -> 5.28 us  [on_device(): pl.pallas_call(functools.partial(second_kernel, frames, *scales), out_sha...]
    ppermute x1, waiting for transfers between devices: 1.47 us -> 0.28 us  [on_device(): first_got = lax.ppermute(first, ('clip', 'space'), swaps(clips, tiles, 0))]
    ppermute x1, starting transfers between devices: 1.58 us -> 0.51 us  [sum_over_devices(): lax.ppermute(send, 'clip', pairs(clips, 2))]
    ppermute x1, waiting for transfers between devices: 1.53 us -> 0.51 us  [sum_over_devices(): lax.ppermute(keep.astype(BF16), 'space', pairs(tiles, 1))]
    pallas_call x1, Pallas kernels: 7.56 us -> 6.64 us  [on_device(): pl.pallas_call(functools.partial(first_kernel, frames), out_shape=tuple(v...]
  transfers between devices with their start and end apart: 9 -> 9, of which waited for: 8 -> 7; matrix products, arithmetic and copies ran while one was open for 0% -> 0% of each run, Pallas kernels for 10% -> 14%
where the time goes in v5:
time: 38.4 us; the launch traced here: 38.3 us
  Pallas kernels  16.3 us (42%)
  starting transfers between devices  12.2 us (32%)
  waiting for transfers between devices  9.02 us (23%)
  between operations  0.68 us (2%)
    pallas_call x1, Pallas kernels, on_device(): pl.pallas_call(functools.partial(first_kernel, frames), out_shape=tuple(v...  6.64 us
    pallas_call x1, Pallas kernels, on_device(): pl.pallas_call(functools.partial(second_kernel, frames, *scales), out_sha...  5.28 us
    ppermute x3, starting transfers between devices, sum_over_devices(): got = [lax.ppermute(out, 'space', pairs(tiles, b)) for b in bits[::-1]]  4.45 us
    ppermute x1, starting transfers between devices, sum_over_devices(): lax.ppermute(send, ('clip', 'space'), across)  3.81 us
    pallas_call x1, Pallas kernels, on_device(): pl.pallas_call(functools.partial(third_kernel, frames, clips, tiles, *sca...  3.65 us
    ppermute x3, waiting for transfers between devices, sum_over_devices(): got = [lax.ppermute(out, 'space', pairs(tiles, b)) for b in bits[::-1]]  3.63 us
    ppermute x1, starting transfers between devices, on_device(): first_got = lax.ppermute(first, ('clip', 'space'), swaps(clips, tiles, 0))  3 us
    ppermute x1, waiting for transfers between devices, sum_over_devices(): lax.ppermute(send, 'clip', pairs(clips, 2))  1.95 us
  transfers between devices with their start and end apart: 9, of which 7 were waited for; matrix products, arithmetic and copies ran while one was open for 0% of the time, Pallas kernels for 14%

profile of v5, /device:TPU:0, one launch (start us, length us, event | category | flops | bytes accessed | tf_op | source)
XLA Modules:
  0.0 38.3 jit_solution(2320049823707594707)
XLA Ops:
  0.6 6.6 %teacher_first.1 = (bf16[2,6,32,256]{3,2,1,0:T(8,128)(2,1)S(1)}, f32[2,2,2,32,256]{4,3,2,1,0:T(8,128)S(1)}, bf16[2,4,32,256]{3,2,1,0:T(8,128)(2,1)S(1)}, bf16[2,...) custom-call(bf16[2,8,32,512]{3,2,1,0:T(8,128)(2,1)} %bitcast.7, ...), custom_call_target="tpu_custom_call" | custom-call | flops 3000000000 | bytes 9000000 | tf_op jit(solution)/shard_map/teacher_first/pallas_call | solution.py:546
  7.3 3.0 %collective-permute-start = (bf16[2,4,32,256]{3,2,1,0:T(8,128)(2,1)S(1)}, bf16[2,4,32,256]{3,2,1,0:T(8,128)(2,1)S(1)}, u32[]{:S(2)}, u32[]{:S(2)}) collective-permute-start(bf16[2,4,32,256]{3,2,1,0:T(8,128)(2,1)S(1)} %get-tuple-element.31), channel_id=1, source_target_pairs={{0,1},{1,0},{2,3},{3,2},{4,5},{5,4},{6,7},{7,6},{8,9},{9,8},{10,11... | collective-permute-start | bytes 393224 | tf_op jit(solution)/shard_map/ppermute | solution.py:576
  10.3 0.0 collective-permute-start.1
  10.3 5.3 %inner_rows.1 = (bf16[2,16,64,256]{3,2,1,0:T(8,128)(2,1)}, bf16[2,2,3,2,2,256,256]{6,5,4,3,2,1,0:T(8,128)(2,1)S(1)}, bf16[2,2,3,64,128]{4,3,2,1,0:T(8,128)(2,1)S...) custom-call(bf16[2,6,32,256]{3,2,1,0:T(8,128)(2,1)S(1)} %get-tuple-e, ...), custom_call_target="tpu_custom_call" | custom-call | flops 5000000000 | bytes 20000000 | tf_op jit(solution)/shard_map/inner_rows/pallas_call | solution.py:582
  15.6 0.3 collective-permute-done.first
  15.9 0.0 collective-permute-done.1.second
  15.9 3.6 %border_rows.1 = (bf16[2,16,64,256]{3,2,1,0:T(8,128)(2,1)}, f32[2,112,256]{2,1,0:T(8,128)S(1)}, bf16[2,112,256]{2,1,0:T(8,128)(2,1)S(1)}) custom-call(bf16[2,4,32,256]{3,2,1,0:T(8,128)(2,1)S(1)} %collective-permute-done.first, bf16[2,4,32,256]{3,2,1,0:T(8,128)(2,1)S(1)} %collective-permute-done.1.second, ...), custom_call_target="tpu_custom_call", output_to_operand_aliasing={{0}: (16, {})} | custom-call | flops 3000000000 | bytes 20000000 | tf_op jit(solution)/shard_map/border_rows/pallas_call | solution.py:607
  19.5 0.3 collective-permute-start.2
  19.8 1.1 %collective-permute-done.2 = bf16[2,112,256]{2,1,0:T(8,128)(2,1)S(1)} collective-permute-done((bf16[2,112,256]{2,1,0:T(8,128)(2,1)S(1)}, bf16[2,112,256]{2,1,0:T(8,128)(2,1)S(1)}, u32[]{:S(2)}, u32[]{:S(2)}) %collective-permute-start.2) | collective-permute-done | bytes 114720 | tf_op jit(solution)/shard_map/ppermute | solution.py:480
  21.0 3.8 %collective-permute-start.5 = (bf16[1,112,256]{2,1,0:T(8,128)(2,1)S(1)}, bf16[1,112,256]{2,1,0:T(8,128)(2,1)S(1)}, u32[]{:S(2)}, u32[]{:S(2)}) collective-permute-start(bf16[1,112,256]{2,1,0:T(8,128)(2,1)S(1)} %get-tuple-element.60), channel_id=1, source_target_pairs={{0,17},{1,16},{2,19},{3,18},{4,21},{5,20},{6,23},{7,22},{8,25},{9,... | collective-permute-start | bytes 172040 | tf_op jit(solution)/shard_map/ppermute | solution.py:487
  24.8 0.5 %collective-permute-start.4 = (bf16[1,112,256]{2,1,0:T(8,128)(2,1)S(1)}, bf16[1,112,256]{2,1,0:T(8,128)(2,1)S(1)}, u32[]{:S(2)}, u32[]{:S(2)}) collective-permute-start(bf16[1,112,256]{2,1,0:T(8,128)(2,1)S(1)} %get-tuple-element.60), channel_id=1, source_target_pairs={{0,16},{8,24},{16,0},{24,8},{1,17},{9,25},{17,1},{25,9},{2,18},{10... | collective-permute-start | bytes 172040 | tf_op jit(solution)/shard_map/ppermute | solution.py:486
  25.3 0.1 collective-permute-start.3
  25.4 1.6 %collective-permute-done.5 = bf16[1,112,256]{2,1,0:T(8,128)(2,1)S(1)} collective-permute-done((bf16[1,112,256]{2,1,0:T(8,128)(2,1)S(1)}, bf16[1,112,256]{2,1,0:T(8,128)(2,1)S(1)}, u32[]{:S(2)}, u32[]{:S(2)}) %collective-permute-start.5) | collective-permute-done | bytes 57376 | tf_op jit(solution)/shard_map/ppermute | solution.py:487
  27.0 1.9 %collective-permute-done.4 = bf16[1,112,256]{2,1,0:T(8,128)(2,1)S(1)} collective-permute-done((bf16[1,112,256]{2,1,0:T(8,128)(2,1)S(1)}, bf16[1,112,256]{2,1,0:T(8,128)(2,1)S(1)}, u32[]{:S(2)}, u32[]{:S(2)}) %collective-permute-start.4) | collective-permute-done | bytes 57376 | tf_op jit(solution)/shard_map/ppermute | solution.py:486
  28.9 0.5 %collective-permute-done.3 = bf16[1,112,256]{2,1,0:T(8,128)(2,1)S(1)} collective-permute-done((bf16[1,112,256]{2,1,0:T(8,128)(2,1)S(1)}, bf16[1,112,256]{2,1,0:T(8,128)(2,1)S(1)}, u32[]{:S(2)}, u32[]{:S(2)}) %collective-permute-start.3) | collective-permute-done | bytes 57376 | tf_op jit(solution)/shard_map/ppermute | solution.py:485
  29.5 2.4 %collective-permute-start.6 = (bf16[112,256]{1,0:T(8,128)(2,1)S(1)}, bf16[112,256]{1,0:T(8,128)(2,1)S(1)}, u32[]{:S(2)}, u32[]{:S(2)}) collective-permute-start(bf16[112,256]{1,0:T(8,128)(2,1)S(1)} %get-tuple-element.57), channel_id=1, source_target_pairs={{0,6},{1,7},{2,4},{3,5},{4,2},{5,3},{6,0},{7,1},{8,14},{9,15},{10,... | collective-permute-start | bytes 172040 | tf_op jit(solution)/shard_map/ppermute | solution.py:502
  31.9 0.7 %collective-permute-start.7 = (bf16[112,256]{1,0:T(8,128)(2,1)S(1)}, bf16[112,256]{1,0:T(8,128)(2,1)S(1)}, u32[]{:S(2)}, u32[]{:S(2)}) collective-permute-start(bf16[112,256]{1,0:T(8,128)(2,1)S(1)} %get-tuple-element.57), channel_id=1, source_target_pairs={{0,4},{1,5},{2,6},{3,7},{4,0},{5,1},{6,2},{7,3},{8,12},{9,13},{10,... | collective-permute-start | bytes 172040 | tf_op jit(solution)/shard_map/ppermute | solution.py:502
  32.6 1.3 %collective-permute-start.8 = (bf16[112,256]{1,0:T(8,128)(2,1)S(1)}, bf16[112,256]{1,0:T(8,128)(2,1)S(1)}, u32[]{:S(2)}, u32[]{:S(2)}) collective-permute-start(bf16[112,256]{1,0:T(8,128)(2,1)S(1)} %get-tuple-element.57), channel_id=1, source_target_pairs={{0,2},{1,3},{2,0},{3,1},{4,6},{5,7},{6,4},{7,5},{8,10},{9,11},{10,... | collective-permute-start | bytes 172040 | tf_op jit(solution)/shard_map/ppermute | solution.py:502
  33.9 1.7 %collective-permute-done.6.refs_0_ = bf16[112,256]{1,0:T(8,128)(2,1)S(1)} collective-permute-done((bf16[112,256]{1,0:T(8,128)(2,1)S(1)}, bf16[112,256]{1,0:T(8,128)(2,1)S(1)}, u32[]{:S(2)}, u32[]{:S(2)}) %collective-permute-start.6) | collective-permute-done | bytes 57376 | tf_op jit(solution)/shard_map/ppermute | solution.py:502
  35.6 1.9 %collective-permute-done.7.refs_1_ = bf16[112,256]{1,0:T(8,128)(2,1)S(1)} collective-permute-done((bf16[112,256]{1,0:T(8,128)(2,1)S(1)}, bf16[112,256]{1,0:T(8,128)(2,1)S(1)}, u32[]{:S(2)}, u32[]{:S(2)}) %collective-permute-start.7) | collective-permute-done | bytes 57376 | tf_op jit(solution)/shard_map/ppermute | solution.py:502
  37.6 0.0 collective-permute-done.8.refs_2_
  37.6 0.7 %unpack.1 = (f32[64,256]{1,0:T(8,128)}, f32[3,3,3,64]{3,2,1,0:T(4,128)}, f32[32,256]{1,0:T(8,128)}, f32[3,3,3,32]{3,2,1,0:T(4,128)}) custom-call(f32[112,256]{1,0:T(8,128)S(1)} %get-tuple-element.58.total_ref, bf16[112,256]{1,0:T(8,128)(2,1)S(1)} %collective-permute-done.6.refs_0_, bf16[112,256]{1,0:T(8,128)(2,1)S(1)} %collective-permute-done.7.refs_1_, ...), custom_call_target="tpu_custom_call" | custom-call | tf_op jit(solution)/shard_map/unpack/pallas_call | solution.py:636
  (3 shorter events, 0.1 us)
Async XLA Ops:
  7.3 8.6 %collective-permute-start = (bf16[2,4,32,256]{3,2,1,0:T(8,128)(2,1)S(1)}, bf16[2,4,32,256]{3,2,1,0:T(8,128)(2,1)S(1)}, u32[]{:S(2)}, u32[]{:S(2)}) collective-permute-start(bf16[2,4,32,256]{3,2,1,0:T(8,128)(2,1)S(1)} %get-tuple-element.31), channel_id=1, source_target_pairs={{0,1},{1,0},{2,3},{3,2},{4,5},{5,4},{6,7},{7,6},{8,9},{9,8},{10,11... | collective-permute-start | bytes 393224 | tf_op jit(solution)/shard_map/ppermute | solution.py:576
  10.3 5.6 %collective-permute-start.1 = (bf16[2,4,32,256]{3,2,1,0:T(8,128)(2,1)S(1)}, bf16[2,4,32,256]{3,2,1,0:T(8,128)(2,1)S(1)}, u32[]{:S(2)}, u32[]{:S(2)}) collective-permute-start(bf16[2,4,32,256]{3,2,1,0:T(8,128)(2,1)S(1)} %get-tuple-element.32), channel_id=1, source_target_pairs={{0,8},{1,2},{2,1},{3,4},{4,3},{5,6},{6,5},{7,15},{8,0},{9,10},{10,... | collective-permute-start | bytes 393224 | tf_op jit(solution)/shard_map/ppermute | solution.py:577
  19.5 1.4 %collective-permute-start.2 = (bf16[2,112,256]{2,1,0:T(8,128)(2,1)S(1)}, bf16[2,112,256]{2,1,0:T(8,128)(2,1)S(1)}, u32[]{:S(2)}, u32[]{:S(2)}) collective-permute-start(bf16[2,112,256]{2,1,0:T(8,128)(2,1)S(1)} %get-tuple-element.51), channel_id=1, source_target_pairs={{0,8},{8,0},{16,24},{24,16},{1,9},{9,1},{17,25},{25,17},{2,10},{10... | collective-permute-start | bytes 344072 | tf_op jit(solution)/shard_map/ppermute | solution.py:480
  21.0 6.0 %collective-permute-start.5 = (bf16[1,112,256]{2,1,0:T(8,128)(2,1)S(1)}, bf16[1,112,256]{2,1,0:T(8,128)(2,1)S(1)}, u32[]{:S(2)}, u32[]{:S(2)}) collective-permute-start(bf16[1,112,256]{2,1,0:T(8,128)(2,1)S(1)} %get-tuple-element.60), channel_id=1, source_target_pairs={{0,17},{1,16},{2,19},{3,18},{4,21},{5,20},{6,23},{7,22},{8,25},{9,... | collective-permute-start | bytes 172040 | tf_op jit(solution)/shard_map/ppermute | solution.py:487
  24.8 4.2 %collective-permute-start.4 = (bf16[1,112,256]{2,1,0:T(8,128)(2,1)S(1)}, bf16[1,112,256]{2,1,0:T(8,128)(2,1)S(1)}, u32[]{:S(2)}, u32[]{:S(2)}) collective-permute-start(bf16[1,112,256]{2,1,0:T(8,128)(2,1)S(1)} %get-tuple-element.60), channel_id=1, source_target_pairs={{0,16},{8,24},{16,0},{24,8},{1,17},{9,25},{17,1},{25,9},{2,18},{10... | collective-permute-start | bytes 172040 | tf_op jit(solution)/shard_map/ppermute | solution.py:486
  25.3 4.2 %collective-permute-start.3 = (bf16[1,112,256]{2,1,0:T(8,128)(2,1)S(1)}, bf16[1,112,256]{2,1,0:T(8,128)(2,1)S(1)}, u32[]{:S(2)}, u32[]{:S(2)}) collective-permute-start(bf16[1,112,256]{2,1,0:T(8,128)(2,1)S(1)} %get-tuple-element.59), channel_id=1, source_target_pairs={{0,1},{1,0},{2,3},{3,2},{4,5},{5,4},{6,7},{7,6},{8,9},{9,8},{10,11... | collective-permute-start | bytes 172040 | tf_op jit(solution)/shard_map/ppermute | solution.py:485
  29.5 6.1 %collective-permute-start.6 = (bf16[112,256]{1,0:T(8,128)(2,1)S(1)}, bf16[112,256]{1,0:T(8,128)(2,1)S(1)}, u32[]{:S(2)}, u32[]{:S(2)}) collective-permute-start(bf16[112,256]{1,0:T(8,128)(2,1)S(1)} %get-tuple-element.57), channel_id=1, source_target_pairs={{0,6},{1,7},{2,4},{3,5},{4,2},{5,3},{6,0},{7,1},{8,14},{9,15},{10,... | collective-permute-start | bytes 172040 | tf_op jit(solution)/shard_map/ppermute | solution.py:502
  31.9 5.7 %collective-permute-start.7 = (bf16[112,256]{1,0:T(8,128)(2,1)S(1)}, bf16[112,256]{1,0:T(8,128)(2,1)S(1)}, u32[]{:S(2)}, u32[]{:S(2)}) collective-permute-start(bf16[112,256]{1,0:T(8,128)(2,1)S(1)} %get-tuple-element.57), channel_id=1, source_target_pairs={{0,4},{1,5},{2,6},{3,7},{4,0},{5,1},{6,2},{7,3},{8,12},{9,13},{10,... | collective-permute-start | bytes 172040 | tf_op jit(solution)/shard_map/ppermute | solution.py:502
  32.6 5.0 %collective-permute-start.8 = (bf16[112,256]{1,0:T(8,128)(2,1)S(1)}, bf16[112,256]{1,0:T(8,128)(2,1)S(1)}, u32[]{:S(2)}, u32[]{:S(2)}) collective-permute-start(bf16[112,256]{1,0:T(8,128)(2,1)S(1)} %get-tuple-element.57), channel_id=1, source_target_pairs={{0,2},{1,3},{2,0},{3,1},{4,6},{5,7},{6,4},{7,5},{8,10},{9,11},{10,... | collective-permute-start | bytes 172040 | tf_op jit(solution)/shard_map/ppermute | solution.py:502

commit v6 on v5

--- a/solution.py
+++ b/solution.py
@@ -409,13 +409,12 @@
     low_back[...] = back.reshape(low_back.shape)
     border_gradient(low_pad, low_back, gklow_in, gklow)
 
-    student = high_student[...].reshape(-1, high_ch)
-    target = jnp.concatenate(
-        [fine_target(fine.at[side, cell], slice(0, 2)) for side in range(2) for cell in range(cells)], axis=0
-    )
-    value, back = level(student, target, phigh[...], scale_high, ghigh)
-    mismatch[...] = value.astype(BF16).reshape(mismatch.shape)
-    high_back[...] = back.reshape(high_back.shape)
+    for side in range(2):
+        student = high_student[side].reshape(-1, high_ch)
+        target = jnp.concatenate([fine_target(fine.at[side, cell], slice(0, 2)) for cell in range(cells)], axis=0)
+        value, back = level(student, target, phigh[...], scale_high, ghigh)
+        mismatch[side] = value.astype(BF16).reshape(mismatch.shape[1:])
+        high_back[side] = back.reshape(high_back.shape[1:])
     stores = [
         copies.start(mismatch.at[0], mismatch_hbm.at[:, pl.ds(0, 4)]),
         copies.start(mismatch.at[1], mismatch_hbm.at[:, pl.ds(2 * rows - 4, 4)]),

time: 38.4 us -> 38.1 us (level)
  no operation moved by 1% of the time
where the time goes in v6:
time: 38.1 us; the launch traced here: 38 us
  Pallas kernels  16 us (42%)
  starting transfers between devices  12.2 us (32%)
  waiting for transfers between devices  9.02 us (24%)
  between operations  0.68 us (2%)
    pallas_call x1, Pallas kernels, on_device(): pl.pallas_call(functools.partial(first_kernel, frames), out_shape=tuple(v...  6.64 us
    pallas_call x1, Pallas kernels, on_device(): pl.pallas_call(functools.partial(second_kernel, frames, *scales), out_sha...  5.28 us
    ppermute x3, starting transfers between devices, sum_over_devices(): got = [lax.ppermute(out, 'space', pairs(tiles, b)) for b in bits[::-1]]  4.45 us
    ppermute x1, starting transfers between devices, sum_over_devices(): lax.ppermute(send, ('clip', 'space'), across)  3.81 us
    ppermute x3, waiting for transfers between devices, sum_over_devices(): got = [lax.ppermute(out, 'space', pairs(tiles, b)) for b in bits[::-1]]  3.63 us
    pallas_call x1, Pallas kernels, on_device(): pl.pallas_call(functools.partial(third_kernel, frames, clips, tiles, *sca...  3.35 us
    ppermute x1, starting transfers between devices, on_device(): first_got = lax.ppermute(first, ('clip', 'space'), swaps(clips, tiles, 0))  3 us
    ppermute x1, waiting for transfers between devices, sum_over_devices(): lax.ppermute(send, 'clip', pairs(clips, 2))  1.95 us
  transfers between devices with their start and end apart: 9, of which 7 were waited for; matrix products, arithmetic and copies ran while one was open for 0% of the time, Pallas kernels for 14%

profile of v6, /device:TPU:0, one launch (start us, length us, event | category | flops | bytes accessed | tf_op | source)
XLA Modules:
  0.0 38.0 jit_solution(480257048734087530)
XLA Ops:
  0.6 6.6 %teacher_first.1 = (bf16[2,6,32,256]{3,2,1,0:T(8,128)(2,1)S(1)}, f32[2,2,2,32,256]{4,3,2,1,0:T(8,128)S(1)}, bf16[2,4,32,256]{3,2,1,0:T(8,128)(2,1)S(1)}, bf16[2,...) custom-call(bf16[2,8,32,512]{3,2,1,0:T(8,128)(2,1)} %bitcast.7, ...), custom_call_target="tpu_custom_call" | custom-call | flops 3000000000 | bytes 9000000 | tf_op jit(solution)/shard_map/teacher_first/pallas_call | solution.py:545
  7.3 3.0 %collective-permute-start = (bf16[2,4,32,256]{3,2,1,0:T(8,128)(2,1)S(1)}, bf16[2,4,32,256]{3,2,1,0:T(8,128)(2,1)S(1)}, u32[]{:S(2)}, u32[]{:S(2)}) collective-permute-start(bf16[2,4,32,256]{3,2,1,0:T(8,128)(2,1)S(1)} %get-tuple-element.31), channel_id=1, source_target_pairs={{0,1},{1,0},{2,3},{3,2},{4,5},{5,4},{6,7},{7,6},{8,9},{9,8},{10,11... | collective-permute-start | bytes 393224 | tf_op jit(solution)/shard_map/ppermute | solution.py:575
  10.3 0.0 collective-permute-start.1
  10.3 5.3 %inner_rows.1 = (bf16[2,16,64,256]{3,2,1,0:T(8,128)(2,1)}, bf16[2,2,3,2,2,256,256]{6,5,4,3,2,1,0:T(8,128)(2,1)S(1)}, bf16[2,2,3,64,128]{4,3,2,1,0:T(8,128)(2,1)S...) custom-call(bf16[2,6,32,256]{3,2,1,0:T(8,128)(2,1)S(1)} %get-tuple-e, ...), custom_call_target="tpu_custom_call" | custom-call | flops 5000000000 | bytes 20000000 | tf_op jit(solution)/shard_map/inner_rows/pallas_call | solution.py:581
  15.6 0.3 collective-permute-done.first
  15.9 0.0 collective-permute-done.1.second
  15.9 3.3 %border_rows.1 = (bf16[2,16,64,256]{3,2,1,0:T(8,128)(2,1)}, f32[2,112,256]{2,1,0:T(8,128)S(1)}, bf16[2,112,256]{2,1,0:T(8,128)(2,1)S(1)}) custom-call(bf16[2,4,32,256]{3,2,1,0:T(8,128)(2,1)S(1)} %collective-permute-done.first, bf16[2,4,32,256]{3,2,1,0:T(8,128)(2,1)S(1)} %collective-permute-done.1.second, ...), custom_call_target="tpu_custom_call", output_to_operand_aliasing={{0}: (16, {})} | custom-call | flops 3000000000 | bytes 20000000 | tf_op jit(solution)/shard_map/border_rows/pallas_call | solution.py:606
  19.2 0.3 collective-permute-start.2
  19.5 1.1 %collective-permute-done.2 = bf16[2,112,256]{2,1,0:T(8,128)(2,1)S(1)} collective-permute-done((bf16[2,112,256]{2,1,0:T(8,128)(2,1)S(1)}, bf16[2,112,256]{2,1,0:T(8,128)(2,1)S(1)}, u32[]{:S(2)}, u32[]{:S(2)}) %collective-permute-start.2) | collective-permute-done | bytes 114720 | tf_op jit(solution)/shard_map/ppermute | solution.py:479
  20.7 3.8 %collective-permute-start.5 = (bf16[1,112,256]{2,1,0:T(8,128)(2,1)S(1)}, bf16[1,112,256]{2,1,0:T(8,128)(2,1)S(1)}, u32[]{:S(2)}, u32[]{:S(2)}) collective-permute-start(bf16[1,112,256]{2,1,0:T(8,128)(2,1)S(1)} %get-tuple-element.60), channel_id=1, source_target_pairs={{0,17},{1,16},{2,19},{3,18},{4,21},{5,20},{6,23},{7,22},{8,25},{9,... | collective-permute-start | bytes 172040 | tf_op jit(solution)/shard_map/ppermute | solution.py:486
  24.5 0.5 %collective-permute-start.4 = (bf16[1,112,256]{2,1,0:T(8,128)(2,1)S(1)}, bf16[1,112,256]{2,1,0:T(8,128)(2,1)S(1)}, u32[]{:S(2)}, u32[]{:S(2)}) collective-permute-start(bf16[1,112,256]{2,1,0:T(8,128)(2,1)S(1)} %get-tuple-element.60), channel_id=1, source_target_pairs={{0,16},{8,24},{16,0},{24,8},{1,17},{9,25},{17,1},{25,9},{2,18},{10... | collective-permute-start | bytes 172040 | tf_op jit(solution)/shard_map/ppermute | solution.py:485
  25.0 0.1 collective-permute-start.3
  25.1 1.6 %collective-permute-done.5 = bf16[1,112,256]{2,1,0:T(8,128)(2,1)S(1)} collective-permute-done((bf16[1,112,256]{2,1,0:T(8,128)(2,1)S(1)}, bf16[1,112,256]{2,1,0:T(8,128)(2,1)S(1)}, u32[]{:S(2)}, u32[]{:S(2)}) %collective-permute-start.5) | collective-permute-done | bytes 57376 | tf_op jit(solution)/shard_map/ppermute | solution.py:486
  26.7 1.9 %collective-permute-done.4 = bf16[1,112,256]{2,1,0:T(8,128)(2,1)S(1)} collective-permute-done((bf16[1,112,256]{2,1,0:T(8,128)(2,1)S(1)}, bf16[1,112,256]{2,1,0:T(8,128)(2,1)S(1)}, u32[]{:S(2)}, u32[]{:S(2)}) %collective-permute-start.4) | collective-permute-done | bytes 57376 | tf_op jit(solution)/shard_map/ppermute | solution.py:485
  28.6 0.5 %collective-permute-done.3 = bf16[1,112,256]{2,1,0:T(8,128)(2,1)S(1)} collective-permute-done((bf16[1,112,256]{2,1,0:T(8,128)(2,1)S(1)}, bf16[1,112,256]{2,1,0:T(8,128)(2,1)S(1)}, u32[]{:S(2)}, u32[]{:S(2)}) %collective-permute-start.3) | collective-permute-done | bytes 57376 | tf_op jit(solution)/shard_map/ppermute | solution.py:484
  29.2 2.4 %collective-permute-start.6 = (bf16[112,256]{1,0:T(8,128)(2,1)S(1)}, bf16[112,256]{1,0:T(8,128)(2,1)S(1)}, u32[]{:S(2)}, u32[]{:S(2)}) collective-permute-start(bf16[112,256]{1,0:T(8,128)(2,1)S(1)} %get-tuple-element.57), channel_id=1, source_target_pairs={{0,6},{1,7},{2,4},{3,5},{4,2},{5,3},{6,0},{7,1},{8,14},{9,15},{10,... | collective-permute-start | bytes 172040 | tf_op jit(solution)/shard_map/ppermute | solution.py:501
  31.6 0.7 %collective-permute-start.7 = (bf16[112,256]{1,0:T(8,128)(2,1)S(1)}, bf16[112,256]{1,0:T(8,128)(2,1)S(1)}, u32[]{:S(2)}, u32[]{:S(2)}) collective-permute-start(bf16[112,256]{1,0:T(8,128)(2,1)S(1)} %get-tuple-element.57), channel_id=1, source_target_pairs={{0,4},{1,5},{2,6},{3,7},{4,0},{5,1},{6,2},{7,3},{8,12},{9,13},{10,... | collective-permute-start | bytes 172040 | tf_op jit(solution)/shard_map/ppermute | solution.py:501
  32.3 1.3 %collective-permute-start.8 = (bf16[112,256]{1,0:T(8,128)(2,1)S(1)}, bf16[112,256]{1,0:T(8,128)(2,1)S(1)}, u32[]{:S(2)}, u32[]{:S(2)}) collective-permute-start(bf16[112,256]{1,0:T(8,128)(2,1)S(1)} %get-tuple-element.57), channel_id=1, source_target_pairs={{0,2},{1,3},{2,0},{3,1},{4,6},{5,7},{6,4},{7,5},{8,10},{9,11},{10,... | collective-permute-start | bytes 172040 | tf_op jit(solution)/shard_map/ppermute | solution.py:501
  33.6 1.7 %collective-permute-done.6.refs_0_ = bf16[112,256]{1,0:T(8,128)(2,1)S(1)} collective-permute-done((bf16[112,256]{1,0:T(8,128)(2,1)S(1)}, bf16[112,256]{1,0:T(8,128)(2,1)S(1)}, u32[]{:S(2)}, u32[]{:S(2)}) %collective-permute-start.6) | collective-permute-done | bytes 57376 | tf_op jit(solution)/shard_map/ppermute | solution.py:501
  35.3 1.9 %collective-permute-done.7.refs_1_ = bf16[112,256]{1,0:T(8,128)(2,1)S(1)} collective-permute-done((bf16[112,256]{1,0:T(8,128)(2,1)S(1)}, bf16[112,256]{1,0:T(8,128)(2,1)S(1)}, u32[]{:S(2)}, u32[]{:S(2)}) %collective-permute-start.7) | collective-permute-done | bytes 57376 | tf_op jit(solution)/shard_map/ppermute | solution.py:501
  37.3 0.0 collective-permute-done.8.refs_2_
  37.3 0.7 %unpack.1 = (f32[64,256]{1,0:T(8,128)}, f32[3,3,3,64]{3,2,1,0:T(4,128)}, f32[32,256]{1,0:T(8,128)}, f32[3,3,3,32]{3,2,1,0:T(4,128)}) custom-call(f32[112,256]{1,0:T(8,128)S(1)} %get-tuple-element.58.total_ref, bf16[112,256]{1,0:T(8,128)(2,1)S(1)} %collective-permute-done.6.refs_0_, bf16[112,256]{1,0:T(8,128)(2,1)S(1)} %collective-permute-done.7.refs_1_, ...), custom_call_target="tpu_custom_call" | custom-call | tf_op jit(solution)/shard_map/unpack/pallas_call | solution.py:635
  (3 shorter events, 0.1 us)
Async XLA Ops:
  7.3 8.6 %collective-permute-start = (bf16[2,4,32,256]{3,2,1,0:T(8,128)(2,1)S(1)}, bf16[2,4,32,256]{3,2,1,0:T(8,128)(2,1)S(1)}, u32[]{:S(2)}, u32[]{:S(2)}) collective-permute-start(bf16[2,4,32,256]{3,2,1,0:T(8,128)(2,1)S(1)} %get-tuple-element.31), channel_id=1, source_target_pairs={{0,1},{1,0},{2,3},{3,2},{4,5},{5,4},{6,7},{7,6},{8,9},{9,8},{10,11... | collective-permute-start | bytes 393224 | tf_op jit(solution)/shard_map/ppermute | solution.py:575
  10.3 5.6 %collective-permute-start.1 = (bf16[2,4,32,256]{3,2,1,0:T(8,128)(2,1)S(1)}, bf16[2,4,32,256]{3,2,1,0:T(8,128)(2,1)S(1)}, u32[]{:S(2)}, u32[]{:S(2)}) collective-permute-start(bf16[2,4,32,256]{3,2,1,0:T(8,128)(2,1)S(1)} %get-tuple-element.32), channel_id=1, source_target_pairs={{0,8},{1,2},{2,1},{3,4},{4,3},{5,6},{6,5},{7,15},{8,0},{9,10},{10,... | collective-permute-start | bytes 393224 | tf_op jit(solution)/shard_map/ppermute | solution.py:576
  19.2 1.4 %collective-permute-start.2 = (bf16[2,112,256]{2,1,0:T(8,128)(2,1)S(1)}, bf16[2,112,256]{2,1,0:T(8,128)(2,1)S(1)}, u32[]{:S(2)}, u32[]{:S(2)}) collective-permute-start(bf16[2,112,256]{2,1,0:T(8,128)(2,1)S(1)} %get-tuple-element.51), channel_id=1, source_target_pairs={{0,8},{8,0},{16,24},{24,16},{1,9},{9,1},{17,25},{25,17},{2,10},{10... | collective-permute-start | bytes 344072 | tf_op jit(solution)/shard_map/ppermute | solution.py:479
  20.7 6.0 %collective-permute-start.5 = (bf16[1,112,256]{2,1,0:T(8,128)(2,1)S(1)}, bf16[1,112,256]{2,1,0:T(8,128)(2,1)S(1)}, u32[]{:S(2)}, u32[]{:S(2)}) collective-permute-start(bf16[1,112,256]{2,1,0:T(8,128)(2,1)S(1)} %get-tuple-element.60), channel_id=1, source_target_pairs={{0,17},{1,16},{2,19},{3,18},{4,21},{5,20},{6,23},{7,22},{8,25},{9,... | collective-permute-start | bytes 172040 | tf_op jit(solution)/shard_map/ppermute | solution.py:486
  24.5 4.2 %collective-permute-start.4 = (bf16[1,112,256]{2,1,0:T(8,128)(2,1)S(1)}, bf16[1,112,256]{2,1,0:T(8,128)(2,1)S(1)}, u32[]{:S(2)}, u32[]{:S(2)}) collective-permute-start(bf16[1,112,256]{2,1,0:T(8,128)(2,1)S(1)} %get-tuple-element.60), channel_id=1, source_target_pairs={{0,16},{8,24},{16,0},{24,8},{1,17},{9,25},{17,1},{25,9},{2,18},{10... | collective-permute-start | bytes 172040 | tf_op jit(solution)/shard_map/ppermute | solution.py:485
  25.0 4.2 %collective-permute-start.3 = (bf16[1,112,256]{2,1,0:T(8,128)(2,1)S(1)}, bf16[1,112,256]{2,1,0:T(8,128)(2,1)S(1)}, u32[]{:S(2)}, u32[]{:S(2)}) collective-permute-start(bf16[1,112,256]{2,1,0:T(8,128)(2,1)S(1)} %get-tuple-element.59), channel_id=1, source_target_pairs={{0,1},{1,0},{2,3},{3,2},{4,5},{5,4},{6,7},{7,6},{8,9},{9,8},{10,11... | collective-permute-start | bytes 172040 | tf_op jit(solution)/shard_map/ppermute | solution.py:484
  29.2 6.1 %collective-permute-start.6 = (bf16[112,256]{1,0:T(8,128)(2,1)S(1)}, bf16[112,256]{1,0:T(8,128)(2,1)S(1)}, u32[]{:S(2)}, u32[]{:S(2)}) collective-permute-start(bf16[112,256]{1,0:T(8,128)(2,1)S(1)} %get-tuple-element.57), channel_id=1, source_target_pairs={{0,6},{1,7},{2,4},{3,5},{4,2},{5,3},{6,0},{7,1},{8,14},{9,15},{10,... | collective-permute-start | bytes 172040 | tf_op jit(solution)/shard_map/ppermute | solution.py:501
  31.6 5.7 %collective-permute-start.7 = (bf16[112,256]{1,0:T(8,128)(2,1)S(1)}, bf16[112,256]{1,0:T(8,128)(2,1)S(1)}, u32[]{:S(2)}, u32[]{:S(2)}) collective-permute-start(bf16[112,256]{1,0:T(8,128)(2,1)S(1)} %get-tuple-element.57), channel_id=1, source_target_pairs={{0,4},{1,5},{2,6},{3,7},{4,0},{5,1},{6,2},{7,3},{8,12},{9,13},{10,... | collective-permute-start | bytes 172040 | tf_op jit(solution)/shard_map/ppermute | solution.py:501
  32.3 5.0 %collective-permute-start.8 = (bf16[112,256]{1,0:T(8,128)(2,1)S(1)}, bf16[112,256]{1,0:T(8,128)(2,1)S(1)}, u32[]{:S(2)}, u32[]{:S(2)}) collective-permute-start(bf16[112,256]{1,0:T(8,128)(2,1)S(1)} %get-tuple-element.57), channel_id=1, source_target_pairs={{0,2},{1,3},{2,0},{3,1},{4,6},{5,7},{6,4},{7,5},{8,10},{9,11},{10,... | collective-permute-start | bytes 172040 | tf_op jit(solution)/shard_map/ppermute | solution.py:501

commit v7 on v6

--- a/solution.py
+++ b/solution.py
@@ -294,8 +294,8 @@
 def second_kernel(
     frames, scale_low, scale_high,
     feature, w2, low_wide, high_wide, high_student, klow, khigh, plow, phigh,
-    mismatch_hbm, wc, border_student, glow, ghigh, gklow, gkhigh,
-    mismatch, gated, fine, low_student, low_back, high_back, sems,
+    mismatch_hbm, gated, wc, border_student, glow, ghigh, gklow, gkhigh,
+    mismatch, fine, low_student, low_back, high_back, sems,
 ):
     cells, count, cols, out = feature.shape
     rows = count + 2
@@ -347,7 +347,7 @@
 ):
     del mismatch_in
     _, cells, _, cols, out = edge.shape
-    rows = inner.shape[1] + 2
+    rows = inner.shape[3] + 2
     low_ch, high_ch = low_wide.shape[-1], high_wide.shape[-1]
     mine, tile = lax.axis_index("clip"), lax.axis_index("space")
     even = lax.rem(tile, 2) == 0
@@ -381,8 +381,8 @@
                     feature[side, cell] = whole
                 for j, value in enumerate(gate_rows(whole)):
                     gated[j, side, cell, 2 * side + k] = value
-                for j, value in enumerate(gate_rows(inner[cell, side * (rows - 4) + k].astype(F32))):
-                    gated[j, side, cell, 2 - 2 * side + k] = value
+                for j in range(3):
+                    gated[j, side, cell, 2 - 2 * side + k] = inner[j, 0, cell, side * (rows - 4) + k]
 
     second_feature(frames, gated, wc, 2, fine)
 
@@ -578,17 +578,16 @@
     adapters = (((low_ch, out), F32), ((high_ch, out), F32))
     partial_sums = (((27, 8, low_ch), F32), ((27, 8, high_ch), F32))
     kernels = (((32, low_ch), F32), ((32, high_ch), F32))
-    mismatch, wc, border_student, *sums = pl.pallas_call(
+    mismatch, inner_gated, wc, border_student, *sums = pl.pallas_call(
         functools.partial(second_kernel, frames, *scales),
         out_shape=(
             pltpu.HBM((cells, 2 * rows, 2 * cols, out), BF16),
-            *vm(wc_spec, ((2, cells, 3, 2 * cols, high_ch), BF16), *adapters, *partial_sums),
+            *vm(((3, 1, cells, rows - 2, cols, out), BF16), wc_spec, ((2, cells, 3, 2 * cols, high_ch), BF16), *adapters, *partial_sums),
         ),
         in_specs=[VMEM] * 9,
-        out_specs=(HBM,) + (VMEM,) * 6,
+        out_specs=(HBM,) + (VMEM,) * 7,
         scratch_shapes=vm(
             ((cells, 2 * inner, 2 * cols, out), BF16),
-            ((3, 1, cells, rows - 2, cols, out), BF16),
             ((1, cells, inner, 2, out // 128, 2 * cols, 128), F32),
             ((cells, rows - 2, cols, low_ch), BF16),
             ((cells, rows - 2, cols, low_ch), F32),
@@ -628,7 +627,7 @@
         compiler_params=pltpu.CompilerParams(vmem_limit_bytes=20 * MIB),
         cost_estimate=pl.CostEstimate(flops=3 * 10**9, bytes_accessed=20 * 10**6, transcendentals=0),
         name="border_rows",
-    )(first_got, second_got, edge, inner_feature, wc, border_student, *sums, low_wide, high_wide, klow, khigh, plow, phigh, *in_hbm(mismatch))
+    )(first_got, second_got, edge, inner_gated, wc, border_student, *sums, low_wide, high_wide, klow, khigh, plow, phigh, *in_hbm(mismatch))
 
     total, got = sum_over_devices(keep, send, clips, tiles)
     low_rows, high_rows = low_ch // clips, high_ch // clips

time: 38.1 us -> 38.1 us (level)
  no operation moved by 1% of the time
where the time goes in v7:
time: 38.1 us; the launch traced here: 38 us
  Pallas kernels  16 us (42%)
  starting transfers between devices  12.3 us (32%)
  waiting for transfers between devices  8.94 us (23%)
  between operations  0.68 us (2%)
    pallas_call x1, Pallas kernels, on_device(): pl.pallas_call(functools.partial(first_kernel, frames), out_shape=tuple(v...  6.65 us
    pallas_call x1, Pallas kernels, on_device(): pl.pallas_call(functools.partial(second_kernel, frames, *scales), out_sha...  5.3 us
    ppermute x3, starting transfers between devices, sum_over_devices(): got = [lax.ppermute(out, 'space', pairs(tiles, b)) for b in bits[::-1]]  4.45 us
    ppermute x1, starting transfers between devices, sum_over_devices(): lax.ppermute(send, ('clip', 'space'), across)  3.83 us
    ppermute x3, waiting for transfers between devices, sum_over_devices(): got = [lax.ppermute(out, 'space', pairs(tiles, b)) for b in bits[::-1]]  3.61 us
    pallas_call x1, Pallas kernels, on_device(): pl.pallas_call(functools.partial(third_kernel, frames, clips, tiles, *sca...  3.33 us
    ppermute x1, starting transfers between devices, on_device(): first_got = lax.ppermute(first, ('clip', 'space'), swaps(clips, tiles, 0))  3.01 us
    ppermute x1, waiting for transfers between devices, sum_over_devices(): lax.ppermute(send, 'clip', pairs(clips, 2))  1.95 us
  transfers between devices with their start and end apart: 9, of which 7 were waited for; matrix products, arithmetic and copies ran while one was open for 0% of the time, Pallas kernels for 14%

profile of v7, /device:TPU:0, one launch (start us, length us, event | category | flops | bytes accessed | tf_op | source)
XLA Modules:
  0.0 38.0 jit_solution(621449044735775298)
XLA Ops:
  0.6 6.6 %teacher_first.1 = (bf16[2,6,32,256]{3,2,1,0:T(8,128)(2,1)S(1)}, f32[2,2,2,32,256]{4,3,2,1,0:T(8,128)S(1)}, bf16[2,4,32,256]{3,2,1,0:T(8,128)(2,1)S(1)}, bf16[2,...) custom-call(bf16[2,8,32,512]{3,2,1,0:T(8,128)(2,1)} %bitcast.8, ...), custom_call_target="tpu_custom_call" | custom-call | flops 3000000000 | bytes 9000000 | tf_op jit(solution)/shard_map/teacher_first/pallas_call | solution.py:545
  7.3 3.0 %collective-permute-start = (bf16[2,4,32,256]{3,2,1,0:T(8,128)(2,1)S(1)}, bf16[2,4,32,256]{3,2,1,0:T(8,128)(2,1)S(1)}, u32[]{:S(2)}, u32[]{:S(2)}) collective-permute-start(bf16[2,4,32,256]{3,2,1,0:T(8,128)(2,1)S(1)} %get-tuple-element.32), channel_id=1, source_target_pairs={{0,1},{1,0},{2,3},{3,2},{4,5},{5,4},{6,7},{7,6},{8,9},{9,8},{10,11... | collective-permute-start | bytes 393224 | tf_op jit(solution)/shard_map/ppermute | solution.py:575
  10.3 0.0 collective-permute-start.1
  10.3 5.3 %inner_rows.1 = (bf16[2,16,64,256]{3,2,1,0:T(8,128)(2,1)}, bf16[3,1,2,6,32,256]{5,4,3,2,1,0:T(8,128)(2,1)S(1)}, bf16[2,2,3,2,2,256,256]{6,5,4,3,2,1,0:T(8,128)(2...) custom-call(bf16[2,6,32,256]{3,2,1,0:T(8,128)(2,1)S(1)} %get-tuple-e, ...), custom_call_target="tpu_custom_call" | custom-call | flops 5000000000 | bytes 20000000 | tf_op jit(solution)/shard_map/inner_rows/pallas_call | solution.py:581
  15.6 0.3 collective-permute-done.first
  15.9 0.0 collective-permute-done.1.second
  15.9 3.3 %border_rows.1 = (bf16[2,16,64,256]{3,2,1,0:T(8,128)(2,1)}, f32[2,112,256]{2,1,0:T(8,128)S(1)}, bf16[2,112,256]{2,1,0:T(8,128)(2,1)S(1)}) custom-call(bf16[2,4,32,256]{3,2,1,0:T(8,128)(2,1)S(1)} %collective-permute-done.first, bf16[2,4,32,256]{3,2,1,0:T(8,128)(2,1)S(1)} %collective-permute-done.1.second, ...), custom_call_target="tpu_custom_call", output_to_operand_aliasing={{0}: (16, {})} | custom-call | flops 3000000000 | bytes 20000000 | tf_op jit(solution)/shard_map/border_rows/pallas_call | solution.py:605
  19.2 0.4 collective-permute-start.2
  19.6 1.0 %collective-permute-done.2 = bf16[2,112,256]{2,1,0:T(8,128)(2,1)S(1)} collective-permute-done((bf16[2,112,256]{2,1,0:T(8,128)(2,1)S(1)}, bf16[2,112,256]{2,1,0:T(8,128)(2,1)S(1)}, u32[]{:S(2)}, u32[]{:S(2)}) %collective-permute-start.2) | collective-permute-done | bytes 114720 | tf_op jit(solution)/shard_map/ppermute | solution.py:479
  20.7 3.8 %collective-permute-start.5 = (bf16[1,112,256]{2,1,0:T(8,128)(2,1)S(1)}, bf16[1,112,256]{2,1,0:T(8,128)(2,1)S(1)}, u32[]{:S(2)}, u32[]{:S(2)}) collective-permute-start(bf16[1,112,256]{2,1,0:T(8,128)(2,1)S(1)} %get-tuple-element.62), channel_id=1, source_target_pairs={{0,17},{1,16},{2,19},{3,18},{4,21},{5,20},{6,23},{7,22},{8,25},{9,... | collective-permute-start | bytes 172040 | tf_op jit(solution)/shard_map/ppermute | solution.py:486
  24.5 0.5 %collective-permute-start.4 = (bf16[1,112,256]{2,1,0:T(8,128)(2,1)S(1)}, bf16[1,112,256]{2,1,0:T(8,128)(2,1)S(1)}, u32[]{:S(2)}, u32[]{:S(2)}) collective-permute-start(bf16[1,112,256]{2,1,0:T(8,128)(2,1)S(1)} %get-tuple-element.62), channel_id=1, source_target_pairs={{0,16},{8,24},{16,0},{24,8},{1,17},{9,25},{17,1},{25,9},{2,18},{10... | collective-permute-start | bytes 172040 | tf_op jit(solution)/shard_map/ppermute | solution.py:485
  25.0 0.1 collective-permute-start.3
  25.1 1.6 %collective-permute-done.5 = bf16[1,112,256]{2,1,0:T(8,128)(2,1)S(1)} collective-permute-done((bf16[1,112,256]{2,1,0:T(8,128)(2,1)S(1)}, bf16[1,112,256]{2,1,0:T(8,128)(2,1)S(1)}, u32[]{:S(2)}, u32[]{:S(2)}) %collective-permute-start.5) | collective-permute-done | bytes 57376 | tf_op jit(solution)/shard_map/ppermute | solution.py:486
  26.7 1.9 %collective-permute-done.4 = bf16[1,112,256]{2,1,0:T(8,128)(2,1)S(1)} collective-permute-done((bf16[1,112,256]{2,1,0:T(8,128)(2,1)S(1)}, bf16[1,112,256]{2,1,0:T(8,128)(2,1)S(1)}, u32[]{:S(2)}, u32[]{:S(2)}) %collective-permute-start.4) | collective-permute-done | bytes 57376 | tf_op jit(solution)/shard_map/ppermute | solution.py:485
  28.7 0.5 %collective-permute-done.3 = bf16[1,112,256]{2,1,0:T(8,128)(2,1)S(1)} collective-permute-done((bf16[1,112,256]{2,1,0:T(8,128)(2,1)S(1)}, bf16[1,112,256]{2,1,0:T(8,128)(2,1)S(1)}, u32[]{:S(2)}, u32[]{:S(2)}) %collective-permute-start.3) | collective-permute-done | bytes 57376 | tf_op jit(solution)/shard_map/ppermute | solution.py:484
  29.2 2.4 %collective-permute-start.6 = (bf16[112,256]{1,0:T(8,128)(2,1)S(1)}, bf16[112,256]{1,0:T(8,128)(2,1)S(1)}, u32[]{:S(2)}, u32[]{:S(2)}) collective-permute-start(bf16[112,256]{1,0:T(8,128)(2,1)S(1)} %get-tuple-element.59), channel_id=1, source_target_pairs={{0,6},{1,7},{2,4},{3,5},{4,2},{5,3},{6,0},{7,1},{8,14},{9,15},{10,... | collective-permute-start | bytes 172040 | tf_op jit(solution)/shard_map/ppermute | solution.py:501
  31.6 0.7 %collective-permute-start.7 = (bf16[112,256]{1,0:T(8,128)(2,1)S(1)}, bf16[112,256]{1,0:T(8,128)(2,1)S(1)}, u32[]{:S(2)}, u32[]{:S(2)}) collective-permute-start(bf16[112,256]{1,0:T(8,128)(2,1)S(1)} %get-tuple-element.59), channel_id=1, source_target_pairs={{0,4},{1,5},{2,6},{3,7},{4,0},{5,1},{6,2},{7,3},{8,12},{9,13},{10,... | collective-permute-start | bytes 172040 | tf_op jit(solution)/shard_map/ppermute | solution.py:501
  32.3 1.3 %collective-permute-start.8 = (bf16[112,256]{1,0:T(8,128)(2,1)S(1)}, bf16[112,256]{1,0:T(8,128)(2,1)S(1)}, u32[]{:S(2)}, u32[]{:S(2)}) collective-permute-start(bf16[112,256]{1,0:T(8,128)(2,1)S(1)} %get-tuple-element.59), channel_id=1, source_target_pairs={{0,2},{1,3},{2,0},{3,1},{4,6},{5,7},{6,4},{7,5},{8,10},{9,11},{10,... | collective-permute-start | bytes 172040 | tf_op jit(solution)/shard_map/ppermute | solution.py:501
  33.7 1.7 %collective-permute-done.6.refs_0_ = bf16[112,256]{1,0:T(8,128)(2,1)S(1)} collective-permute-done((bf16[112,256]{1,0:T(8,128)(2,1)S(1)}, bf16[112,256]{1,0:T(8,128)(2,1)S(1)}, u32[]{:S(2)}, u32[]{:S(2)}) %collective-permute-start.6) | collective-permute-done | bytes 57376 | tf_op jit(solution)/shard_map/ppermute | solution.py:501
  35.3 1.9 %collective-permute-done.7.refs_1_ = bf16[112,256]{1,0:T(8,128)(2,1)S(1)} collective-permute-done((bf16[112,256]{1,0:T(8,128)(2,1)S(1)}, bf16[112,256]{1,0:T(8,128)(2,1)S(1)}, u32[]{:S(2)}, u32[]{:S(2)}) %collective-permute-start.7) | collective-permute-done | bytes 57376 | tf_op jit(solution)/shard_map/ppermute | solution.py:501
  37.3 0.0 collective-permute-done.8.refs_2_
  37.3 0.7 %unpack.1 = (f32[64,256]{1,0:T(8,128)}, f32[3,3,3,64]{3,2,1,0:T(4,128)}, f32[32,256]{1,0:T(8,128)}, f32[3,3,3,32]{3,2,1,0:T(4,128)}) custom-call(f32[112,256]{1,0:T(8,128)S(1)} %get-tuple-element.60.total_ref, bf16[112,256]{1,0:T(8,128)(2,1)S(1)} %collective-permute-done.6.refs_0_, bf16[112,256]{1,0:T(8,128)(2,1)S(1)} %collective-permute-done.7.refs_1_, ...), custom_call_target="tpu_custom_call" | custom-call | tf_op jit(solution)/shard_map/unpack/pallas_call | solution.py:634
  (3 shorter events, 0.1 us)
Async XLA Ops:
  7.3 8.6 %collective-permute-start = (bf16[2,4,32,256]{3,2,1,0:T(8,128)(2,1)S(1)}, bf16[2,4,32,256]{3,2,1,0:T(8,128)(2,1)S(1)}, u32[]{:S(2)}, u32[]{:S(2)}) collective-permute-start(bf16[2,4,32,256]{3,2,1,0:T(8,128)(2,1)S(1)} %get-tuple-element.32), channel_id=1, source_target_pairs={{0,1},{1,0},{2,3},{3,2},{4,5},{5,4},{6,7},{7,6},{8,9},{9,8},{10,11... | collective-permute-start | bytes 393224 | tf_op jit(solution)/shard_map/ppermute | solution.py:575
  10.3 5.6 %collective-permute-start.1 = (bf16[2,4,32,256]{3,2,1,0:T(8,128)(2,1)S(1)}, bf16[2,4,32,256]{3,2,1,0:T(8,128)(2,1)S(1)}, u32[]{:S(2)}, u32[]{:S(2)}) collective-permute-start(bf16[2,4,32,256]{3,2,1,0:T(8,128)(2,1)S(1)} %get-tuple-element.33), channel_id=1, source_target_pairs={{0,8},{1,2},{2,1},{3,4},{4,3},{5,6},{6,5},{7,15},{8,0},{9,10},{10,... | collective-permute-start | bytes 393224 | tf_op jit(solution)/shard_map/ppermute | solution.py:576
  19.2 1.4 %collective-permute-start.2 = (bf16[2,112,256]{2,1,0:T(8,128)(2,1)S(1)}, bf16[2,112,256]{2,1,0:T(8,128)(2,1)S(1)}, u32[]{:S(2)}, u32[]{:S(2)}) collective-permute-start(bf16[2,112,256]{2,1,0:T(8,128)(2,1)S(1)} %get-tuple-element.53), channel_id=1, source_target_pairs={{0,8},{8,0},{16,24},{24,16},{1,9},{9,1},{17,25},{25,17},{2,10},{10... | collective-permute-start | bytes 344072 | tf_op jit(solution)/shard_map/ppermute | solution.py:479
  20.7 6.1 %collective-permute-start.5 = (bf16[1,112,256]{2,1,0:T(8,128)(2,1)S(1)}, bf16[1,112,256]{2,1,0:T(8,128)(2,1)S(1)}, u32[]{:S(2)}, u32[]{:S(2)}) collective-permute-start(bf16[1,112,256]{2,1,0:T(8,128)(2,1)S(1)} %get-tuple-element.62), channel_id=1, source_target_pairs={{0,17},{1,16},{2,19},{3,18},{4,21},{5,20},{6,23},{7,22},{8,25},{9,... | collective-permute-start | bytes 172040 | tf_op jit(solution)/shard_map/ppermute | solution.py:486
  24.5 4.2 %collective-permute-start.4 = (bf16[1,112,256]{2,1,0:T(8,128)(2,1)S(1)}, bf16[1,112,256]{2,1,0:T(8,128)(2,1)S(1)}, u32[]{:S(2)}, u32[]{:S(2)}) collective-permute-start(bf16[1,112,256]{2,1,0:T(8,128)(2,1)S(1)} %get-tuple-element.62), channel_id=1, source_target_pairs={{0,16},{8,24},{16,0},{24,8},{1,17},{9,25},{17,1},{25,9},{2,18},{10... | collective-permute-start | bytes 172040 | tf_op jit(solution)/shard_map/ppermute | solution.py:485
  25.0 4.2 %collective-permute-start.3 = (bf16[1,112,256]{2,1,0:T(8,128)(2,1)S(1)}, bf16[1,112,256]{2,1,0:T(8,128)(2,1)S(1)}, u32[]{:S(2)}, u32[]{:S(2)}) collective-permute-start(bf16[1,112,256]{2,1,0:T(8,128)(2,1)S(1)} %get-tuple-element.61), channel_id=1, source_target_pairs={{0,1},{1,0},{2,3},{3,2},{4,5},{5,4},{6,7},{7,6},{8,9},{9,8},{10,11... | collective-permute-start | bytes 172040 | tf_op jit(solution)/shard_map/ppermute | solution.py:484
  29.2 6.1 %collective-permute-start.6 = (bf16[112,256]{1,0:T(8,128)(2,1)S(1)}, bf16[112,256]{1,0:T(8,128)(2,1)S(1)}, u32[]{:S(2)}, u32[]{:S(2)}) collective-permute-start(bf16[112,256]{1,0:T(8,128)(2,1)S(1)} %get-tuple-element.59), channel_id=1, source_target_pairs={{0,6},{1,7},{2,4},{3,5},{4,2},{5,3},{6,0},{7,1},{8,14},{9,15},{10,... | collective-permute-start | bytes 172040 | tf_op jit(solution)/shard_map/ppermute | solution.py:501
  31.6 5.7 %collective-permute-start.7 = (bf16[112,256]{1,0:T(8,128)(2,1)S(1)}, bf16[112,256]{1,0:T(8,128)(2,1)S(1)}, u32[]{:S(2)}, u32[]{:S(2)}) collective-permute-start(bf16[112,256]{1,0:T(8,128)(2,1)S(1)} %get-tuple-element.59), channel_id=1, source_target_pairs={{0,4},{1,5},{2,6},{3,7},{4,0},{5,1},{6,2},{7,3},{8,12},{9,13},{10,... | collective-permute-start | bytes 172040 | tf_op jit(solution)/shard_map/ppermute | solution.py:501
  32.3 5.0 %collective-permute-start.8 = (bf16[112,256]{1,0:T(8,128)(2,1)S(1)}, bf16[112,256]{1,0:T(8,128)(2,1)S(1)}, u32[]{:S(2)}, u32[]{:S(2)}) collective-permute-start(bf16[112,256]{1,0:T(8,128)(2,1)S(1)} %get-tuple-element.59), channel_id=1, source_target_pairs={{0,2},{1,3},{2,0},{3,1},{4,6},{5,7},{6,4},{7,5},{8,10},{9,11},{10,... | collective-permute-start | bytes 172040 | tf_op jit(solution)/shard_map/ppermute | solution.py:501
